TPU v7x, 32 devices: a whole 2x2x4 slice. The times are simulated.
32 devices in a mesh: grp: 4 (over z), seq: 8 (over y, x, core).
Axes of the slice: x: 2, y: 2, z: 4, core: 2. Of those that a mesh axis runs over, the one named last changes fastest.
Arguments:
- queries: bfloat16 [16384, 4096], P(('seq', 'grp')), may hold values from -6 to 6
- keys: bfloat16 [16384, 4096], P(('seq', 'grp')), may hold values from -6 to 6
- values: bfloat16 [16384, 4096], P(('seq', 'grp')), may hold values from -6 to 6
- log_decay: float32 [32, 16384], P('grp', 'seq'), may hold values from -1.3 to 0, as said below
- gain: float32 [4096], P('grp'), may hold values from 0.5 to 1.5
Outputs:
- attended: bfloat16 [16384, 4096], P('seq', 'grp')
Inputs may be any that keep to these rules, and one draw needn't show every extreme that they name: log_decay is negative everywhere.
All inputs are finite; a program needn't handle non-finite values.
Results may differ from a plain program's by a relative error of at most 0.0059.
Values may be sent and summed in bfloat16 or wider, within the bound.
No kernel may reach another device: no remote copies, remote signals or barrier semaphores. Data moves between devices by JAX's collectives and lax.ppermute only.
A program may use at most 128 MiB of HBM per device.

v0:
```python
import jax
import jax.numpy as jnp
from jax import lax
from jax.sharding import PartitionSpec as P


def entering_2(array, axis, combine, identity):
    length, mine = (lax.axis_size(axis), lax.axis_index(axis))
    everything = jax.tree.map(lambda part: lax.all_gather(part, axis), array)
    start = jax.tree.map(
        lambda part, zero: jnp.broadcast_to(jnp.asarray(zero, part.dtype), part.shape),
        array,
        identity,
    )

    def step(k, before):
        reached = k < mine
        new = combine(before, jax.tree.map(lambda part: part[k], everything))
        return jax.tree.map(lambda a, b: jnp.where(reached, a, b), new, before)

    return lax.fori_loop(0, length, step, start)


def local_mix(query_heads, key_heads, value_heads, levels):
    row_total = query_heads.shape[0]
    block_rows = min(512, row_total)
    pieces = []
    for start in range(0, row_total, block_rows):
        finish = start + block_rows
        scores = jnp.einsum(
            "thd,shd->hts",
            query_heads[start:finish],
            key_heads[:finish],
            preferred_element_type=jnp.float32,
        )
        causal = (
            jnp.arange(start, finish, dtype=jnp.int32)[:, None]
            >= jnp.arange(finish, dtype=jnp.int32)[None, :]
        )
        decay_gap = jnp.where(
            causal[None], levels[:, start:finish, None] - levels[:, None, :finish], 0.0
        )
        weights = jnp.where(causal[None], scores * jnp.exp(decay_gap), 0.0).astype(jnp.bfloat16)
        pieces.append(
            jnp.einsum(
                "hts,shd->thd", weights, value_heads[:finish], preferred_element_type=jnp.float32
            )
        )
    return jnp.concatenate(pieces, axis=0)


def local(queries, keys, values, log_decay, gain):
    head_count = log_decay.shape[0]
    row_count = log_decay.shape[1]
    head_width = gain.shape[0] // head_count
    query_rows, key_rows, value_rows = (
        lax.all_to_all(queries, "grp", split_axis=1, concat_axis=0, tiled=True),
        lax.all_to_all(keys, "grp", split_axis=1, concat_axis=0, tiled=True),
        lax.all_to_all(values, "grp", split_axis=1, concat_axis=0, tiled=True),
    )
    key_heads = key_rows.reshape(row_count, head_count, head_width)
    value_heads = value_rows.reshape(row_count, head_count, head_width)
    levels = jnp.cumsum(log_decay, axis=1)
    block_total = levels[:, -1]
    tail_decay = jnp.exp(block_total[:, None] - levels)
    scaled_keys = (key_heads.astype(jnp.float32) * tail_decay.T[:, :, None]).astype(jnp.bfloat16)
    block_state = jnp.einsum(
        "thd,the->hde", scaled_keys, value_heads, preferred_element_type=jnp.float32
    )

    def combine_blocks(earlier, later_part):
        return (
            earlier[0] + later_part[0],
            jnp.exp(later_part[0])[:, None, None] * earlier[1] + later_part[1],
        )

    identity = (jnp.zeros_like(block_total), jnp.zeros_like(block_state))
    _, entering = entering_2((block_total, block_state), "seq", combine_blocks, identity)
    query_heads = query_rows.reshape(row_count, head_count, head_width)
    local_part = local_mix(query_heads, key_heads, value_heads, levels)
    state_half = entering.astype(jnp.bfloat16)
    scaled_queries = (query_heads.astype(jnp.float32) * jnp.exp(levels).T[:, :, None]).astype(
        jnp.bfloat16
    )
    carried_part = jnp.einsum(
        "thd,hde->the", scaled_queries, state_half, preferred_element_type=jnp.float32
    )
    mixture = local_part + carried_part
    mean_square = jnp.mean(mixture * mixture, axis=2, keepdims=True)
    normed = mixture * lax.rsqrt(mean_square + 1e-06) * gain.reshape(head_count, head_width)[None]
    return normed.reshape(row_count, head_count * head_width).astype(jnp.bfloat16)


def solution(mesh):
    in_specs = (
        P(("seq", "grp"), None),
        P(("seq", "grp"), None),
        P(("seq", "grp"), None),
        P("grp", "seq"),
        P("grp"),
    )
    out_specs = P("seq", "grp")
    return jax.shard_map(local, mesh=mesh, in_specs=in_specs, out_specs=out_specs, check_vma=False)
```

profile of v0, /device:TPU:10, one launch (start us, length us, event | category | flops | bytes accessed | tf_op | source)
XLA Modules:
  0.0 466.8 jit_solution(14680001478203578593)
XLA Ops:
  6.5 6.4 %copy.67 = bf16[512,4096]{0,1:T(8,128)(2,1)} copy(bf16[512,4096]{1,0:T(8,128)(2,1)} %param.8) | data formatting | bytes 8388608 | tf_op args[1]
  12.9 5.3 %all-to-all-start.1 = ((bf16[512,4,1024]{0,2,1:T(8,128)(2,1)}), bf16[512,4,1024]{0,2,1:T(8,128)(2,1)}, u32[]{:S(2)}, u32[]{:S(2)}) async-start(bf16[512,4,1024]{0,2,1:T(8,128)(2,1)} %bitcast.91), calls=%async_computation.1 | async-start | bytes 8388608 | tf_op jit(solution)/shard_map/all_to_all | solution.py:58
  18.3 6.5 %copy.71 = bf16[512,4096]{0,1:T(8,128)(2,1)} copy(bf16[512,4096]{1,0:T(8,128)(2,1)} %param.9) | data formatting | bytes 8388608 | tf_op args[2]
  24.7 83.6 %all-to-all-done.1 = bf16[512,4,1024]{0,2,1:T(8,128)(2,1)} async-done(((bf16[512,4,1024]{0,2,1:T(8,128)(2,1)}), bf16[512,4,1024]{0,2,1:T(8,128)(2,1)}, u32[]{:S(2)}, u32[]{:S(2)}) %all-to-all-start.1) | async-done | bytes 4194336 | tf_op jit(solution)/shard_map/all_to_all | solution.py:58
  108.3 8.2 %all-to-all-start.2 = ((bf16[512,4,1024]{0,2,1:T(8,128)(2,1)}), bf16[512,4,1024]{0,2,1:T(8,128)(2,1)}, u32[]{:S(2)}, u32[]{:S(2)}) async-start(bf16[512,4,1024]{0,2,1:T(8,128)(2,1)} %bitcast.88), calls=%async_computation.2 | async-start | bytes 8388608 | tf_op jit(solution)/shard_map/all_to_all | solution.py:59
  116.5 6.5 %copy.66 = bf16[512,4096]{0,1:T(8,128)(2,1)} copy(bf16[512,4096]{1,0:T(8,128)(2,1)} %param.7) | data formatting | bytes 8388608 | tf_op args[0]
  123.0 82.8 %all-to-all-done.2 = bf16[512,4,1024]{0,2,1:T(8,128)(2,1)} async-done(((bf16[512,4,1024]{0,2,1:T(8,128)(2,1)}), bf16[512,4,1024]{0,2,1:T(8,128)(2,1)}, u32[]{:S(2)}, u32[]{:S(2)}) %all-to-all-start.2) | async-done | bytes 4194336 | tf_op jit(solution)/shard_map/all_to_all | solution.py:59
  205.8 8.4 %all-to-all-start = ((bf16[512,4,1024]{0,2,1:T(8,128)(2,1)}), bf16[512,4,1024]{0,2,1:T(8,128)(2,1)}, u32[]{:S(2)}, u32[]{:S(2)}) async-start(bf16[512,4,1024]{0,2,1:T(8,128)(2,1)} %bitcast.86), calls=%async_computation | async-start | bytes 8388608 | tf_op jit(solution)/shard_map/all_to_all | solution.py:57
  214.2 2.3 reduce-window.6
  217.2 1.3 copy.89
  219.9 11.0 %all-reduce = f32[64]{0:T(128)S(1)} all-reduce(f32[64]{0:T(128)S(1)} %bitcast_dynamic-update-slice_fusion), channel_id=2, replica_groups=mesh['grp'=4,'seq'=8] {'seq'}, use_global_device_ids=true, to_apply=%add | all-reduce | flops 64 | bytes 512
  231.6 1.3 copy.93
  235.5 1.7 iota_compare_fusion
  237.7 6.2 %copy.83 = bf16[4,512,1024]{2,1,0:T(8,128)(2,1)} copy(bf16[4,512,1024]{1,2,0:T(8,128)(2,1)} %bitcast.4) | data formatting | bytes 8388608 | tf_op jit(solution)/shard_map/all_to_all | solution.py:58
  243.9 3.7 slice.128
  247.6 6.3 %copy.86 = bf16[4,512,1024]{2,1,0:T(8,128)(2,1)} copy(bf16[4,512,1024]{1,2,0:T(8,128)(2,1)} %bitcast.8) | data formatting | bytes 8388608 | tf_op jit(solution)/shard_map/all_to_all | solution.py:59
  253.9 3.7 slice.131
  257.7 3.1 slice.123
  260.8 1.9 slice.126
  262.7 2.3 slice.118
  264.9 2.3 slice.121
  268.3 1.3 copy-done.2
  271.1 4.8 %multiply_convert_fusion.1 = bf16[2048,8,128]{2,1,0:T(8,128)(2,1)S(1)} fusion(f32[2048,8]{1,0:T(8,128)S(1)} %copy-done.3, bf16[256,8,8,128]{3,2,1,0:T(8,128)(2,1)S(1)} %copy.113), kind=kLoop, calls=%fused_computation.11 | loop fusion | flops 6291456 | bytes 8454144 | tf_op jit(solution)/shard_map/convert_element_type | solution.py:66
  275.9 3.3 fusion.3
  279.3 24.3 %all-to-all-done = bf16[512,4,1024]{0,2,1:T(8,128)(2,1)} async-done(((bf16[512,4,1024]{0,2,1:T(8,128)(2,1)}), bf16[512,4,1024]{0,2,1:T(8,128)(2,1)}, u32[]{:S(2)}, u32[]{:S(2)}) %all-to-all-start) | async-done | bytes 4194336 | tf_op jit(solution)/shard_map/all_to_all | solution.py:57
  303.6 4.3 fusion.46
  307.8 4.6 copy.78
  312.5 4.4 copy.111
  316.9 4.6 copy.81
  321.5 4.4 copy.112
  325.9 4.3 copy.73
  330.2 3.5 copy.109
  333.7 2.4 copy.76
  336.1 3.6 copy.110
  339.7 6.6 %bitcast_convert_fusion = f32[4,512,1024]{1,2,0:T(8,128)} fusion(bf16[512,4,1024]{0,2,1:T(8,128)(2,1)} %all-to-all-done), kind=kLoop, calls=%fused_computation.48 | loop fusion | flops 2097152 | bytes 12582912 | tf_op jit(solution)/shard_map/convert_element_type | solution.py:82
  346.2 8.7 %copy.92 = f32[4,512,1024]{2,1,0:T(8,128)} copy(f32[4,512,1024]{1,2,0:T(8,128)} %bitcast_convert_fusion) | data formatting | bytes 16777216 | tf_op jit(solution)/shard_map/convert_element_type | solution.py:82
  355.0 5.6 %copy.115 = f32[256,8,8,128]{3,2,1,0:T(8,128)S(1)} copy(f32[256,8,8,128]{3,1,2,0:T(8,128)} %bitcast.85) | data formatting | bytes 16777216
  360.6 4.3 fusion.1
  364.9 7.0 %fusion.35 = f32[512,8,128]{2,0,1:T(8,128)} fusion(bf16[512,8,128]{0,2,1:T(8,128)(2,1)} %bitcast.105, f32[8,512]{1,0:T(8,128)} %get-tuple-element.134, pred[512,512]{1,0:T(8,128)(4,1)} %iota_compare_fusion.3, bf16[512,8,128]{0,2,1:T(8,128)(2,1)} %bitcast.109, bf16[512,8,128]{0,2,1:T(8,128)(2,1)} %bitcast.104), kind=kOutput, calls=%fused_computation.34 | convolution fusion | flops 1084227584 | bytes 5521408 | tf_op jit(solution)/shard_map/hts,shd->thd/dot_general | solution.py:45
  371.9 9.9 %fusion.36 = f32[512,8,128]{2,0,1:T(8,128)} fusion(bf16[1024,8,128]{2,1,0:T(8,128)(2,1)} %bitcast.102, bf16[512,8,128]{0,2,1:T(8,128)(2,1)} %bitcast.108, f32[8,1024]{1,0:T(8,128)S(1)} %slice.125, f32[8,512]{1,0:T(8,128)} %get-tuple-element.137, pred[512,1024]{1,0:T(8,128)(4,1)} %iota_compare_fusion.2, bf16[1024,8,128]{2,1,0:T(8,128)(2,1)S(1)} %bitcast.101), kind=kOutput, calls=%fused_computation.35 | convolution fusion | flops 2168455168 | bytes 7913472 | tf_op jit(solution)/shard_map/hts,shd->thd/dot_general | solution.py:45
  381.7 19.4 %fusion.30 = f32[512,8,128]{2,0,1:T(8,128)} fusion(bf16[2048,8,128]{2,1,0:T(8,128)(2,1)} %bitcast.98, bf16[512,8,128]{0,2,1:T(8,128)(2,1)} %bitcast.107, f32[8,2048]{1,0:T(8,128)S(1)} %bitcast.114, f32[8,512]{1,0:T(8,128)} %get-tuple-element.135, pred[512,2048]{1,0:T(8,128)(4,1)} %iota_compare_fusion, bf16[2048,8,128]{2,1,0:T(8,128)(2,1)} %bitcast.87), kind=kOutput, calls=%fused_computation.33 | convolution fusion | flops 4336910336 | bytes 12664832 | tf_op jit(solution)/shard_map/hts,shd->thd/dot_general | solution.py:45
  401.2 13.2 %fusion.25 = f32[512,8,128]{2,0,1:T(8,128)} fusion(bf16[1536,8,128]{2,1,0:T(8,128)(2,1)} %bitcast.100, bf16[512,8,128]{0,2,1:T(8,128)(2,1)S(1)} %bitcast.106, f32[8,1536]{1,0:T(8,128)S(1)} %slice.130, f32[8,512]{1,0:T(8,128)S(1)} %copy-done.9, pred[512,1536]{1,0:T(8,128)(4,1)S(1)} %iota_compare_fusion.1, bf16[1536,8,128]{2,1,0:T(8,128)(2,1)} %bitcast.99), kind=kOutput, calls=%fused_computation.32 | convolution fusion | flops 3252682752 | bytes 10289152 | tf_op jit(solution)/shard_map/hts,shd->thd/dot_general | solution.py:45
  414.5 15.2 %while.14 = (s32[]{:T(128)}, f32[8,128,128]{2,1,0:T(8,128)S(1)}, s32[]{:T(128)}, f32[8,8]{1,0:T(8,128)}, f32[8,8,128,128]{3,2,1,0:T(8,128)}, /*index=5*/s32[]{:T(128)}, s32[]{:T(128)}) while((s32[]{:T(128)}, f32[8,128,128]{2,1,0:T(8,128)S(1)}, s32[]{:T(128)}, f32[8,8]{1,0:T(8,128)}, f32[8,8,128,128]{3,2,1,0:T(8,128)}, ...), condition=%wide.region_3.4_spmd.clone, body=%wide.region_2.3_spmd.clone.sunk | while | flops 524292 | bytes 1573065 | solution.py:21
  415.1 1.2 fusion.55
  429.7 10.2 %multiply_reduce_fusion = (f32[2048,8]{0,1:T(8,128)S(1)}, f32[2048,8,128]{2,0,1:T(8,128)}) fusion(f32[8,128,128]{2,1,0:T(8,128)S(1)} %get-tuple-element.99, bf16[2048,8,128]{2,1,0:T(8,128)(2,1)} %fusion.1, f32[512,8,128]{2,0,1:T(8,128)} %fusion.30, f32[512,8,128]{2,0,1:T(8,128)} %fusion.25, f32[512,8,128]{2,0,1:T(8,128)} %fusion.36, f32[512,8,128]{2,0,1:T(8,128)} %fusion.35), kind=kOutput, calls=%fused_computation.10 | convolution fusion | flops 549568512 | bytes 21561344 | tf_op jit(solution)/shard_map/thd,hde->the/dot_general | solution.py:85
  439.9 6.8 %multiply_convert_fusion = bf16[2048,8,128]{2,0,1:T(8,128)(2,1)} fusion(f32[2048,8,128]{2,0,1:T(8,128)} %get-tuple-element.139, f32[8,128]{1,0:T(8,128)S(1)} %bitcast.117, f32[2048,8]{0,1:T(8,128)S(1)} %add_rsqrt_fusion), kind=kLoop, calls=%fused_computation.9 | loop fusion | flops 6291456 | bytes 12652544 | tf_op jit(solution)/shard_map/convert_element_type | solution.py:91
  446.7 6.5 %copy.97 = bf16[2048,8,128]{0,2,1:T(8,128)(2,1)} copy(bf16[2048,8,128]{2,0,1:T(8,128)(2,1)} %multiply_convert_fusion) | data formatting | bytes 8388608 | tf_op jit(solution)/shard_map/convert_element_type | solution.py:91
  453.3 6.4 %copy.98 = bf16[2048,1024]{1,0:T(8,128)(2,1)} copy(bf16[2048,1024]{0,1:T(8,128)(2,1)} %bitcast.92) | data formatting | bytes 8388608 | tf_op jit(solution)/shard_map/convert_element_type | solution.py:91
  (66 shorter events, 21.5 us)
Async XLA Ops:
  12.9 95.4 %all-to-all-start.1 = ((bf16[512,4,1024]{0,2,1:T(8,128)(2,1)}), bf16[512,4,1024]{0,2,1:T(8,128)(2,1)}, u32[]{:S(2)}, u32[]{:S(2)}) async-start(bf16[512,4,1024]{0,2,1:T(8,128)(2,1)} %bitcast.91), calls=%async_computation.1 | async-start | bytes 8388608 | tf_op jit(solution)/shard_map/all_to_all | solution.py:58
  108.3 97.5 %all-to-all-start.2 = ((bf16[512,4,1024]{0,2,1:T(8,128)(2,1)}), bf16[512,4,1024]{0,2,1:T(8,128)(2,1)}, u32[]{:S(2)}, u32[]{:S(2)}) async-start(bf16[512,4,1024]{0,2,1:T(8,128)(2,1)} %bitcast.88), calls=%async_computation.2 | async-start | bytes 8388608 | tf_op jit(solution)/shard_map/all_to_all | solution.py:59
  205.8 8.4 %copy-start.8 = (f32[8,2048]{1,0:T(8,128)S(1)}, f32[8,2048]{1,0:T(8,128)}, u32[]{:S(2)}) copy-start(f32[8,2048]{1,0:T(8,128)} %param.10) | copy-start | bytes 196612
  205.8 12.8 %copy-start.11 = (u32[32]{0:T(128)S(1)}, u32[32]{0:T(128)}, u32[]{:S(2)}) copy-start(u32[32]{0:T(128)} %constant.47) | copy-start | bytes 388
  205.8 97.8 %all-to-all-start = ((bf16[512,4,1024]{0,2,1:T(8,128)(2,1)}), bf16[512,4,1024]{0,2,1:T(8,128)(2,1)}, u32[]{:S(2)}, u32[]{:S(2)}) async-start(bf16[512,4,1024]{0,2,1:T(8,128)(2,1)} %bitcast.86), calls=%async_computation | async-start | bytes 8388608 | tf_op jit(solution)/shard_map/all_to_all | solution.py:57
  214.2 200.3 %all-gather.4.cloned.1.call-start = ((), (), s32[]{:S(2)}) async-start(), calls=%async_computation.3 | async-start | bytes 4718592 | tf_op jit(solution)/shard_map/all_gather | solution.py:9
  260.8 6.4 %copy-start.1 = (bf16[4,512,1024]{2,1,0:T(8,128)(2,1)S(1)}, bf16[4,512,1024]{2,1,0:T(8,128)(2,1)}, u32[]{:S(2)}) copy-start(bf16[4,512,1024]{2,1,0:T(8,128)(2,1)} %copy.83) | copy-start | bytes 12582916
  267.2 2.4 copy-start.2
  268.3 2.4 copy-start
  269.6 1.5 copy-start.3
  271.1 4.8 %copy-start.4 = (bf16[256,8,8,128]{3,2,1,0:T(8,128)(2,1)}, bf16[256,8,8,128]{3,2,1,0:T(8,128)(2,1)S(1)}, u32[]{:S(2)}) copy-start(bf16[256,8,8,128]{3,2,1,0:T(8,128)(2,1)S(1)} %copy.114) | copy-start | bytes 12582916
  355.0 5.6 %copy-start.5 = (f32[2048,8]{1,0:T(8,128)S(1)}, f32[2048,8]{1,0:T(8,128)}, u32[]{:S(2)}) copy-start(f32[2048,8]{1,0:T(8,128)} %copy.93) | copy-start | bytes 196612
  364.9 7.0 %copy-start.6 = (bf16[128,8,8,128]{3,2,1,0:T(8,128)(2,1)S(1)}, bf16[128,8,8,128]{3,2,1,0:T(8,128)(2,1)}, u32[]{:S(2)}) copy-start(bf16[128,8,8,128]{3,2,1,0:T(8,128)(2,1)} %copy.109) | copy-start | bytes 6291460
  381.7 19.5 %copy-start.7 = (bf16[1,512,1024]{1,2,0:T(8,128)(2,1)S(1)}, bf16[1,512,1024]{1,2,0:T(8,128)(2,1)}, u32[]{:S(2)}) copy-start(bf16[1,512,1024]{1,2,0:T(8,128)(2,1)} %get-tuple-element.130) | copy-start | bytes 3145732
  381.7 19.5 %copy-start.9 = (f32[8,512]{1,0:T(8,128)S(1)}, f32[8,512]{1,0:T(8,128)}, u32[]{:S(2)}) copy-start(f32[8,512]{1,0:T(8,128)} %get-tuple-element.136) | copy-start | bytes 49156
  429.7 10.2 %copy-start.10 = (f32[1024]{0:T(1024)S(1)}, f32[1024]{0:T(1024)}, u32[]{:S(2)}) copy-start(f32[1024]{0:T(1024)} %param.11) | copy-start | bytes 12292
Sparse Core Ops, SparseCore 0:
  279.4 37.6 all-gather.3
where the time goes:
time: 476 us; the launch traced here: 467 us
  waiting for transfers between devices  191 us (40%)
  local copies, waits for them, and re-layouts  126 us (26%)
  matrix products  63.1 us (13%)
  other arithmetic  38.7 us (8%)
  starting transfers between devices  21.9 us (5%)
  between operations  14.5 us (3%)
  blocking collectives  11 us (2%)
    all_to_all x1, waiting for transfers between devices, local(): lax.all_to_all(keys, 'grp', split_axis=1, concat_axis=0, tiled=True)  83.6 us
    all_to_all x1, waiting for transfers between devices, local(): lax.all_to_all(values, 'grp', split_axis=1, concat_axis=0, tiled=True)  82.8 us
    dot_general x4, matrix products, local_mix(): jnp.einsum('hts,shd->thd', weights, value_heads[:finish], preferred_eleme...  49.6 us
    unnamed x39, local copies, waits for them, and re-layouts  45.5 us
    all_to_all x1, waiting for transfers between devices, local(): lax.all_to_all(queries, 'grp', split_axis=1, concat_axis=0, tiled=True)  24.3 us
    slice x5, local copies, waits for them, and re-layouts, local_mix(): key_heads[:finish]  18 us
    slice x5, local copies, waits for them, and re-layouts, local_mix(): value_heads[:finish]  14.9 us
    convert_element_type x2, local copies, waits for them, and re-layouts, local(): normed.reshape(row_count, head_count * head_width).astype(jnp.bfloat16)  12.9 us
  transfers between devices with their start and end apart: 4, of which 3 were waited for; matrix products, arithmetic and copies ran while one was open for 38% of the time, Pallas kernels for 0%

commit v1 on v0

--- a/solution.py
+++ b/solution.py
@@ -1,7 +1,16 @@
+import functools
+
 import jax
 import jax.numpy as jnp
 from jax import lax
+from jax.experimental import pallas as pl
+from jax.experimental.pallas import tpu as pltpu
 from jax.sharding import PartitionSpec as P
+
+GROUPS = (2, 3, 3)
+CHUNK = 256
+F32 = jnp.float32
+BF16 = jnp.bfloat16
 
 
 def entering_2(array, axis, combine, identity):
@@ -49,7 +58,7 @@
     return jnp.concatenate(pieces, axis=0)
 
 
-def local(queries, keys, values, log_decay, gain):
+def local_any(queries, keys, values, log_decay, gain):
     head_count = log_decay.shape[0]
     row_count = log_decay.shape[1]
     head_width = gain.shape[0] // head_count
@@ -91,7 +100,346 @@
     return normed.reshape(row_count, head_count * head_width).astype(jnp.bfloat16)
 
 
+def call(kernel, scalars, arrays, outs, grid=None, in_specs=None, out_specs=None, scratch=(), cost=(0, 0), **kw):
+    whole = [pl.BlockSpec(a.shape, lambda *_, n=a.ndim: (0,) * n) for a in arrays]
+    whole_out = [pl.BlockSpec(o.shape, lambda *_, n=len(o.shape): (0,) * n) for o in outs]
+    return pl.pallas_call(
+        kernel,
+        out_shape=outs,
+        grid_spec=pltpu.PrefetchScalarGridSpec(
+            num_scalar_prefetch=1,
+            grid=grid or (1,),
+            in_specs=in_specs or whole,
+            out_specs=out_specs or whole_out,
+            scratch_shapes=list(scratch),
+        ),
+        compiler_params=pltpu.CompilerParams(vmem_limit_bytes=32 * 1024 * 1024),
+        cost_estimate=pl.CostEstimate(flops=cost[0], bytes_accessed=cost[1], transcendentals=0),
+        **kw,
+    )(scalars, *arrays)
+
+
+def shape(*dims, dtype=BF16):
+    return jax.ShapeDtypeStruct(dims, dtype)
+
+
+def pick(rows, index):
+    at = lax.broadcasted_iota(jnp.int32, rows.shape, 0)
+    return jnp.sum(jnp.where(at == index, rows, 0.0), axis=0, keepdims=True)
+
+
+def pack_decays(z_ref, decay_ref, gain_ref, *out_refs):
+    z = z_ref[0]
+    heads, rows = decay_ref.shape
+    parts = len(out_refs)
+    width = rows // parts
+    lane = lax.broadcasted_iota(jnp.int32, (heads, 128), 1)
+    totals = jnp.zeros((heads, 128), F32)
+    for c in range(parts):
+        total = jnp.sum(decay_ref[:, c * width : (c + 1) * width], axis=1, keepdims=True)
+        totals = jnp.where(lane == c, total, totals)
+    for k, out_ref in enumerate(out_refs):
+        to = lax.rem(z + k, parts)
+        out_ref[:, :width] = decay_ref[:, pl.ds(pl.multiple_of(to * width, 128), width)]
+        out_ref[:, width : width + 128] = totals
+        out_ref[:, width + 128 :] = gain_ref[...]
+
+
+def unpack_decays(z_ref, *refs):
+    parts = len(refs) - 4
+    ins, (levels_ref, totals_ref, gains_ref, decays) = refs[:parts], refs[parts:]
+    z = z_ref[0]
+    heads = ins[0].shape[0]
+    width = decays.shape[1]
+    for k, in_ref in enumerate(ins):
+        home = lax.rem(z + parts - k, parts)
+        at = pl.ds(pl.multiple_of(home * heads, heads), heads)
+        decays[at, :] = in_ref[:, :width]
+        gains_ref[at, :] = in_ref[:, width + 128 :]
+        totals = in_ref[:, width : width + 128]
+        row = lax.broadcasted_iota(jnp.int32, totals_ref.shape[1:], 0)
+        for h in range(heads):
+            rows = jnp.zeros(totals_ref.shape[1:], F32)
+            for c in range(parts):
+                rows = jnp.where(row == c, totals[h : h + 1, c : c + 1], rows)
+            totals_ref[home * heads + h] = rows
+    upper = lax.broadcasted_iota(jnp.int32, (width, width), 0) <= lax.broadcasted_iota(
+        jnp.int32, (width, width), 1
+    )
+    levels_ref[...] = jnp.dot(
+        decays[...],
+        jnp.where(upper, 1.0, 0.0).astype(F32),
+        precision=lax.Precision.HIGHEST,
+        preferred_element_type=F32,
+    )
+
+
+def state_of(key, value, row, end):
+    scaled = (key.T.astype(F32) * jnp.exp(end - row)).astype(BF16)
+    return jnp.dot(scaled, value, preferred_element_type=F32)
+
+
+def quarter_states(head_of, z_ref, key_a, value_a, key_b, value_b, levels_ref, keep_ref, send_ref):
+    z, i = z_ref[0], pl.program_id(0)
+    width = levels_ref.shape[1]
+    for other, key, value, out in ((0, key_a, value_a, keep_ref), (1, key_b, value_b, send_ref)):
+        row = levels_ref[pl.ds(head_of(i, z, other), 1), :]
+        out[0] = state_of(key[...], value[...], row, row[:, width - 1 :]).astype(BF16)
+
+
+def pair_states(head_of, z_ref, keep_ref, got_ref, totals_ref, out_ref):
+    z = z_ref[0]
+    odd = lax.rem(z, 2) == 1
+    for i in range(keep_ref.shape[0]):
+        totals = totals_ref[head_of(i, z, 0)]
+        keep, got = keep_ref[i].astype(F32), got_ref[i].astype(F32)
+        decay = jnp.exp(pick(totals, 2 * lax.div(z, 2) + 1))
+        out_ref[i] = (decay * jnp.where(odd, got, keep) + jnp.where(odd, keep, got)).astype(BF16)
+
+
+def put_log(ref, i, log):
+    high = log.astype(BF16).astype(F32)
+    middle = (log - high).astype(BF16).astype(F32)
+    low = log - high - middle
+    row = lax.broadcasted_iota(jnp.int32, (16, 128), 0)
+    rows = jnp.where(row == 0, high, jnp.where(row == 1, middle, jnp.where(row == 2, low, 0.0)))
+    ref[i, 128:, :] = rows.astype(BF16)
+
+
+def get_log(ref, i):
+    return jnp.sum(ref[i, 128:, :].astype(F32), axis=0, keepdims=True)
+
+
+def block_states(head_of, z_ref, pair_ref, got_ref, totals_ref, out_ref):
+    z = z_ref[0]
+    upper = z >= 2
+    for i in range(pair_ref.shape[0]):
+        totals = totals_ref[head_of(i, z, 0)]
+        mine, got = pair_ref[i].astype(F32), got_ref[i].astype(F32)
+        decay = jnp.exp(pick(totals, 2) + pick(totals, 3))
+        state = decay * jnp.where(upper, got, mine) + jnp.where(upper, mine, got)
+        out_ref[i, :128, :] = state.astype(BF16)
+        put_log(out_ref, i, jnp.sum(totals, axis=0, keepdims=True))
+
+
+def scan_step(bit, s_ref, i, own_ref, got_ref, before, before_log):
+    upper = (s_ref[1] >> bit) & 1 == 1
+    own, got = own_ref[i, :128, :].astype(F32), got_ref[i, :128, :].astype(F32)
+    own_log, got_log = get_log(own_ref, i), get_log(got_ref, i)
+    if before is None:
+        after = jnp.where(upper, got, 0.0)
+        after_log = jnp.where(upper, got_log, 0.0)
+    else:
+        after = jnp.where(upper, jnp.exp(before_log) * got + before, before)
+        after_log = jnp.where(upper, before_log + got_log, before_log)
+    total = jnp.exp(jnp.where(upper, own_log, got_log)) * jnp.where(upper, got, own) + jnp.where(upper, own, got)
+    return after, after_log, total, own_log + got_log
+
+
+def scan_blocks(bit, s_ref, own_ref, got_ref, *refs):
+    before_ref = refs[0] if bit else None
+    after_ref, total_ref = refs[-2:]
+    for i in range(own_ref.shape[0]):
+        before = before_ref[i, :128, :] if bit else None
+        before_log = before_ref[i, 128:129, :] if bit else None
+        after, after_log, total, total_log = scan_step(bit, s_ref, i, own_ref, got_ref, before, before_log)
+        after_ref[i, :128, :] = after
+        after_ref[i, 128:, :] = jnp.broadcast_to(after_log, (8, 128))
+        total_ref[i, :128, :] = total.astype(BF16)
+        put_log(total_ref, i, total_log)
+
+
+def entering_states(head_of, bit, s_ref, own_ref, got_ref, before_ref, keep_ref, keep_got_ref, low_ref, totals_ref, out_ref, send_ref):
+    z = s_ref[0]
+    odd, upper = lax.rem(z, 2) == 1, z >= 2
+    for i in range(own_ref.shape[0]):
+        totals = totals_ref[head_of(i, z, 0)]
+        state = scan_step(
+            bit, s_ref, i, own_ref, got_ref, before_ref[i, :128, :], before_ref[i, 128:129, :]
+        )[0]
+        first, second = pick(totals, 0), pick(totals, 1)
+        even_state = jnp.where(
+            upper, jnp.exp(first + second) * state + low_ref[i].astype(F32), state
+        )
+        even_part = jnp.where(odd, keep_got_ref[i], keep_ref[i]).astype(F32)
+        decay = jnp.exp(jnp.where(upper, pick(totals, 2), first))
+        odd_state = decay * even_state + even_part
+        out_ref[i] = jnp.where(odd, odd_state, even_state).astype(BF16)
+        send_ref[i] = jnp.where(odd, even_state, odd_state).astype(BF16)
+
+
+def mix_head(query, key, value, row, entering, gain):
+    rows = query.shape[0]
+    chunk = min(CHUNK, rows)
+    column = jnp.broadcast_to(row, (128, rows)).T
+    causal = lax.broadcasted_iota(jnp.int32, (chunk, chunk), 0) >= lax.broadcasted_iota(
+        jnp.int32, (chunk, chunk), 1
+    )
+    state = entering.astype(F32)
+    start_level = jnp.zeros((1, 1), F32)
+    pieces = []
+    for start in range(0, rows, chunk):
+        stop = start + chunk
+        q, k, v = query[start:stop], key[start:stop], value[start:stop]
+        r, c = row[:, start:stop], column[start:stop]
+        scores = lax.dot_general(q, k, (((1,), (1,)), ((), ())), preferred_element_type=F32)
+        gap = jnp.where(causal, jnp.concatenate([c] * (chunk // 128), axis=1) - r, -1e30)
+        weights = (scores * jnp.exp(gap)).astype(BF16)
+        scaled = (q.astype(F32) * jnp.exp(c - start_level)).astype(BF16)
+        mixture = jnp.dot(weights, v, preferred_element_type=F32) + jnp.dot(
+            scaled, state.astype(BF16), preferred_element_type=F32
+        )
+        mean_square = jnp.mean(mixture * mixture, axis=1, keepdims=True)
+        pieces.append((mixture * lax.rsqrt(mean_square + 1e-6) * gain).astype(BF16))
+        if stop < rows:
+            end = row[:, stop - 1 : stop]
+            state = jnp.exp(end - start_level) * state + state_of(k, v, r, end)
+            start_level = end
+    return pieces
+
+
+def attend(first, parts, heads, z_ref, *refs):
+    ins, outs = refs[: 4 * parts + 2], refs[4 * parts + 2 :]
+    levels_ref, gains_ref = ins[-2:]
+    for k in range(parts):
+        query, key, value, state = ins[4 * k : 4 * k + 4]
+        head = lax.rem(z_ref[0] + k, parts) * heads + first + pl.program_id(0)
+        pieces = mix_head(
+            query[...], key[...], value[...], levels_ref[pl.ds(head, 1), :], state[0], gains_ref[pl.ds(head, 1), :]
+        )
+        size = pieces[0].shape[0]
+        for n, piece in enumerate(pieces):
+            outs[k][n * size : (n + 1) * size, :] = piece
+
+
+def place(first, parts, with_alias, z_ref, *refs):
+    pieces, out_ref, sems = refs[:parts], refs[-2], refs[-1]
+    rows, width = pieces[0].shape
+    copies = []
+    for k in range(parts):
+        source = lax.rem(z_ref[0] + parts - k, parts)
+        copies.append(
+            pltpu.make_async_copy(
+                pieces[k],
+                out_ref.at[pl.ds(pl.multiple_of(source * rows, rows), rows), pl.ds(first * 128, width)],
+                sems.at[k],
+            )
+        )
+    for copy in copies:
+        copy.start()
+    for copy in copies:
+        copy.wait()
+
+
+def local(queries, keys, values, log_decay, gain):
+    heads, block = log_decay.shape
+    parts = lax.axis_size("grp")
+    blocks = lax.axis_size("seq")
+    rows, columns = queries.shape
+    z, b = lax.axis_index("grp"), lax.axis_index("seq")
+    scalars = jnp.stack([z, b]).astype(jnp.int32)
+
+    def shift(x, k):
+        return lax.ppermute(x, "grp", [(i, (i + k) % parts) for i in range(parts)])
+
+    def swap(x, axis, bit):
+        return lax.ppermute(x, axis, [(i, i ^ bit) for i in range(lax.axis_size(axis))])
+
+    packed = call(
+        pack_decays, scalars, [log_decay, gain.reshape(heads, 128)],
+        [shape(heads, rows + 256, dtype=F32)] * parts,
+    )
+    got = [packed[0]] + [shift(packed[k], k) for k in range(1, parts)]
+    levels, totals, gains = call(
+        unpack_decays, scalars, got,
+        [shape(heads * parts, rows, dtype=F32), shape(heads * parts, 8, 128, dtype=F32), shape(heads * parts, 128, dtype=F32)],
+        scratch=[pltpu.VMEM((heads * parts, rows), F32)],
+    )
+    whole = lambda a: pl.BlockSpec(a.shape, lambda *_: (0,) * a.ndim)
+
+    starts = [sum(GROUPS[:g]) for g in range(len(GROUPS))]
+    pieces = []
+    for first, m in zip(starts, GROUPS):
+        n = 2 * m
+
+        def head_of(i, z, other, first=first, m=m):
+            home = 2 * (i // m) + lax.rem(z + other, 2)
+            return home * heads + first + i % m
+
+        def head_of_dyn(i, z, other, first=first, m=m):
+            home = 2 * lax.div(i, m) + lax.rem(z + other, 2)
+            return home * heads + first + lax.rem(i, m)
+
+        def column(other):
+            return pl.BlockSpec((rows, 128), lambda i, s: (0, head_of_dyn(i, s[0], other)))
+
+        one = pl.BlockSpec((1, 128, 128), lambda i, s: (i, 0, 0))
+        keep, send = call(
+            functools.partial(quarter_states, head_of_dyn), scalars, [keys, values, keys, values, levels],
+            [shape(n, 128, 128)] * 2,
+            grid=(n,),
+            in_specs=[column(0), column(0), column(1), column(1), whole(levels)],
+            out_specs=[one, one],
+            cost=(4 * n * rows * 128 * 128, 4 * n * rows * 256),
+        )
+        got = swap(send, "grp", 1)
+        pair, = call(functools.partial(pair_states, head_of), scalars, [keep, got, totals], [shape(n, 128, 128)])
+        pair_got = swap(pair, "grp", 2)
+        total, = call(functools.partial(block_states, head_of), scalars, [pair, pair_got, totals], [shape(n, 144, 128)])
+        before = []
+        bits = blocks.bit_length() - 1
+        for bit in range(bits - 1):
+            other = swap(total, "seq", 1 << bit)
+            after, total = call(
+                functools.partial(scan_blocks, bit), scalars, [total, other, *before],
+                [shape(n, 136, 128, dtype=F32), shape(n, 144, 128)],
+            )
+            before = [after]
+        other = swap(total, "seq", 1 << (bits - 1))
+        own, send = call(
+            functools.partial(entering_states, head_of, bits - 1), scalars,
+            [total, other, *before, keep, got, pair_got, totals],
+            [shape(n, 128, 128)] * 2,
+        )
+        states = [own, swap(send, "grp", 1)]
+
+        arrays, specs = [], []
+        for k in range(parts):
+            spec = pl.BlockSpec(
+                (rows, 128), lambda j, s, k=k, first=first: (0, lax.rem(s[0] + k, parts) * heads + first + j)
+            )
+            arrays += [queries, keys, values, states[k % 2]]
+            specs += [spec] * 3 + [
+                pl.BlockSpec((1, 128, 128), lambda j, s, k=k, m=m: (lax.div(lax.rem(s[0] + k, parts), 2) * m + j, 0, 0))
+            ]
+        outs = call(
+            functools.partial(attend, first, parts, heads), scalars, [*arrays, levels, gains],
+            [shape(rows, m * 128)] * parts,
+            grid=(m,),
+            in_specs=[*specs, whole(levels), whole(gains)],
+            out_specs=[pl.BlockSpec((rows, 128), lambda j, s: (0, j))] * parts,
+            cost=(parts * m * 4 * rows * 128 * 512, parts * m * rows * 1024),
+        )
+        pieces.append([outs[0]] + [shift(outs[k], k) for k in range(1, parts)])
+
+    out = None
+    for first, group in zip(starts, pieces):
+        alias = [] if out is None else [out]
+        any_spec = pl.BlockSpec(memory_space=pl.ANY)
+        out, = call(
+            functools.partial(place, first, parts, bool(alias)), scalars, [*group, *alias],
+            [shape(block, heads * 128)],
+            in_specs=[any_spec] * (parts + len(alias)),
+            out_specs=[any_spec],
+            scratch=[pltpu.SemaphoreType.DMA((parts,))],
+            input_output_aliases={parts + 1: 0} if alias else {},
+        )
+    return out
+
+
 def solution(mesh):
+    parts, blocks = mesh.shape["grp"], mesh.shape["seq"]
+    fits = parts == 4 and blocks >= 4 and blocks & (blocks - 1) == 0
     in_specs = (
         P(("seq", "grp"), None),
         P(("seq", "grp"), None),
@@ -100,4 +448,6 @@
         P("grp"),
     )
     out_specs = P("seq", "grp")
-    return jax.shard_map(local, mesh=mesh, in_specs=in_specs, out_specs=out_specs, check_vma=False)
+    return jax.shard_map(
+        local if fits else local_any, mesh=mesh, in_specs=in_specs, out_specs=out_specs, check_vma=False
+    )

time: 476 us -> 179 us (0.38); the launches traced: 467 us -> 178 us
  local copies, waits for them, and re-layouts: 126 us -> 5.91 us
  waiting for transfers between devices: 191 us -> 84 us
  matrix products: 63.1 us -> 0 us
  Pallas kernels: 0 us -> 46.5 us
  other arithmetic: 38.7 us -> 0.07 us
  starting transfers between devices: 21.9 us -> 41.3 us
  between operations: 14.5 us -> 0.4 us
  blocking collectives: 11 us -> 0 us
    all_to_all x3 -> x0, waiting for transfers between devices: 191 us -> none  [the longest x1 83.6 us: local(): lax.all_to_all(keys, 'grp', split_axis=1, concat_axis=0, tiled=True)]
    ppermute x0 -> x30, waiting for transfers between devices: none -> 84 us  [the longest x12 52.5 us: shift(): return lax.ppermute(x, 'grp', [(i, (i + k) % parts) for i in range(parts)])]
    dot_general x6 -> x0, matrix products: 63.1 us -> none  [the longest x4 49.6 us: local_mix(): jnp.einsum('hts,shd->thd', weights, value_heads[:finish], preferred_eleme...]
    pallas_call x0 -> x26, Pallas kernels: none -> 46.5 us  [call(): pl.pallas_call(kernel, out_shape=outs, grid_spec=pltpu.PrefetchScalarGrid...]
    ppermute x0 -> x30, starting transfers between devices: none -> 41.3 us  [the longest x18 21.9 us: swap(): lax.ppermute(x, axis, [(i, i ^ bit) for i in range(lax.axis_size(axis))])]
    unnamed x39 -> x12, local copies, waits for them, and re-layouts: 45.5 us -> 5.91 us
    slice x16 -> x0, local copies, waits for them, and re-layouts: 38 us -> none  [the longest x5 18 us: local_mix(): key_heads[:finish]]
    convert_element_type x4 -> x0, other arithmetic: 22.5 us -> none  [the longest x1 6.83 us: local(): normed.reshape(row_count, head_count * head_width).astype(jnp.bfloat16)]
  transfers between devices with their start and end apart: 4 -> 30, of which waited for: 3 -> 14; matrix products, arithmetic and copies ran while one was open for 38% -> 0% of each run, Pallas kernels for 0% -> 22%
where the time goes in v1:
time: 179 us; the launch traced here: 178 us
  waiting for transfers between devices  84 us (47%)
  Pallas kernels  46.5 us (26%)
  starting transfers between devices  41.3 us (23%)
  local copies, waits for them, and re-layouts  5.91 us (3%)
    ppermute x12, waiting for transfers between devices, shift(): return lax.ppermute(x, 'grp', [(i, (i + k) % parts) for i in range(parts)])  52.5 us
    pallas_call x26, Pallas kernels, call(): pl.pallas_call(kernel, out_shape=outs, grid_spec=pltpu.PrefetchScalarGrid...  46.5 us
    ppermute x18, waiting for transfers between devices, swap(): lax.ppermute(x, axis, [(i, i ^ bit) for i in range(lax.axis_size(axis))])  31.6 us
    ppermute x18, starting transfers between devices, swap(): lax.ppermute(x, axis, [(i, i ^ bit) for i in range(lax.axis_size(axis))])  21.9 us
    ppermute x12, starting transfers between devices, shift(): return lax.ppermute(x, 'grp', [(i, (i + k) % parts) for i in range(parts)])  19.4 us
    unnamed x12, local copies, waits for them, and re-layouts  5.91 us
  transfers between devices with their start and end apart: 30, of which 14 were waited for; matrix products, arithmetic and copies ran while one was open for 0% of the time, Pallas kernels for 22%

profile of v1, /device:TPU:10, one launch (start us, length us, event | category | flops | bytes accessed | tf_op | source)
XLA Modules:
  0.0 178.3 jit_solution(10871159276210309944)
XLA Ops:
  0.1 0.8 copy-done.4
  2.2 1.6 collective-permute-start
  3.8 1.2 collective-permute-start.1
  5.0 1.8 %collective-permute-start.2 = (f32[8,768]{1,0:T(8,128)S(1)}, f32[8,768]{1,0:T(8,128)S(1)}, u32[]{:S(2)}, u32[]{:S(2)}) collective-permute-start(f32[8,768]{1,0:T(8,128)S(1)} %get-tuple-element.51), channel_id=1, source_target_pairs={{0,24},{8,0},{16,8},{24,16},{1,25},{9,1},{17,9},{25,17},{2,26},{10... | collective-permute-start | bytes 73736 | tf_op jit(solution)/shard_map/ppermute | solution.py:343
  6.8 1.7 collective-permute-done.1.refs_2_
  8.9 1.0 shard_map.56
  9.9 2.2 %copy-done = bf16[512,4096]{1,0:T(8,128)(2,1)S(1)} copy-done((bf16[512,4096]{1,0:T(8,128)(2,1)S(1)}, bf16[512,4096]{1,0:T(8,128)(2,1)}, u32[]{:S(2)}) %copy-start) | copy-done | bytes 4194328
  12.1 2.2 %copy-done.2 = bf16[512,4096]{1,0:T(8,128)(2,1)S(1)} copy-done((bf16[512,4096]{1,0:T(8,128)(2,1)S(1)}, bf16[512,4096]{1,0:T(8,128)(2,1)}, u32[]{:S(2)}) %copy-start.2) | copy-done | bytes 4194328
  14.3 3.6 %shard_map.64 = (bf16[6,128,128]{2,1,0:T(8,128)(2,1)S(1)}, bf16[6,128,128]{2,1,0:T(8,128)(2,1)S(1)}) custom-call(s32[2]{0:T(128)S(1)} %pad_add_fusion.z_ref.s_ref, bf16[512,4096]{1,0:T(8,128)(2,1)S(1)} %copy-done, bf16[512,4096]{1,0:T(8,128)(2,1)S(1)} %copy-done.2, bf16[512,4096]{1,0:T(8,128)(2,1)S(1)} %copy-done, bf16[512,4096]{1,0:T(8,128)(2,1)S(1)} %copy-done.2, ...), custom_call_target="tpu_custom_call" | custom-call | flops 201326592 | bytes 3145728 | tf_op jit(solution)/shard_map/pallas_call | solution.py:106
  17.9 1.9 %collective-permute-start.12 = (bf16[6,128,128]{2,1,0:T(8,128)(2,1)S(1)}, bf16[6,128,128]{2,1,0:T(8,128)(2,1)S(1)}, u32[]{:S(2)}, u32[]{:S(2)}) collective-permute-start(bf16[6,128,128]{2,1,0:T(8,128)(2,1)S(1)} %get-tuple-element.68), channel_id=1, source_target_pairs={{0,8},{8,0},{16,24},{24,16},{1,9},{9,1},{17,25},{25,17},{2,10},{10... | collective-permute-start | bytes 589832 | tf_op jit(solution)/shard_map/ppermute | solution.py:346
  19.8 3.9 %collective-permute-done.12.got_ref.keep_got_ref = bf16[6,128,128]{2,1,0:T(8,128)(2,1)S(1)} collective-permute-done((bf16[6,128,128]{2,1,0:T(8,128)(2,1)S(1)}, bf16[6,128,128]{2,1,0:T(8,128)(2,1)S(1)}, u32[]{:S(2)}, u32[]{:S(2)}) %collective-permute-start.12) | collective-permute-done | bytes 196640 | tf_op jit(solution)/shard_map/ppermute | solution.py:346
  24.3 3.6 %collective-permute-start.13 = (bf16[6,128,128]{2,1,0:T(8,128)(2,1)S(1)}, bf16[6,128,128]{2,1,0:T(8,128)(2,1)S(1)}, u32[]{:S(2)}, u32[]{:S(2)}) collective-permute-start(bf16[6,128,128]{2,1,0:T(8,128)(2,1)S(1)} %shard_map.65.pair_ref), channel_id=1, source_target_pairs={{0,16},{8,24},{16,0},{24,8},{1,17},{9,25},{17,1},{25,9},{2,18},{10... | collective-permute-start | bytes 589832 | tf_op jit(solution)/shard_map/ppermute | solution.py:346
  27.8 3.6 %shard_map.57 = (bf16[6,128,128]{2,1,0:T(8,128)(2,1)S(1)}, bf16[6,128,128]{2,1,0:T(8,128)(2,1)S(1)}) custom-call(s32[2]{0:T(128)S(1)} %pad_add_fusion.z_ref.s_ref, bf16[512,4096]{1,0:T(8,128)(2,1)S(1)} %copy-done.1, bf16[512,4096]{1,0:T(8,128)(2,1)S(1)} %copy-done.2, bf16[512,4096]{1,0:T(8,128)(2,1)S(1)} %copy-done.1, bf16[512,4096]{1,0:T(8,128)(2,1)S(1)} %copy-done.2, ...), custom_call_target="tpu_custom_call" | custom-call | flops 201326592 | bytes 3145728 | tf_op jit(solution)/shard_map/pallas_call | solution.py:106
  31.5 1.5 collective-permute-done.13.got_ref.low_ref
  33.8 2.6 %shard_map.71 = (bf16[4,128,128]{2,1,0:T(8,128)(2,1)S(1)}, bf16[4,128,128]{2,1,0:T(8,128)(2,1)S(1)}) custom-call(s32[2]{0:T(128)S(1)} %pad_add_fusion.z_ref.s_ref, bf16[512,4096]{1,0:T(8,128)(2,1)S(1)} %copy-done.1, bf16[512,4096]{1,0:T(8,128)(2,1)S(1)} %copy-done.2, bf16[512,4096]{1,0:T(8,128)(2,1)S(1)} %copy-done.1, bf16[512,4096]{1,0:T(8,128)(2,1)S(1)} %copy-done.2, ...), custom_call_target="tpu_custom_call" | custom-call | flops 134217728 | bytes 2097152 | tf_op jit(solution)/shard_map/pallas_call | solution.py:106
  36.4 2.6 %collective-permute-start.21 = (bf16[4,128,128]{2,1,0:T(8,128)(2,1)S(1)}, bf16[4,128,128]{2,1,0:T(8,128)(2,1)S(1)}, u32[]{:S(2)}, u32[]{:S(2)}) collective-permute-start(bf16[4,128,128]{2,1,0:T(8,128)(2,1)S(1)} %get-tuple-element.80), channel_id=1, source_target_pairs={{0,8},{8,0},{16,24},{24,16},{1,9},{9,1},{17,25},{25,17},{2,10},{10... | collective-permute-start | bytes 393224 | tf_op jit(solution)/shard_map/ppermute | solution.py:346
  39.7 1.1 collective-permute-start.4
  42.0 2.2 %collective-permute-done.21.got_ref.keep_got_ref = bf16[4,128,128]{2,1,0:T(8,128)(2,1)S(1)} collective-permute-done((bf16[4,128,128]{2,1,0:T(8,128)(2,1)S(1)}, bf16[4,128,128]{2,1,0:T(8,128)(2,1)S(1)}, u32[]{:S(2)}, u32[]{:S(2)}) %collective-permute-start.21) | collective-permute-done | bytes 131104 | tf_op jit(solution)/shard_map/ppermute | solution.py:346
  44.9 2.9 %collective-permute-start.22 = (bf16[4,128,128]{2,1,0:T(8,128)(2,1)S(1)}, bf16[4,128,128]{2,1,0:T(8,128)(2,1)S(1)}, u32[]{:S(2)}, u32[]{:S(2)}) collective-permute-start(bf16[4,128,128]{2,1,0:T(8,128)(2,1)S(1)} %shard_map.72.pair_ref), channel_id=1, source_target_pairs={{0,16},{8,24},{16,0},{24,8},{1,17},{9,25},{17,1},{25,9},{2,18},{10... | collective-permute-start | bytes 393224 | tf_op jit(solution)/shard_map/ppermute | solution.py:346
  47.8 5.3 %collective-permute-done.4.got_ref.low_ref = bf16[6,128,128]{2,1,0:T(8,128)(2,1)S(1)} collective-permute-done((bf16[6,128,128]{2,1,0:T(8,128)(2,1)S(1)}, bf16[6,128,128]{2,1,0:T(8,128)(2,1)S(1)}, u32[]{:S(2)}, u32[]{:S(2)}) %collective-permute-start.4) | collective-permute-done | bytes 196640 | tf_op jit(solution)/shard_map/ppermute | solution.py:346
  53.8 1.7 collective-permute-done.22.got_ref.low_ref
  56.2 0.7 shard_map.68
  56.9 1.6 collective-permute-start.16
  60.4 1.6 collective-permute-start.6
  62.0 2.8 %collective-permute-done.16.got_ref = bf16[6,144,128]{2,1,0:T(8,128)(2,1)S(1)} collective-permute-done((bf16[6,144,128]{2,1,0:T(8,128)(2,1)S(1)}, bf16[6,144,128]{2,1,0:T(8,128)(2,1)S(1)}, u32[]{:S(2)}, u32[]{:S(2)}) %collective-permute-start.16) | collective-permute-done | bytes 221216 | tf_op jit(solution)/shard_map/ppermute | solution.py:346
  64.8 0.8 shard_map.69
  65.5 2.5 %collective-permute-start.17 = (bf16[6,128,128]{2,1,0:T(8,128)(2,1)S(1)}, bf16[6,128,128]{2,1,0:T(8,128)(2,1)S(1)}, u32[]{:S(2)}, u32[]{:S(2)}) collective-permute-start(bf16[6,128,128]{2,1,0:T(8,128)(2,1)S(1)} %get-tuple-element.74), channel_id=1, source_target_pairs={{0,8},{8,0},{16,24},{24,16},{1,9},{9,1},{17,25},{25,17},{2,10},{10... | collective-permute-start | bytes 589832 | tf_op jit(solution)/shard_map/ppermute | solution.py:346
  68.7 1.6 collective-permute-start.25
  71.6 3.6 %collective-permute-done.25.got_ref = bf16[4,144,128]{2,1,0:T(8,128)(2,1)S(1)} collective-permute-done((bf16[4,144,128]{2,1,0:T(8,128)(2,1)S(1)}, bf16[4,144,128]{2,1,0:T(8,128)(2,1)S(1)}, u32[]{:S(2)}, u32[]{:S(2)}) %collective-permute-start.25) | collective-permute-done | bytes 147488 | tf_op jit(solution)/shard_map/ppermute | solution.py:346
  76.0 7.4 %shard_map.70 = (bf16[512,384]{1,0:T(8,128)(2,1)S(1)}, bf16[512,384]{1,0:T(8,128)(2,1)S(1)}, bf16[512,384]{1,0:T(8,128)(2,1)S(1)}, bf16[512,384]{1,0:T(8,128)(2,1)S(1)}) custom-call(s32[2]{0:T(128)S(1)} %pad_add_fusion.z_ref.s_ref, bf16[512,4096]{1,0:T(8,128)(2,1)S(1)} %copy-done.3, bf16[512,4096]{1,0:T(8,128)(2,1)S(1)} %copy-done.1, ...), custom_call_target="tpu_custom_call" | custom-call | flops 1610612736 | bytes 6291456 | tf_op jit(solution)/shard_map/pallas_call | solution.py:106
  83.4 1.5 collective-permute-start.18
  84.9 0.8 shard_map.62
  86.3 5.1 %shard_map.77 = (bf16[512,256]{1,0:T(8,128)(2,1)S(1)}, bf16[512,256]{1,0:T(8,128)(2,1)S(1)}, bf16[512,256]{1,0:T(8,128)(2,1)S(1)}, bf16[512,256]{1,0:T(8,128)(2,1)S(1)}) custom-call(s32[2]{0:T(128)S(1)} %pad_add_fusion.z_ref.s_ref, bf16[512,4096]{1,0:T(8,128)(2,1)S(1)} %copy-done.3, bf16[512,4096]{1,0:T(8,128)(2,1)S(1)} %copy-done.1, ...), custom_call_target="tpu_custom_call" | custom-call | flops 1073741824 | bytes 4194304 | tf_op jit(solution)/shard_map/pallas_call | solution.py:106
  91.5 2.9 %collective-permute-start.27 = (bf16[512,256]{1,0:T(8,128)(2,1)S(1)}, bf16[512,256]{1,0:T(8,128)(2,1)S(1)}, u32[]{:S(2)}, u32[]{:S(2)}) collective-permute-start(bf16[512,256]{1,0:T(8,128)(2,1)S(1)} %get-tuple-element.88), channel_id=1, source_target_pairs={{0,8},{8,16},{16,24},{24,0},{1,9},{9,17},{17,25},{25,1},{2,10},{10... | collective-permute-start | bytes 786440 | tf_op jit(solution)/shard_map/ppermute | solution.py:343
  94.4 1.0 collective-permute-start.28
  95.4 1.1 collective-permute-start.29
  96.5 10.6 %collective-permute-done.8.refs_7_.refs_15_ = bf16[6,128,128]{2,1,0:T(8,128)(2,1)S(1)} collective-permute-done((bf16[6,128,128]{2,1,0:T(8,128)(2,1)S(1)}, bf16[6,128,128]{2,1,0:T(8,128)(2,1)S(1)}, u32[]{:S(2)}, u32[]{:S(2)}) %collective-permute-start.8) | collective-permute-done | bytes 196640 | tf_op jit(solution)/shard_map/ppermute | solution.py:346
  107.1 7.4 %shard_map.63 = (bf16[512,384]{1,0:T(8,128)(2,1)S(1)}, bf16[512,384]{1,0:T(8,128)(2,1)S(1)}, bf16[512,384]{1,0:T(8,128)(2,1)S(1)}, bf16[512,384]{1,0:T(8,128)(2,1)S(1)}) custom-call(s32[2]{0:T(128)S(1)} %pad_add_fusion.z_ref.s_ref, bf16[512,4096]{1,0:T(8,128)(2,1)S(1)} %copy-done.3, bf16[512,4096]{1,0:T(8,128)(2,1)S(1)} %copy-done.1, ...), custom_call_target="tpu_custom_call" | custom-call | flops 1610612736 | bytes 6291456 | tf_op jit(solution)/shard_map/pallas_call | solution.py:106
  114.5 2.8 %collective-permute-start.20 = (bf16[512,384]{1,0:T(8,128)(2,1)S(1)}, bf16[512,384]{1,0:T(8,128)(2,1)S(1)}, u32[]{:S(2)}, u32[]{:S(2)}) collective-permute-start(bf16[512,384]{1,0:T(8,128)(2,1)S(1)} %get-tuple-element.78), channel_id=1, source_target_pairs={{0,24},{8,0},{16,8},{24,16},{1,25},{9,1},{17,9},{25,17},{2,26},{10... | collective-permute-start | bytes 1179656 | tf_op jit(solution)/shard_map/ppermute | solution.py:343
  117.3 29.1 %collective-permute-done.28.refs_2_ = bf16[512,256]{1,0:T(8,128)(2,1)S(1)} collective-permute-done((bf16[512,256]{1,0:T(8,128)(2,1)S(1)}, bf16[512,256]{1,0:T(8,128)(2,1)S(1)}, u32[]{:S(2)}, u32[]{:S(2)}) %collective-permute-start.28) | collective-permute-done | bytes 262176 | tf_op jit(solution)/shard_map/ppermute | solution.py:343
  146.4 3.4 %collective-permute-start.10 = (bf16[512,384]{1,0:T(8,128)(2,1)S(1)}, bf16[512,384]{1,0:T(8,128)(2,1)S(1)}, u32[]{:S(2)}, u32[]{:S(2)}) collective-permute-start(bf16[512,384]{1,0:T(8,128)(2,1)S(1)} %get-tuple-element.65), channel_id=1, source_target_pairs={{0,16},{8,24},{16,0},{24,8},{1,17},{9,25},{17,1},{25,9},{2,18},{10... | collective-permute-start | bytes 1179656 | tf_op jit(solution)/shard_map/ppermute | solution.py:343
  149.8 2.0 %collective-permute-start.9 = (bf16[512,384]{1,0:T(8,128)(2,1)S(1)}, bf16[512,384]{1,0:T(8,128)(2,1)S(1)}, u32[]{:S(2)}, u32[]{:S(2)}) collective-permute-start(bf16[512,384]{1,0:T(8,128)(2,1)S(1)} %get-tuple-element.64), channel_id=1, source_target_pairs={{0,8},{8,16},{16,24},{24,0},{1,9},{9,17},{17,25},{25,1},{2,10},{10... | collective-permute-start | bytes 1179656 | tf_op jit(solution)/shard_map/ppermute | solution.py:343
  151.8 1.5 shard_map.78.refs_4_
  153.3 5.7 %collective-permute-done.19.refs_2_ = bf16[512,384]{1,0:T(8,128)(2,1)S(1)} collective-permute-done((bf16[512,384]{1,0:T(8,128)(2,1)S(1)}, bf16[512,384]{1,0:T(8,128)(2,1)S(1)}, u32[]{:S(2)}, u32[]{:S(2)}) %collective-permute-start.19) | collective-permute-done | bytes 393248 | tf_op jit(solution)/shard_map/ppermute | solution.py:343
  159.0 1.7 shard_map.79.refs_4_
  160.8 6.7 %collective-permute-done.10.refs_2_ = bf16[512,384]{1,0:T(8,128)(2,1)S(1)} collective-permute-done((bf16[512,384]{1,0:T(8,128)(2,1)S(1)}, bf16[512,384]{1,0:T(8,128)(2,1)S(1)}, u32[]{:S(2)}, u32[]{:S(2)}) %collective-permute-start.10) | collective-permute-done | bytes 393248 | tf_op jit(solution)/shard_map/ppermute | solution.py:343
  167.5 8.9 %collective-permute-done.11.refs_3_ = bf16[512,384]{1,0:T(8,128)(2,1)S(1)} collective-permute-done((bf16[512,384]{1,0:T(8,128)(2,1)S(1)}, bf16[512,384]{1,0:T(8,128)(2,1)S(1)}, u32[]{:S(2)}, u32[]{:S(2)}) %collective-permute-start.11) | collective-permute-done | bytes 393248 | tf_op jit(solution)/shard_map/ppermute | solution.py:343
  176.4 1.7 shard_map.80
  (51 shorter events, 12.4 us)
Async XLA Ops:
  0.1 0.8 copy-start.4
  0.9 0.7 copy-start.5
  2.2 4.6 %collective-permute-start = (f32[8,768]{1,0:T(8,128)S(1)}, f32[8,768]{1,0:T(8,128)S(1)}, u32[]{:S(2)}, u32[]{:S(2)}) collective-permute-start(f32[8,768]{1,0:T(8,128)S(1)} %get-tuple-element.49), channel_id=1, source_target_pairs={{0,8},{8,16},{16,24},{24,0},{1,9},{9,17},{17,25},{25,1},{2,10},{10... | collective-permute-start | bytes 73736 | tf_op jit(solution)/shard_map/ppermute | solution.py:343
  3.8 4.7 %collective-permute-start.1 = (f32[8,768]{1,0:T(8,128)S(1)}, f32[8,768]{1,0:T(8,128)S(1)}, u32[]{:S(2)}, u32[]{:S(2)}) collective-permute-start(f32[8,768]{1,0:T(8,128)S(1)} %get-tuple-element.50), channel_id=1, source_target_pairs={{0,16},{8,24},{16,0},{24,8},{1,17},{9,25},{17,1},{25,9},{2,18},{10... | collective-permute-start | bytes 73736 | tf_op jit(solution)/shard_map/ppermute | solution.py:343
  5.0 3.8 %collective-permute-start.2 = (f32[8,768]{1,0:T(8,128)S(1)}, f32[8,768]{1,0:T(8,128)S(1)}, u32[]{:S(2)}, u32[]{:S(2)}) collective-permute-start(f32[8,768]{1,0:T(8,128)S(1)} %get-tuple-element.51), channel_id=1, source_target_pairs={{0,24},{8,0},{16,8},{24,16},{1,25},{9,1},{17,9},{25,17},{2,26},{10... | collective-permute-start | bytes 73736 | tf_op jit(solution)/shard_map/ppermute | solution.py:343
  9.9 2.2 %copy-start = (bf16[512,4096]{1,0:T(8,128)(2,1)S(1)}, bf16[512,4096]{1,0:T(8,128)(2,1)}, u32[]{:S(2)}) copy-start(bf16[512,4096]{1,0:T(8,128)(2,1)} %refs_13_.5) | copy-start | bytes 12582916
  12.1 2.2 %copy-start.2 = (bf16[512,4096]{1,0:T(8,128)(2,1)S(1)}, bf16[512,4096]{1,0:T(8,128)(2,1)}, u32[]{:S(2)}) copy-start(bf16[512,4096]{1,0:T(8,128)(2,1)} %refs_14_.5) | copy-start | bytes 12582916
  14.3 13.6 %copy-start.1 = (bf16[512,4096]{1,0:T(8,128)(2,1)S(1)}, bf16[512,4096]{1,0:T(8,128)(2,1)}, u32[]{:S(2)}) copy-start(bf16[512,4096]{1,0:T(8,128)(2,1)} %refs_13_.5) | copy-start | bytes 12582916
  17.9 5.7 %collective-permute-start.12 = (bf16[6,128,128]{2,1,0:T(8,128)(2,1)S(1)}, bf16[6,128,128]{2,1,0:T(8,128)(2,1)S(1)}, u32[]{:S(2)}, u32[]{:S(2)}) collective-permute-start(bf16[6,128,128]{2,1,0:T(8,128)(2,1)S(1)} %get-tuple-element.68), channel_id=1, source_target_pairs={{0,8},{8,0},{16,24},{24,16},{1,9},{9,1},{17,25},{25,17},{2,10},{10... | collective-permute-start | bytes 589832 | tf_op jit(solution)/shard_map/ppermute | solution.py:346
  24.3 8.8 %collective-permute-start.13 = (bf16[6,128,128]{2,1,0:T(8,128)(2,1)S(1)}, bf16[6,128,128]{2,1,0:T(8,128)(2,1)S(1)}, u32[]{:S(2)}, u32[]{:S(2)}) collective-permute-start(bf16[6,128,128]{2,1,0:T(8,128)(2,1)S(1)} %shard_map.65.pair_ref), channel_id=1, source_target_pairs={{0,16},{8,24},{16,0},{24,8},{1,17},{9,25},{17,1},{25,9},{2,18},{10... | collective-permute-start | bytes 589832 | tf_op jit(solution)/shard_map/ppermute | solution.py:346
  31.5 7.6 %collective-permute-start.3 = (bf16[6,128,128]{2,1,0:T(8,128)(2,1)S(1)}, bf16[6,128,128]{2,1,0:T(8,128)(2,1)S(1)}, u32[]{:S(2)}, u32[]{:S(2)}) collective-permute-start(bf16[6,128,128]{2,1,0:T(8,128)(2,1)S(1)} %get-tuple-element.54), channel_id=1, source_target_pairs={{0,8},{8,0},{16,24},{24,16},{1,9},{9,1},{17,25},{25,17},{2,10},{10... | collective-permute-start | bytes 589832 | tf_op jit(solution)/shard_map/ppermute | solution.py:346
  33.7 7.0 %collective-permute-start.14 = (bf16[6,144,128]{2,1,0:T(8,128)(2,1)S(1)}, bf16[6,144,128]{2,1,0:T(8,128)(2,1)S(1)}, u32[]{:S(2)}, u32[]{:S(2)}) collective-permute-start(bf16[6,144,128]{2,1,0:T(8,128)(2,1)S(1)} %shard_map.66.own_ref), channel_id=1, source_target_pairs={{0,1},{1,0},{2,3},{3,2},{4,5},{5,4},{6,7},{7,6},{8,9},{9,8},{10,11... | collective-permute-start | bytes 663560 | tf_op jit(solution)/shard_map/ppermute | solution.py:346
  36.4 7.8 %collective-permute-start.21 = (bf16[4,128,128]{2,1,0:T(8,128)(2,1)S(1)}, bf16[4,128,128]{2,1,0:T(8,128)(2,1)S(1)}, u32[]{:S(2)}, u32[]{:S(2)}) collective-permute-start(bf16[4,128,128]{2,1,0:T(8,128)(2,1)S(1)} %get-tuple-element.80), channel_id=1, source_target_pairs={{0,8},{8,0},{16,24},{24,16},{1,9},{9,1},{17,25},{25,17},{2,10},{10... | collective-permute-start | bytes 393224 | tf_op jit(solution)/shard_map/ppermute | solution.py:346
  39.0 37.0 %copy-start.3 = (bf16[512,4096]{1,0:T(8,128)(2,1)S(1)}, bf16[512,4096]{1,0:T(8,128)(2,1)}, u32[]{:S(2)}) copy-start(bf16[512,4096]{1,0:T(8,128)(2,1)} %refs_12_.5) | copy-start | bytes 12582916
  39.7 13.4 %collective-permute-start.4 = (bf16[6,128,128]{2,1,0:T(8,128)(2,1)S(1)}, bf16[6,128,128]{2,1,0:T(8,128)(2,1)S(1)}, u32[]{:S(2)}, u32[]{:S(2)}) collective-permute-start(bf16[6,128,128]{2,1,0:T(8,128)(2,1)S(1)} %shard_map.58.pair_ref), channel_id=1, source_target_pairs={{0,16},{8,24},{16,0},{24,8},{1,17},{9,25},{17,1},{25,9},{2,18},{10... | collective-permute-start | bytes 589832 | tf_op jit(solution)/shard_map/ppermute | solution.py:346
  41.4 14.7 %collective-permute-start.15 = (bf16[6,144,128]{2,1,0:T(8,128)(2,1)S(1)}, bf16[6,144,128]{2,1,0:T(8,128)(2,1)S(1)}, u32[]{:S(2)}, u32[]{:S(2)}) collective-permute-start(bf16[6,144,128]{2,1,0:T(8,128)(2,1)S(1)} %get-tuple-element.69.own_ref), channel_id=1, source_target_pairs={{0,2},{1,3},{2,0},{3,1},{4,6},{5,7},{6,4},{7,5},{8,10},{9,11},{10,... | collective-permute-start | bytes 663560 | tf_op jit(solution)/shard_map/ppermute | solution.py:346
  44.9 10.5 %collective-permute-start.22 = (bf16[4,128,128]{2,1,0:T(8,128)(2,1)S(1)}, bf16[4,128,128]{2,1,0:T(8,128)(2,1)S(1)}, u32[]{:S(2)}, u32[]{:S(2)}) collective-permute-start(bf16[4,128,128]{2,1,0:T(8,128)(2,1)S(1)} %shard_map.72.pair_ref), channel_id=1, source_target_pairs={{0,16},{8,24},{16,0},{24,8},{1,17},{9,25},{17,1},{25,9},{2,18},{10... | collective-permute-start | bytes 393224 | tf_op jit(solution)/shard_map/ppermute | solution.py:346
  53.7 6.0 %collective-permute-start.5 = (bf16[6,144,128]{2,1,0:T(8,128)(2,1)S(1)}, bf16[6,144,128]{2,1,0:T(8,128)(2,1)S(1)}, u32[]{:S(2)}, u32[]{:S(2)}) collective-permute-start(bf16[6,144,128]{2,1,0:T(8,128)(2,1)S(1)} %shard_map.59.own_ref), channel_id=1, source_target_pairs={{0,1},{1,0},{2,3},{3,2},{4,5},{5,4},{6,7},{7,6},{8,9},{9,8},{10,11... | collective-permute-start | bytes 663560 | tf_op jit(solution)/shard_map/ppermute | solution.py:346
  56.1 2.4 %collective-permute-start.23 = (bf16[4,144,128]{2,1,0:T(8,128)(2,1)S(1)}, bf16[4,144,128]{2,1,0:T(8,128)(2,1)S(1)}, u32[]{:S(2)}, u32[]{:S(2)}) collective-permute-start(bf16[4,144,128]{2,1,0:T(8,128)(2,1)S(1)} %shard_map.73.own_ref), channel_id=1, source_target_pairs={{0,1},{1,0},{2,3},{3,2},{4,5},{5,4},{6,7},{7,6},{8,9},{9,8},{10,11... | collective-permute-start | bytes 442376 | tf_op jit(solution)/shard_map/ppermute | solution.py:346
  56.9 7.9 %collective-permute-start.16 = (bf16[6,144,128]{2,1,0:T(8,128)(2,1)S(1)}, bf16[6,144,128]{2,1,0:T(8,128)(2,1)S(1)}, u32[]{:S(2)}, u32[]{:S(2)}) collective-permute-start(bf16[6,144,128]{2,1,0:T(8,128)(2,1)S(1)} %get-tuple-element.71.own_ref), channel_id=1, source_target_pairs={{0,4},{1,5},{2,6},{3,7},{4,0},{5,1},{6,2},{7,3},{8,12},{9,13},{10,... | collective-permute-start | bytes 663560 | tf_op jit(solution)/shard_map/ppermute | solution.py:346
  59.1 9.0 %collective-permute-start.24 = (bf16[4,144,128]{2,1,0:T(8,128)(2,1)S(1)}, bf16[4,144,128]{2,1,0:T(8,128)(2,1)S(1)}, u32[]{:S(2)}, u32[]{:S(2)}) collective-permute-start(bf16[4,144,128]{2,1,0:T(8,128)(2,1)S(1)} %get-tuple-element.81.own_ref), channel_id=1, source_target_pairs={{0,2},{1,3},{2,0},{3,1},{4,6},{5,7},{6,4},{7,5},{8,10},{9,11},{10,... | collective-permute-start | bytes 442376 | tf_op jit(solution)/shard_map/ppermute | solution.py:346
  60.4 9.9 %collective-permute-start.6 = (bf16[6,144,128]{2,1,0:T(8,128)(2,1)S(1)}, bf16[6,144,128]{2,1,0:T(8,128)(2,1)S(1)}, u32[]{:S(2)}, u32[]{:S(2)}) collective-permute-start(bf16[6,144,128]{2,1,0:T(8,128)(2,1)S(1)} %get-tuple-element.56.own_ref), channel_id=1, source_target_pairs={{0,2},{1,3},{2,0},{3,1},{4,6},{5,7},{6,4},{7,5},{8,10},{9,11},{10,... | collective-permute-start | bytes 663560 | tf_op jit(solution)/shard_map/ppermute | solution.py:346
  65.5 10.4 %collective-permute-start.17 = (bf16[6,128,128]{2,1,0:T(8,128)(2,1)S(1)}, bf16[6,128,128]{2,1,0:T(8,128)(2,1)S(1)}, u32[]{:S(2)}, u32[]{:S(2)}) collective-permute-start(bf16[6,128,128]{2,1,0:T(8,128)(2,1)S(1)} %get-tuple-element.74), channel_id=1, source_target_pairs={{0,8},{8,0},{16,24},{24,16},{1,9},{9,1},{17,25},{25,17},{2,10},{10... | collective-permute-start | bytes 589832 | tf_op jit(solution)/shard_map/ppermute | solution.py:346
  68.7 6.5 %collective-permute-start.25 = (bf16[4,144,128]{2,1,0:T(8,128)(2,1)S(1)}, bf16[4,144,128]{2,1,0:T(8,128)(2,1)S(1)}, u32[]{:S(2)}, u32[]{:S(2)}) collective-permute-start(bf16[4,144,128]{2,1,0:T(8,128)(2,1)S(1)} %get-tuple-element.83.own_ref), channel_id=1, source_target_pairs={{0,4},{1,5},{2,6},{3,7},{4,0},{5,1},{6,2},{7,3},{8,12},{9,13},{10,... | collective-permute-start | bytes 442376 | tf_op jit(solution)/shard_map/ppermute | solution.py:346
  71.0 13.9 %collective-permute-start.7 = (bf16[6,144,128]{2,1,0:T(8,128)(2,1)S(1)}, bf16[6,144,128]{2,1,0:T(8,128)(2,1)S(1)}, u32[]{:S(2)}, u32[]{:S(2)}) collective-permute-start(bf16[6,144,128]{2,1,0:T(8,128)(2,1)S(1)} %get-tuple-element.58.own_ref), channel_id=1, source_target_pairs={{0,4},{1,5},{2,6},{3,7},{4,0},{5,1},{6,2},{7,3},{8,12},{9,13},{10,... | collective-permute-start | bytes 663560 | tf_op jit(solution)/shard_map/ppermute | solution.py:346
  75.9 10.4 %collective-permute-start.26 = (bf16[4,128,128]{2,1,0:T(8,128)(2,1)S(1)}, bf16[4,128,128]{2,1,0:T(8,128)(2,1)S(1)}, u32[]{:S(2)}, u32[]{:S(2)}) collective-permute-start(bf16[4,128,128]{2,1,0:T(8,128)(2,1)S(1)} %get-tuple-element.86), channel_id=1, source_target_pairs={{0,8},{8,0},{16,24},{24,16},{1,9},{9,1},{17,25},{25,17},{2,10},{10... | collective-permute-start | bytes 393224 | tf_op jit(solution)/shard_map/ppermute | solution.py:346
  83.4 66.4 %collective-permute-start.18 = (bf16[512,384]{1,0:T(8,128)(2,1)S(1)}, bf16[512,384]{1,0:T(8,128)(2,1)S(1)}, u32[]{:S(2)}, u32[]{:S(2)}) collective-permute-start(bf16[512,384]{1,0:T(8,128)(2,1)S(1)} %get-tuple-element.76), channel_id=1, source_target_pairs={{0,8},{8,16},{16,24},{24,0},{1,9},{9,17},{17,25},{25,1},{2,10},{10... | collective-permute-start | bytes 1179656 | tf_op jit(solution)/shard_map/ppermute | solution.py:343
  85.7 21.3 %collective-permute-start.8 = (bf16[6,128,128]{2,1,0:T(8,128)(2,1)S(1)}, bf16[6,128,128]{2,1,0:T(8,128)(2,1)S(1)}, u32[]{:S(2)}, u32[]{:S(2)}) collective-permute-start(bf16[6,128,128]{2,1,0:T(8,128)(2,1)S(1)} %get-tuple-element.61), channel_id=1, source_target_pairs={{0,8},{8,0},{16,24},{24,16},{1,9},{9,1},{17,25},{25,17},{2,10},{10... | collective-permute-start | bytes 589832 | tf_op jit(solution)/shard_map/ppermute | solution.py:346
  91.5 23.0 %collective-permute-start.27 = (bf16[512,256]{1,0:T(8,128)(2,1)S(1)}, bf16[512,256]{1,0:T(8,128)(2,1)S(1)}, u32[]{:S(2)}, u32[]{:S(2)}) collective-permute-start(bf16[512,256]{1,0:T(8,128)(2,1)S(1)} %get-tuple-element.88), channel_id=1, source_target_pairs={{0,8},{8,16},{16,24},{24,0},{1,9},{9,17},{17,25},{25,1},{2,10},{10... | collective-permute-start | bytes 786440 | tf_op jit(solution)/shard_map/ppermute | solution.py:343
  94.4 51.9 %collective-permute-start.28 = (bf16[512,256]{1,0:T(8,128)(2,1)S(1)}, bf16[512,256]{1,0:T(8,128)(2,1)S(1)}, u32[]{:S(2)}, u32[]{:S(2)}) collective-permute-start(bf16[512,256]{1,0:T(8,128)(2,1)S(1)} %get-tuple-element.89), channel_id=1, source_target_pairs={{0,16},{8,24},{16,0},{24,8},{1,17},{9,25},{17,1},{25,9},{2,18},{10... | collective-permute-start | bytes 786440 | tf_op jit(solution)/shard_map/ppermute | solution.py:343
  95.4 54.4 %collective-permute-start.29 = (bf16[512,256]{1,0:T(8,128)(2,1)S(1)}, bf16[512,256]{1,0:T(8,128)(2,1)S(1)}, u32[]{:S(2)}, u32[]{:S(2)}) collective-permute-start(bf16[512,256]{1,0:T(8,128)(2,1)S(1)} %get-tuple-element.90), channel_id=1, source_target_pairs={{0,24},{8,0},{16,8},{24,16},{1,25},{9,1},{17,9},{25,17},{2,26},{10... | collective-permute-start | bytes 786440 | tf_op jit(solution)/shard_map/ppermute | solution.py:343
  107.1 52.0 %collective-permute-start.19 = (bf16[512,384]{1,0:T(8,128)(2,1)S(1)}, bf16[512,384]{1,0:T(8,128)(2,1)S(1)}, u32[]{:S(2)}, u32[]{:S(2)}) collective-permute-start(bf16[512,384]{1,0:T(8,128)(2,1)S(1)} %get-tuple-element.77), channel_id=1, source_target_pairs={{0,16},{8,24},{16,0},{24,8},{1,17},{9,25},{17,1},{25,9},{2,18},{10... | collective-permute-start | bytes 1179656 | tf_op jit(solution)/shard_map/ppermute | solution.py:343
  114.5 44.6 %collective-permute-start.20 = (bf16[512,384]{1,0:T(8,128)(2,1)S(1)}, bf16[512,384]{1,0:T(8,128)(2,1)S(1)}, u32[]{:S(2)}, u32[]{:S(2)}) collective-permute-start(bf16[512,384]{1,0:T(8,128)(2,1)S(1)} %get-tuple-element.78), channel_id=1, source_target_pairs={{0,24},{8,0},{16,8},{24,16},{1,25},{9,1},{17,9},{25,17},{2,26},{10... | collective-permute-start | bytes 1179656 | tf_op jit(solution)/shard_map/ppermute | solution.py:343
  146.4 21.1 %collective-permute-start.10 = (bf16[512,384]{1,0:T(8,128)(2,1)S(1)}, bf16[512,384]{1,0:T(8,128)(2,1)S(1)}, u32[]{:S(2)}, u32[]{:S(2)}) collective-permute-start(bf16[512,384]{1,0:T(8,128)(2,1)S(1)} %get-tuple-element.65), channel_id=1, source_target_pairs={{0,16},{8,24},{16,0},{24,8},{1,17},{9,25},{17,1},{25,9},{2,18},{10... | collective-permute-start | bytes 1179656 | tf_op jit(solution)/shard_map/ppermute | solution.py:343
  149.7 26.7 %collective-permute-start.11 = (bf16[512,384]{1,0:T(8,128)(2,1)S(1)}, bf16[512,384]{1,0:T(8,128)(2,1)S(1)}, u32[]{:S(2)}, u32[]{:S(2)}) collective-permute-start(bf16[512,384]{1,0:T(8,128)(2,1)S(1)} %get-tuple-element.66), channel_id=1, source_target_pairs={{0,24},{8,0},{16,8},{24,16},{1,25},{9,1},{17,9},{25,17},{2,26},{10... | collective-permute-start | bytes 1179656 | tf_op jit(solution)/shard_map/ppermute | solution.py:343
  149.8 26.7 %collective-permute-start.9 = (bf16[512,384]{1,0:T(8,128)(2,1)S(1)}, bf16[512,384]{1,0:T(8,128)(2,1)S(1)}, u32[]{:S(2)}, u32[]{:S(2)}) collective-permute-start(bf16[512,384]{1,0:T(8,128)(2,1)S(1)} %get-tuple-element.64), channel_id=1, source_target_pairs={{0,8},{8,16},{16,24},{24,0},{1,9},{9,17},{17,25},{25,1},{2,10},{10... | collective-permute-start | bytes 1179656 | tf_op jit(solution)/shard_map/ppermute | solution.py:343

commit v2 on v1

v2 whole, which is shorter than its diff:
```python
import functools

import jax
import jax.numpy as jnp
from jax import lax
from jax.experimental import pallas as pl
from jax.experimental.pallas import tpu as pltpu
from jax.sharding import PartitionSpec as P

GROUPS = ((3, 0, (1, 2)), (5, 0, (1, 2, 2)))
ORDER = ('k0', 'k1', 'k0', 'k0', 'k1', 'k0', 'k0', 'k1', 'k0', 'k1', 'k0', 'w001', 'k1', 'w003', 'k0', 'w002', 'k1', 'w011', 'k1', 'w012', 'k1', 'w013', 'w101', 'k1', 'p00', 'p01', 'p10', 'p11', 'p12')
CHUNK = 256
VMEM_BYTES = 16 * 1024 * 1024
SCALE = 1.0e9
STREAM_VMEM_BYTES = 16 * 1024 * 1024
F32 = jnp.float32
BF16 = jnp.bfloat16


def entering_2(array, axis, combine, identity):
    length, mine = (lax.axis_size(axis), lax.axis_index(axis))
    everything = jax.tree.map(lambda part: lax.all_gather(part, axis), array)
    start = jax.tree.map(
        lambda part, zero: jnp.broadcast_to(jnp.asarray(zero, part.dtype), part.shape),
        array,
        identity,
    )

    def step(k, before):
        reached = k < mine
        new = combine(before, jax.tree.map(lambda part: part[k], everything))
        return jax.tree.map(lambda a, b: jnp.where(reached, a, b), new, before)

    return lax.fori_loop(0, length, step, start)


def local_mix(query_heads, key_heads, value_heads, levels):
    row_total = query_heads.shape[0]
    block_rows = min(512, row_total)
    pieces = []
    for start in range(0, row_total, block_rows):
        finish = start + block_rows
        scores = jnp.einsum(
            "thd,shd->hts",
            query_heads[start:finish],
            key_heads[:finish],
            preferred_element_type=jnp.float32,
        )
        causal = (
            jnp.arange(start, finish, dtype=jnp.int32)[:, None]
            >= jnp.arange(finish, dtype=jnp.int32)[None, :]
        )
        decay_gap = jnp.where(
            causal[None], levels[:, start:finish, None] - levels[:, None, :finish], 0.0
        )
        weights = jnp.where(causal[None], scores * jnp.exp(decay_gap), 0.0).astype(jnp.bfloat16)
        pieces.append(
            jnp.einsum(
                "hts,shd->thd", weights, value_heads[:finish], preferred_element_type=jnp.float32
            )
        )
    return jnp.concatenate(pieces, axis=0)


def local_any(queries, keys, values, log_decay, gain):
    head_count = log_decay.shape[0]
    row_count = log_decay.shape[1]
    head_width = gain.shape[0] // head_count
    query_rows, key_rows, value_rows = (
        lax.all_to_all(queries, "grp", split_axis=1, concat_axis=0, tiled=True),
        lax.all_to_all(keys, "grp", split_axis=1, concat_axis=0, tiled=True),
        lax.all_to_all(values, "grp", split_axis=1, concat_axis=0, tiled=True),
    )
    key_heads = key_rows.reshape(row_count, head_count, head_width)
    value_heads = value_rows.reshape(row_count, head_count, head_width)
    levels = jnp.cumsum(log_decay, axis=1)
    block_total = levels[:, -1]
    tail_decay = jnp.exp(block_total[:, None] - levels)
    scaled_keys = (key_heads.astype(jnp.float32) * tail_decay.T[:, :, None]).astype(jnp.bfloat16)
    block_state = jnp.einsum(
        "thd,the->hde", scaled_keys, value_heads, preferred_element_type=jnp.float32
    )

    def combine_blocks(earlier, later_part):
        return (
            earlier[0] + later_part[0],
            jnp.exp(later_part[0])[:, None, None] * earlier[1] + later_part[1],
        )

    identity = (jnp.zeros_like(block_total), jnp.zeros_like(block_state))
    _, entering = entering_2((block_total, block_state), "seq", combine_blocks, identity)
    query_heads = query_rows.reshape(row_count, head_count, head_width)
    local_part = local_mix(query_heads, key_heads, value_heads, levels)
    state_half = entering.astype(jnp.bfloat16)
    scaled_queries = (query_heads.astype(jnp.float32) * jnp.exp(levels).T[:, :, None]).astype(
        jnp.bfloat16
    )
    carried_part = jnp.einsum(
        "thd,hde->the", scaled_queries, state_half, preferred_element_type=jnp.float32
    )
    mixture = local_part + carried_part
    mean_square = jnp.mean(mixture * mixture, axis=2, keepdims=True)
    normed = mixture * lax.rsqrt(mean_square + 1e-06) * gain.reshape(head_count, head_width)[None]
    return normed.reshape(row_count, head_count * head_width).astype(jnp.bfloat16)


def in_vmem():
    return pl.BlockSpec(memory_space=pltpu.VMEM)


def anywhere():
    return pl.BlockSpec(memory_space=pl.ANY)


class Calls:
    def __init__(self, scalars):
        self.scalars, self.after = scalars, []

    def __call__(self, kernel, arrays, outs, streams=(), out_specs=None, scratch=(), cost=1000, aliases=None):
        count = len(arrays) + len(streams)
        after, self.after = [a for a in self.after if not any(a is b for b in arrays)], []

        def body(s_ref, *refs):
            kernel(s_ref, *refs[:count], *refs[count + len(after) :])

        results = pl.pallas_call(
            body,
            out_shape=outs,
            in_specs=[
                pl.BlockSpec(memory_space=pltpu.SMEM),
                *[anywhere() if aliases and n in aliases else in_vmem() for n in range(len(arrays))],
                *[pl.BlockSpec(memory_space=pltpu.HBM)] * len(streams),
                *[anywhere()] * len(after),
            ],
            out_specs=out_specs or [in_vmem()] * len(outs),
            scratch_shapes=list(scratch),
            compiler_params=pltpu.CompilerParams(vmem_limit_bytes=STREAM_VMEM_BYTES if streams else VMEM_BYTES),
            cost_estimate=pl.CostEstimate(flops=cost, bytes_accessed=1000, transcendentals=0),
            input_output_aliases={n + 1: o for n, o in (aliases or {}).items()},
        )(self.scalars, *arrays, *streams, *after)
        self.after.append(results[0])
        return results


def cost_us(time):
    return int(time * SCALE)


def shape(*dims, dtype=BF16):
    return jax.ShapeDtypeStruct(dims, dtype)


def pick(rows, index):
    at = lax.broadcasted_iota(jnp.int32, rows.shape, 0)
    return jnp.sum(jnp.where(at == index, rows, 0.0), axis=0, keepdims=True)


def pack_decays(s_ref, decay_ref, gain_ref, *out_refs):
    z = s_ref[0]
    heads, rows = decay_ref.shape
    parts = len(out_refs)
    width = rows // parts
    lane = lax.broadcasted_iota(jnp.int32, (heads, 128), 1)
    totals = jnp.zeros((heads, 128), F32)
    for c in range(parts):
        total = jnp.sum(decay_ref[:, c * width : (c + 1) * width], axis=1, keepdims=True)
        totals = jnp.where(lane == c, total, totals)
    for k, out_ref in enumerate(out_refs):
        to = lax.rem(z + k, parts)
        out_ref[:, :width] = decay_ref[:, pl.ds(pl.multiple_of(to * width, 128), width)]
        out_ref[:, width : width + 128] = totals
        out_ref[:, width + 128 :] = gain_ref[...]


def unpack_decays(z_ref, *refs):
    parts = len(refs) - 4
    ins, (levels_ref, totals_ref, gains_ref, decays) = refs[:parts], refs[parts:]
    z = z_ref[0]
    heads = ins[0].shape[0]
    width = decays.shape[1]
    for k, in_ref in enumerate(ins):
        home = lax.rem(z + parts - k, parts)
        at = pl.ds(pl.multiple_of(home * heads, heads), heads)
        decays[at, :] = in_ref[:, :width]
        gains_ref[at, :] = in_ref[:, width + 128 :]
        totals = in_ref[:, width : width + 128]
        row = lax.broadcasted_iota(jnp.int32, totals_ref.shape[1:], 0)
        for h in range(heads):
            rows = jnp.zeros(totals_ref.shape[1:], F32)
            for c in range(parts):
                rows = jnp.where(row == c, totals[h : h + 1, c : c + 1], rows)
            totals_ref[home * heads + h] = rows
    upper = lax.broadcasted_iota(jnp.int32, (width, width), 0) <= lax.broadcasted_iota(
        jnp.int32, (width, width), 1
    )
    levels_ref[...] = jnp.dot(
        decays[...],
        jnp.where(upper, 1.0, 0.0).astype(F32),
        precision=lax.Precision.HIGHEST,
        preferred_element_type=F32,
    )


def put_log(ref, i, log):
    high = log.astype(BF16).astype(F32)
    middle = (log - high).astype(BF16).astype(F32)
    low = log - high - middle
    row = lax.broadcasted_iota(jnp.int32, (16, 128), 0)
    rows = jnp.where(row == 0, high, jnp.where(row == 1, middle, jnp.where(row == 2, low, 0.0)))
    ref[(*i, pl.ds(ref.shape[-2] - 16, 16))] = rows.astype(BF16)


def get_log(ref, i):
    return jnp.sum(ref[(*i, pl.ds(ref.shape[-2] - 16, 16))].astype(F32), axis=0, keepdims=True)


def state_of(key, value, row, end):
    scaled = (key.T.astype(F32) * jnp.exp(end - row)).astype(BF16)
    return jnp.dot(scaled, value, preferred_element_type=F32)


def half_states(first, heads, s_ref, levels_ref, keys_ref, values_ref, keep_ref, send_ref):
    z = s_ref[0]
    m = keep_ref.shape[0] // 2
    rows = levels_ref.shape[1]
    places = [(out, n, 2 * n + lax.rem(z + other, 2)) for other, out in enumerate((keep_ref, send_ref)) for n in range(2)]

    def step(*refs):
        j = pl.program_id(0)
        for k, (out, n, home) in enumerate(places):
            row = levels_ref[pl.ds(home * heads + first + j, 1), :]
            state = state_of(refs[2 * k][...], refs[2 * k + 1][...], row, row[:, rows - 1 :])
            out[n * m + j] = state.astype(BF16)

    specs = [pl.BlockSpec((rows, 128), lambda j, home=home: (0, home * heads + first + j)) for _, _, home in places]
    pltpu.emit_pipeline(step, grid=(m,), in_specs=[spec for spec in specs for _ in range(2)])(
        *[keys_ref, values_ref] * len(places)
    )


def pair_states(head_of, z_ref, keep_ref, got_ref, totals_ref, out_ref):
    z = z_ref[0]
    odd = lax.rem(z, 2) == 1
    for i in range(keep_ref.shape[0]):
        totals = totals_ref[head_of(i, z, 0)]
        keep, got = keep_ref[i].astype(F32), got_ref[i].astype(F32)
        decay = jnp.exp(pick(totals, 2 * lax.div(z, 2) + 1))
        out_ref[i] = (decay * jnp.where(odd, got, keep) + jnp.where(odd, keep, got)).astype(BF16)
    count = keep_ref.shape[0]
    for j in range(out_ref.shape[0] - count):
        i = (1 - lax.div(z, 2)) * (count // 2) + j
        out_ref[count + j] = jnp.where(odd, got_ref[i], keep_ref[i])


def block_states(head_of, z_ref, pair_ref, got_ref, totals_ref, out_ref):
    z = z_ref[0]
    upper = z >= 2
    for i in range(out_ref.shape[0]):
        totals = totals_ref[head_of(i, z, 0)]
        mine, got = pair_ref[i].astype(F32), got_ref[i].astype(F32)
        decay = jnp.exp(pick(totals, 2) + pick(totals, 3))
        state = decay * jnp.where(upper, got, mine) + jnp.where(upper, mine, got)
        out_ref[i, :128, :] = state.astype(BF16)
        put_log(out_ref, (i,), jnp.sum(totals, axis=0, keepdims=True))


def scan_step(bit, s_ref, i, own_ref, got_ref, before, before_log):
    upper = (s_ref[1] >> bit) & 1 == 1
    own, got = own_ref[i, :128, :].astype(F32), got_ref[i, :128, :].astype(F32)
    own_log, got_log = get_log(own_ref, (i,)), get_log(got_ref, (i,))
    if before is None:
        after = jnp.where(upper, got, 0.0)
        after_log = jnp.where(upper, got_log, 0.0)
    else:
        after = jnp.where(upper, jnp.exp(before_log) * got + before, before)
        after_log = jnp.where(upper, before_log + got_log, before_log)
    total = jnp.exp(jnp.where(upper, own_log, got_log)) * jnp.where(upper, got, own) + jnp.where(upper, own, got)
    return after, after_log, total, own_log + got_log


def scan_blocks(bit, s_ref, own_ref, got_ref, *refs):
    before_ref = refs[0] if bit else None
    after_ref, total_ref = refs[-2:]
    for i in range(own_ref.shape[0]):
        before = before_ref[i, :128, :] if bit else None
        before_log = before_ref[i, 128:129, :] if bit else None
        after, after_log, total, total_log = scan_step(bit, s_ref, i, own_ref, got_ref, before, before_log)
        after_ref[i, :128, :] = after
        after_ref[i, 128:, :] = jnp.broadcast_to(after_log, (8, 128))
        total_ref[i, :128, :] = total.astype(BF16)
        put_log(total_ref, (i,), total_log)


def entering_states(first, heads, done, bit, s_ref, own_ref, got_ref, before_ref, keep_ref, keep_got_ref, pair_ref, pair_got_ref, totals_ref, *outs):
    z = s_ref[0]
    odd, upper = lax.rem(z, 2) == 1, z >= 2
    count = own_ref.shape[0]
    m = count // 2

    def parts_of(i, head):
        totals = totals_ref[head]
        state = scan_step(
            bit, s_ref, i, own_ref, got_ref, before_ref[i, :128, :], before_ref[i, 128:129, :]
        )[0]
        low = jnp.where(upper, pair_got_ref[i], pair_ref[i]).astype(F32)
        even_part = jnp.where(odd, keep_got_ref[i], keep_ref[i]).astype(F32)
        middle = jnp.exp(pick(totals, 0) + pick(totals, 1)) * state + low
        return totals, state, middle, even_part

    for i in range(count):
        n, j = divmod(i, m)
        if j < done:
            continue
        totals, state, middle, even_part = parts_of(i, (2 * n + lax.rem(z, 2)) * heads + first + j)
        even_state = jnp.where(upper, middle, state)
        odd_state = jnp.exp(pick(totals, jnp.where(upper, 2, 0))) * even_state + even_part
        at = n * (m - done) + j - done
        outs[0][at] = jnp.where(odd, odd_state, even_state).astype(BF16)
        outs[1][at] = jnp.where(odd, even_state, odd_state).astype(BF16)
    for j in range(done):
        totals, state, middle, even_part = parts_of(lax.div(z, 2) * m + j, z * heads + first + j)
        other = pair_got_ref[count + j].astype(F32)
        first_part, third_part = jnp.where(upper, other, even_part), jnp.where(upper, even_part, other)
        outs[2][j, 0] = state.astype(BF16)
        outs[2][j, 1] = (jnp.exp(pick(totals, 0)) * state + first_part).astype(BF16)
        outs[2][j, 2] = middle.astype(BF16)
        outs[2][j, 3] = (jnp.exp(pick(totals, 2)) * middle + third_part).astype(BF16)


def norm(mixture, gain):
    mean_square = jnp.mean(mixture * mixture, axis=1, keepdims=True)
    return (mixture * lax.rsqrt(mean_square + 1e-6) * gain).astype(BF16)


def column_of(row):
    return jnp.broadcast_to(row, (128, row.shape[1])).T


def mix_head(query, key, value, row, entering=None):
    rows = query.shape[0]
    chunk = min(CHUNK, rows)
    column = column_of(row)
    causal = lax.broadcasted_iota(jnp.int32, (chunk, chunk), 0) >= lax.broadcasted_iota(
        jnp.int32, (chunk, chunk), 1
    )
    state = None if entering is None else entering.astype(F32)
    start_level = jnp.zeros((1, 1), F32)
    pieces = []
    for start in range(0, rows, chunk):
        stop = start + chunk
        q, k, v = query[start:stop], key[start:stop], value[start:stop]
        r, c = row[:, start:stop], column[start:stop]
        scores = lax.dot_general(q, k, (((1,), (1,)), ((), ())), preferred_element_type=F32)
        gap = jnp.where(causal, jnp.concatenate([c] * (chunk // 128), axis=1) - r, -1e30)
        weights = (scores * jnp.exp(gap)).astype(BF16)
        mixture = jnp.dot(weights, v, preferred_element_type=F32)
        if state is not None:
            scaled = (q.astype(F32) * jnp.exp(c - start_level)).astype(BF16)
            mixture = mixture + jnp.dot(scaled, state.astype(BF16), preferred_element_type=F32)
        pieces.append(mixture)
        if stop < rows:
            end = row[:, stop - 1 : stop]
            added = state_of(k, v, r, end)
            state = added if state is None else jnp.exp(end - start_level) * state + added
            start_level = end
    return pieces


def attend(first, heads, states_of, s_ref, levels_ref, gains_ref, *refs):
    z = s_ref[0]
    parts = 4
    streams, outs = refs[-3 - parts : -parts], refs[-parts:]
    states = refs[: -3 - parts]
    rows = levels_ref.shape[1]

    def step(*blocks):
        j = pl.program_id(0)
        for k in range(parts):
            home = lax.rem(z + k, parts)
            at = pl.ds(home * heads + first + j, 1)
            query, key, value = blocks[3 * k : 3 * k + 3]
            pieces = mix_head(query[...], key[...], value[...], levels_ref[at, :], states_of(states, k, home, j))
            size = pieces[0].shape[0]
            for n, piece in enumerate(pieces):
                blocks[3 * parts + k][n * size : (n + 1) * size, :] = norm(piece, gains_ref[at, :])

    specs = [
        pl.BlockSpec((rows, 128), lambda j, k=k: (0, lax.rem(z + k, parts) * heads + first + j)) for k in range(parts)
    ]
    pltpu.emit_pipeline(
        step,
        grid=(outs[0].shape[1] // 128,),
        in_specs=[spec for spec in specs for _ in range(3)],
        out_specs=[pl.BlockSpec((rows, 128), lambda j: (0, j))] * parts,
    )(*list(streams) * parts, *outs)


def own_parts(first, heads, s_ref, levels_ref, queries_ref, keys_ref, values_ref, *outs):
    z = s_ref[0]
    parts = len(outs)
    rows = levels_ref.shape[1]
    count = outs[0].shape[1] // 256

    def step(*blocks):
        j = pl.program_id(0)
        for k in range(parts):
            head = lax.rem(z + k, parts) * heads + first + j
            query, key, value = blocks[3 * k : 3 * k + 3]
            pieces = mix_head(query[...], key[...], value[...], levels_ref[pl.ds(head, 1), :])
            size = pieces[0].shape[0]
            for n, piece in enumerate(pieces):
                outs[k][n * size : (n + 1) * size, pl.ds(pl.multiple_of(j * 128, 128), 128)] = piece.astype(BF16)
            outs[k][:, pl.ds(pl.multiple_of((count + j) * 128, 128), 128)] = query[...]

    specs = [
        pl.BlockSpec((rows, 128), lambda j, k=k: (0, lax.rem(z + k, parts) * heads + first + j)) for k in range(parts)
    ]
    pltpu.emit_pipeline(step, grid=(count,), in_specs=[spec for spec in specs for _ in range(3)])(
        *[queries_ref, keys_ref, values_ref] * parts
    )


def finish(first, heads, s_ref, decay_ref, gains_ref, states_ref, *refs):
    parts = len(refs) // 2
    z = s_ref[0]
    rows, width = refs[parts].shape
    upper = lax.broadcasted_iota(jnp.int32, (rows, rows), 0) <= lax.broadcasted_iota(jnp.int32, (rows, rows), 1)
    upper = jnp.where(upper, 1.0, 0.0).astype(F32)
    for k in range(parts):
        c = lax.rem(z + parts - k, parts)
        levels = jnp.dot(
            decay_ref[:, pl.ds(pl.multiple_of(c * rows, 128), rows)], upper,
            precision=lax.Precision.HIGHEST, preferred_element_type=F32,
        )
        for j in range(width // 128):
            column = column_of(levels[first + j : first + j + 1, :])
            at = slice(j * 128, (j + 1) * 128)
            query = refs[k][:, width + j * 128 : width + (j + 1) * 128]
            scaled = (query.astype(F32) * jnp.exp(column)).astype(BF16)
            mixture = refs[k][:, at].astype(F32) + jnp.dot(scaled, states_ref[j, c], preferred_element_type=F32)
            refs[parts + k][:, at] = norm(mixture, gains_ref[pl.ds(z * heads + first + j, 1), :])


def place(first, parts, s_ref, *refs):
    pieces, out_ref, sems = refs[:parts], refs[-2], refs[-1]
    rows, width = pieces[0].shape
    copies = []
    for k in range(parts):
        source = lax.rem(s_ref[0] + parts - k, parts)
        copies.append(
            pltpu.make_async_copy(
                pieces[k],
                out_ref.at[pl.ds(pl.multiple_of(source * rows, rows), rows), pl.ds(first * 128, width)],
                sems.at[k],
            )
        )
    for copy in copies:
        copy.start()
    for copy in copies:
        copy.wait()


def local(queries, keys, values, log_decay, gain):
    heads, block = log_decay.shape
    parts, blocks = lax.axis_size("grp"), lax.axis_size("seq")
    rows = queries.shape[0]
    call = Calls(jnp.stack([lax.axis_index("grp"), lax.axis_index("seq")]).astype(jnp.int32))

    def shift(x, k):
        return lax.ppermute(x, "grp", [(i, (i + k) % parts) for i in range(parts)])

    def swap(x, axis, bit):
        return lax.ppermute(x, axis, [(i, i ^ bit) for i in range(lax.axis_size(axis))])

    starts = [sum(group[0] for group in GROUPS[:g]) for g in range(len(GROUPS))]
    packed = call(
        pack_decays, [log_decay, gain.reshape(heads, 128)], [shape(heads, rows + 256, dtype=F32)] * parts,
        cost=cost_us(8),
    )
    got = [packed[0]] + [shift(packed[k], k) for k in range(1, parts)]
    levels, totals, gains = call(
        unpack_decays, got,
        [shape(heads * parts, rows, dtype=F32), shape(heads * parts, 8, 128, dtype=F32), shape(heads * parts, 128, dtype=F32)],
        scratch=[pltpu.VMEM((heads * parts, rows), F32)],
        cost=cost_us(8),
    )

    def outputs(first, m, states, states_of):
        outs = call(
            functools.partial(attend, first, heads, states_of), [levels, gains, *states],
            [shape(rows, m * 128)] * parts,
            streams=[queries, keys, values],
            cost=cost_us(2.5 * m),
        )
        return first, [outs[0]] + [shift(outs[k], k) for k in range(1, parts)]

    def travel(first, m, done, calls, home_states):
        n = 2 * m

        def head_of(i, z, other):
            return (2 * (i // m) + lax.rem(z + other, 2)) * heads + first + i % m

        keep, send = call(
            functools.partial(half_states, first, heads), [levels],
            [shape(n, 128, 128)] * 2,
            streams=[keys, values],
            cost=cost_us(m),
        )
        got = swap(send, "grp", 1)
        yield
        pair, = call(functools.partial(pair_states, head_of), [keep, got, totals], [shape(n + done, 128, 128)])
        pair_got = swap(pair, "grp", 2)
        yield
        total, = call(functools.partial(block_states, head_of), [pair, pair_got, totals], [shape(n, 144, 128)])
        before = []
        bits = blocks.bit_length() - 1
        for bit in range(bits - 1):
            other = swap(total, "seq", 1 << bit)
            yield
            after, total = call(
                functools.partial(scan_blocks, bit), [total, other, *before],
                [shape(n, 136, 128, dtype=F32), shape(n, 144, 128)],
            )
            before = [after]
        other = swap(total, "seq", 1 << (bits - 1))
        yield
        rest = m - done
        own, send, *home = call(
            functools.partial(entering_states, first, heads, done, bits - 1),
            [total, other, *before, keep, got, pair, pair_got, totals],
            [shape(2 * rest, 128, 128)] * 2 + [shape(done, parts, 128, 128)] * (done > 0),
        )
        home_states.extend(home)
        states = [own, swap(send, "grp", 1)]
        yield
        start = 0
        for count in calls:

            def states_of(refs, k, home, j, start=start):
                return refs[k % 2][lax.div(home, 2) * rest + start + j]

            yield outputs(first + done + start, count, states, states_of)
            start += count

    def finished(first, done, arrived, home_states):
        parcels = call(
            functools.partial(own_parts, first, heads), [levels], [shape(rows, 2 * done * 128)] * parts,
            streams=[queries, keys, values],
            cost=cost_us(2 * done),
        )
        arrived += [parcels[0]] + [shift(parcels[k], k) for k in range(1, parts)]
        yield
        yield first, call(
            functools.partial(finish, first, heads), [log_decay, gains, *home_states, *arrived],
            [shape(rows, done * 128)] * parts,
        )

    home_states = [[] for _ in GROUPS]
    work = [travel(first, *group, home) for first, group, home in zip(starts, GROUPS, home_states)]
    arrived = [[] for _ in GROUPS]
    home_work = [
        finished(first, group[1], parcels, home)
        for first, group, parcels, home in zip(starts, GROUPS, arrived, home_states)
    ]
    pieces, out = [[] for _ in GROUPS], None
    for action, g, *rest in ORDER:
        g = int(g)
        if action in "kh":
            piece = next(work[g] if action == "k" else home_work[g])
            if piece is not None:
                pieces[g].append(piece)
        elif action == "d":
            call.after.append(arrived[g][int(rest[0])])
        elif action == "w":
            call.after.append(pieces[g][int(rest[0])][1][int(rest[1])])
        else:
            first, piece = pieces[g][int(rest[0])]
            out, = call(
                functools.partial(place, first, parts), [*piece, *([] if out is None else [out])],
                [shape(block, heads * 128)],
                out_specs=[anywhere()],
                scratch=[pltpu.SemaphoreType.DMA((parts,))],
                aliases={} if out is None else {parts: 0},
            )
    return out


def solution(mesh):
    parts, blocks = mesh.shape["grp"], mesh.shape["seq"]
    fits = parts == 4 and blocks >= 4 and blocks & (blocks - 1) == 0
    in_specs = (
        P(("seq", "grp"), None),
        P(("seq", "grp"), None),
        P(("seq", "grp"), None),
        P("grp", "seq"),
        P("grp"),
    )
    out_specs = P("seq", "grp")
    return jax.shard_map(
        local if fits else local_any, mesh=mesh, in_specs=in_specs, out_specs=out_specs, check_vma=False
    )
```

time: 179 us -> 163 us (0.911)
  waiting for transfers between devices: 84 us -> 76.5 us
  Pallas kernels: 46.5 us -> 42.5 us
  local copies, waits for them, and re-layouts: 5.91 us -> 3.96 us
    ppermute x18 -> x12, starting transfers between devices: 21.9 us -> 15.4 us  [swap(): lax.ppermute(x, axis, [(i, i ^ bit) for i in range(lax.axis_size(axis))])]
    ppermute x18 -> x12, waiting for transfers between devices: 31.6 us -> 26.4 us  [swap(): lax.ppermute(x, axis, [(i, i ^ bit) for i in range(lax.axis_size(axis))])]
    ppermute x12 -> x18, starting transfers between devices: 19.4 us -> 24.2 us  [shift(): return lax.ppermute(x, 'grp', [(i, (i + k) % parts) for i in range(parts)])]
    pallas_call x26 -> x24, Pallas kernels: 46.5 us -> 42.5 us  [__call__(): pl.pallas_call(body, out_shape=outs, in_specs=[pl.BlockSpec(memory_space=...]
    ppermute x12 -> x18, waiting for transfers between devices: 52.5 us -> 50.1 us  [shift(): return lax.ppermute(x, 'grp', [(i, (i + k) % parts) for i in range(parts)])]
    unnamed x12 -> x10, local copies, waits for them, and re-layouts: 5.91 us -> 3.96 us
  transfers between devices with their start and end apart: 30 -> 30, of which waited for: 14 -> 19; matrix products, arithmetic and copies ran while one was open for 0% -> 0% of each run, Pallas kernels for 22% -> 21%
where the time goes in v2:
time: 163 us
  waiting for transfers between devices  76.5 us (47%)
  Pallas kernels  42.5 us (26%)
  starting transfers between devices  39.6 us (24%)
  local copies, waits for them, and re-layouts  3.96 us (2%)
    ppermute x18, waiting for transfers between devices, shift(): return lax.ppermute(x, 'grp', [(i, (i + k) % parts) for i in range(parts)])  50.1 us
    pallas_call x24, Pallas kernels, __call__(): pl.pallas_call(body, out_shape=outs, in_specs=[pl.BlockSpec(memory_space=...  42.5 us
    ppermute x12, waiting for transfers between devices, swap(): lax.ppermute(x, axis, [(i, i ^ bit) for i in range(lax.axis_size(axis))])  26.4 us
    ppermute x18, starting transfers between devices, shift(): return lax.ppermute(x, 'grp', [(i, (i + k) % parts) for i in range(parts)])  24.2 us
    ppermute x12, starting transfers between devices, swap(): lax.ppermute(x, axis, [(i, i ^ bit) for i in range(lax.axis_size(axis))])  15.4 us
    unnamed x10, local copies, waits for them, and re-layouts  3.96 us
  transfers between devices with their start and end apart: 30, of which 19 were waited for; matrix products, arithmetic and copies ran while one was open for 0% of the time, Pallas kernels for 21%

profile of v2, /device:TPU:10, one launch (start us, length us, event | category | flops | bytes accessed | tf_op | source)
XLA Modules:
  0.0 163.0 jit_solution(10432465674957255296)
XLA Ops:
  2.2 1.6 collective-permute-start
  3.8 1.2 collective-permute-start.1
  5.0 1.8 %collective-permute-start.2 = (f32[8,768]{1,0:T(8,128)S(1)}, f32[8,768]{1,0:T(8,128)S(1)}, u32[]{:S(2)}, u32[]{:S(2)}) collective-permute-start(f32[8,768]{1,0:T(8,128)S(1)} %get-tuple-element.51), channel_id=1, source_target_pairs={{0,24},{8,0},{16,8},{24,16},{1,25},{9,1},{17,9},{25,17},{2,26},{10... | collective-permute-start | bytes 73736 | tf_op jit(solution)/shard_map/ppermute | solution.py:470
  6.8 1.7 %collective-permute-done.1.refs_2_ = f32[8,768]{1,0:T(8,128)S(1)} collective-permute-done((f32[8,768]{1,0:T(8,128)S(1)}, f32[8,768]{1,0:T(8,128)S(1)}, u32[]{:S(2)}, u32[]{:S(2)}) %collective-permute-start.1) | collective-permute-done | bytes 24608 | tf_op jit(solution)/shard_map/ppermute | solution.py:470
  11.1 1.3 copy-done.1
  12.3 2.7 %shard_map.57 = (bf16[6,128,128]{2,1,0:T(8,128)(2,1)S(1)}, bf16[6,128,128]{2,1,0:T(8,128)(2,1)S(1)}) custom-call(s32[2]{0:T(128)S(1)} %pad_add_fusion.s_ref, f32[32,512]{1,0:T(8,128)S(1)} %get-tuple-element.52.refs_0_, bf16[512,4096]{1,0:T(8,128)(2,1)S(1)} %copy-done, bf16[512,4096]{1,0:T(8,128)(2,1)S(1)} %copy-done.1), custom_call_target="tpu_custom_call" | custom-call | flops 3000000000 | bytes 1000 | tf_op jit(solution)/shard_map/pallas_call | solution.py:126
  15.1 1.9 %collective-permute-start.4 = (bf16[6,128,128]{2,1,0:T(8,128)(2,1)S(1)}, bf16[6,128,128]{2,1,0:T(8,128)(2,1)S(1)}, u32[]{:S(2)}, u32[]{:S(2)}) collective-permute-start(bf16[6,128,128]{2,1,0:T(8,128)(2,1)S(1)} %get-tuple-element.58), channel_id=1, source_target_pairs={{0,8},{8,0},{16,24},{24,16},{1,9},{9,1},{17,25},{25,17},{2,10},{10... | collective-permute-start | bytes 589832 | tf_op jit(solution)/shard_map/ppermute | solution.py:473
  16.9 4.2 %shard_map.58 = (bf16[10,128,128]{2,1,0:T(8,128)(2,1)S(1)}, bf16[10,128,128]{2,1,0:T(8,128)(2,1)S(1)}) custom-call(s32[2]{0:T(128)S(1)} %pad_add_fusion.s_ref, f32[32,512]{1,0:T(8,128)S(1)} %get-tuple-element.52.refs_0_, bf16[512,4096]{1,0:T(8,128)(2,1)S(1)} %copy-done, bf16[512,4096]{1,0:T(8,128)(2,1)S(1)} %copy-done.1, ...), custom_call_target="tpu_custom_call" | custom-call | flops 5000000000 | bytes 1000 | tf_op jit(solution)/shard_map/pallas_call | solution.py:126
  21.8 3.2 %collective-permute-start.5 = (bf16[6,128,128]{2,1,0:T(8,128)(2,1)S(1)}, bf16[6,128,128]{2,1,0:T(8,128)(2,1)S(1)}, u32[]{:S(2)}, u32[]{:S(2)}) collective-permute-start(bf16[6,128,128]{2,1,0:T(8,128)(2,1)S(1)} %shard_map.59.refs_0_.refs_5_), channel_id=1, source_target_pairs={{0,16},{8,24},{16,0},{24,8},{1,17},{9,25},{17,1},{25,9},{2,18},{10... | collective-permute-start | bytes 589832 | tf_op jit(solution)/shard_map/ppermute | solution.py:473
  25.6 5.3 %collective-permute-done.5.refs_1_.refs_6_ = bf16[6,128,128]{2,1,0:T(8,128)(2,1)S(1)} collective-permute-done((bf16[6,128,128]{2,1,0:T(8,128)(2,1)S(1)}, bf16[6,128,128]{2,1,0:T(8,128)(2,1)S(1)}, u32[]{:S(2)}, u32[]{:S(2)}) %collective-permute-start.5) | collective-permute-done | bytes 196640 | tf_op jit(solution)/shard_map/ppermute | solution.py:473
  31.6 3.7 %collective-permute-done.3.refs_1_.refs_4_ = bf16[10,128,128]{2,1,0:T(8,128)(2,1)S(1)} collective-permute-done((bf16[10,128,128]{2,1,0:T(8,128)(2,1)S(1)}, bf16[10,128,128]{2,1,0:T(8,128)(2,1)S(1)}, u32[]{:S(2)}, u32[]{:S(2)}) %collective-permute-start.3) | collective-permute-done | bytes 327712 | tf_op jit(solution)/shard_map/ppermute | solution.py:473
  36.0 1.4 collective-permute-start.6
  38.7 5.4 %collective-permute-done.8.refs_1_ = bf16[6,144,128]{2,1,0:T(8,128)(2,1)S(1)} collective-permute-done((bf16[6,144,128]{2,1,0:T(8,128)(2,1)S(1)}, bf16[6,144,128]{2,1,0:T(8,128)(2,1)S(1)}, u32[]{:S(2)}, u32[]{:S(2)}) %collective-permute-start.8) | collective-permute-done | bytes 221216 | tf_op jit(solution)/shard_map/ppermute | solution.py:473
  44.8 1.6 collective-permute-start.10
  46.4 3.6 %collective-permute-done.6.refs_1_.refs_6_ = bf16[10,128,128]{2,1,0:T(8,128)(2,1)S(1)} collective-permute-done((bf16[10,128,128]{2,1,0:T(8,128)(2,1)S(1)}, bf16[10,128,128]{2,1,0:T(8,128)(2,1)S(1)}, u32[]{:S(2)}, u32[]{:S(2)}) %collective-permute-start.6) | collective-permute-done | bytes 327712 | tf_op jit(solution)/shard_map/ppermute | solution.py:473
  51.6 2.5 %collective-permute-start.12 = (bf16[6,128,128]{2,1,0:T(8,128)(2,1)S(1)}, bf16[6,128,128]{2,1,0:T(8,128)(2,1)S(1)}, u32[]{:S(2)}, u32[]{:S(2)}) collective-permute-start(bf16[6,128,128]{2,1,0:T(8,128)(2,1)S(1)} %get-tuple-element.66), channel_id=1, source_target_pairs={{0,8},{8,0},{16,24},{24,16},{1,9},{9,1},{17,25},{25,17},{2,10},{10... | collective-permute-start | bytes 589832 | tf_op jit(solution)/shard_map/ppermute | solution.py:473
  55.4 4.2 %collective-permute-done.12.refs_3_ = bf16[6,128,128]{2,1,0:T(8,128)(2,1)S(1)} collective-permute-done((bf16[6,128,128]{2,1,0:T(8,128)(2,1)S(1)}, bf16[6,128,128]{2,1,0:T(8,128)(2,1)S(1)}, u32[]{:S(2)}, u32[]{:S(2)}) %collective-permute-start.12) | collective-permute-done | bytes 196640 | tf_op jit(solution)/shard_map/ppermute | solution.py:473
  59.6 2.5 %shard_map.67 = (bf16[512,128]{1,0:T(8,128)(2,1)S(1)}, bf16[512,128]{1,0:T(8,128)(2,1)S(1)}, bf16[512,128]{1,0:T(8,128)(2,1)S(1)}, bf16[512,128]{1,0:T(8,128)(2,1)S(1)}) custom-call(s32[2]{0:T(128)S(1)} %pad_add_fusion.s_ref, f32[32,512]{1,0:T(8,128)S(1)} %get-tuple-element.52.refs_0_, f32[32,128]{1,0:T(8,128)S(1)} %get-tuple-element.53.refs_1_, ...), custom_call_target="tpu_custom_call" | custom-call | flops 2500000000 | bytes 1000 | tf_op jit(solution)/shard_map/pallas_call | solution.py:126
  62.1 1.6 collective-permute-start.13
  64.2 2.7 %collective-permute-start.16 = (bf16[512,128]{1,0:T(8,128)(2,1)S(1)}, bf16[512,128]{1,0:T(8,128)(2,1)S(1)}, u32[]{:S(2)}, u32[]{:S(2)}) collective-permute-start(bf16[512,128]{1,0:T(8,128)(2,1)S(1)} %get-tuple-element.73), channel_id=1, source_target_pairs={{0,16},{8,24},{16,0},{24,8},{1,17},{9,25},{17,1},{25,9},{2,18},{10... | collective-permute-start | bytes 393224 | tf_op jit(solution)/shard_map/ppermute | solution.py:470
  68.3 1.6 collective-permute-start.14
  69.9 5.2 %collective-permute-done.15.refs_8_.refs_3_ = bf16[512,128]{1,0:T(8,128)(2,1)S(1)} collective-permute-done((bf16[512,128]{1,0:T(8,128)(2,1)S(1)}, bf16[512,128]{1,0:T(8,128)(2,1)S(1)}, u32[]{:S(2)}, u32[]{:S(2)}) %collective-permute-start.15) | collective-permute-done | bytes 131104 | tf_op jit(solution)/shard_map/ppermute | solution.py:470
  75.1 4.7 %shard_map.69 = (bf16[512,256]{1,0:T(8,128)(2,1)S(1)}, bf16[512,256]{1,0:T(8,128)(2,1)S(1)}, bf16[512,256]{1,0:T(8,128)(2,1)S(1)}, bf16[512,256]{1,0:T(8,128)(2,1)S(1)}) custom-call(s32[2]{0:T(128)S(1)} %pad_add_fusion.s_ref, f32[32,512]{1,0:T(8,128)S(1)} %get-tuple-element.52.refs_0_, f32[32,128]{1,0:T(8,128)S(1)} %get-tuple-element.53.refs_1_, ...), custom_call_target="tpu_custom_call" | custom-call | flops 5000000000 | bytes 1000 | tf_op jit(solution)/shard_map/pallas_call | solution.py:126
  80.8 1.4 collective-permute-start.17
  82.1 2.3 %collective-permute-start.18 = (bf16[512,256]{1,0:T(8,128)(2,1)S(1)}, bf16[512,256]{1,0:T(8,128)(2,1)S(1)}, u32[]{:S(2)}, u32[]{:S(2)}) collective-permute-start(bf16[512,256]{1,0:T(8,128)(2,1)S(1)} %get-tuple-element.76), channel_id=1, source_target_pairs={{0,8},{8,16},{16,24},{24,0},{1,9},{9,17},{17,25},{25,1},{2,10},{10... | collective-permute-start | bytes 786440 | tf_op jit(solution)/shard_map/ppermute | solution.py:470
  84.5 1.4 collective-permute-start.19
  85.9 2.0 %collective-permute-start.20 = (bf16[512,256]{1,0:T(8,128)(2,1)S(1)}, bf16[512,256]{1,0:T(8,128)(2,1)S(1)}, u32[]{:S(2)}, u32[]{:S(2)}) collective-permute-start(bf16[512,256]{1,0:T(8,128)(2,1)S(1)} %get-tuple-element.80), channel_id=1, source_target_pairs={{0,24},{8,0},{16,8},{24,16},{1,25},{9,1},{17,9},{25,17},{2,26},{10... | collective-permute-start | bytes 786440 | tf_op jit(solution)/shard_map/ppermute | solution.py:470
  87.9 9.2 %collective-permute-done.18.refs_7_.refs_1_ = bf16[512,256]{1,0:T(8,128)(2,1)S(1)} collective-permute-done((bf16[512,256]{1,0:T(8,128)(2,1)S(1)}, bf16[512,256]{1,0:T(8,128)(2,1)S(1)}, u32[]{:S(2)}, u32[]{:S(2)}) %collective-permute-start.18) | collective-permute-done | bytes 262176 | tf_op jit(solution)/shard_map/ppermute | solution.py:470
  97.1 4.2 %collective-permute-done.17.refs_3_ = bf16[10,128,128]{2,1,0:T(8,128)(2,1)S(1)} collective-permute-done((bf16[10,128,128]{2,1,0:T(8,128)(2,1)S(1)}, bf16[10,128,128]{2,1,0:T(8,128)(2,1)S(1)}, u32[]{:S(2)}, u32[]{:S(2)}) %collective-permute-start.17) | collective-permute-done | bytes 327712 | tf_op jit(solution)/shard_map/ppermute | solution.py:473
  101.4 2.5 %shard_map.71 = (bf16[512,128]{1,0:T(8,128)(2,1)S(1)}, bf16[512,128]{1,0:T(8,128)(2,1)S(1)}, bf16[512,128]{1,0:T(8,128)(2,1)S(1)}, bf16[512,128]{1,0:T(8,128)(2,1)S(1)}) custom-call(s32[2]{0:T(128)S(1)} %pad_add_fusion.s_ref, f32[32,512]{1,0:T(8,128)S(1)} %get-tuple-element.52.refs_0_, f32[32,128]{1,0:T(8,128)S(1)} %get-tuple-element.53.refs_1_, ...), custom_call_target="tpu_custom_call" | custom-call | flops 2500000000 | bytes 1000 | tf_op jit(solution)/shard_map/pallas_call | solution.py:126
  103.9 1.4 collective-permute-start.21
  105.3 3.5 %collective-permute-start.28 = (bf16[512,128]{1,0:T(8,128)(2,1)S(1)}, bf16[512,128]{1,0:T(8,128)(2,1)S(1)}, u32[]{:S(2)}, u32[]{:S(2)}) collective-permute-start(bf16[512,128]{1,0:T(8,128)(2,1)S(1)} %get-tuple-element.89), channel_id=1, source_target_pairs={{0,16},{8,24},{16,0},{24,8},{1,17},{9,25},{17,1},{25,9},{2,18},{10... | collective-permute-start | bytes 393224 | tf_op jit(solution)/shard_map/ppermute | solution.py:470
  109.2 4.7 %shard_map.72 = (bf16[512,256]{1,0:T(8,128)(2,1)S(1)}, bf16[512,256]{1,0:T(8,128)(2,1)S(1)}, bf16[512,256]{1,0:T(8,128)(2,1)S(1)}, bf16[512,256]{1,0:T(8,128)(2,1)S(1)}) custom-call(s32[2]{0:T(128)S(1)} %pad_add_fusion.s_ref, f32[32,512]{1,0:T(8,128)S(1)} %get-tuple-element.52.refs_0_, f32[32,128]{1,0:T(8,128)S(1)} %get-tuple-element.53.refs_1_, ...), custom_call_target="tpu_custom_call" | custom-call | flops 5000000000 | bytes 1000 | tf_op jit(solution)/shard_map/pallas_call | solution.py:126
  113.9 1.7 %collective-permute-start.25 = (bf16[512,256]{1,0:T(8,128)(2,1)S(1)}, bf16[512,256]{1,0:T(8,128)(2,1)S(1)}, u32[]{:S(2)}, u32[]{:S(2)}) collective-permute-start(bf16[512,256]{1,0:T(8,128)(2,1)S(1)} %get-tuple-element.86), channel_id=1, source_target_pairs={{0,8},{8,16},{16,24},{24,0},{1,9},{9,17},{17,25},{25,1},{2,10},{10... | collective-permute-start | bytes 786440 | tf_op jit(solution)/shard_map/ppermute | solution.py:470
  115.6 2.1 %collective-permute-done.20.refs_8_.refs_3_ = bf16[512,256]{1,0:T(8,128)(2,1)S(1)} collective-permute-done((bf16[512,256]{1,0:T(8,128)(2,1)S(1)}, bf16[512,256]{1,0:T(8,128)(2,1)S(1)}, u32[]{:S(2)}, u32[]{:S(2)}) %collective-permute-start.20) | collective-permute-done | bytes 262176 | tf_op jit(solution)/shard_map/ppermute | solution.py:470
  118.5 4.7 %shard_map.73 = (bf16[512,256]{1,0:T(8,128)(2,1)S(1)}, bf16[512,256]{1,0:T(8,128)(2,1)S(1)}, bf16[512,256]{1,0:T(8,128)(2,1)S(1)}, bf16[512,256]{1,0:T(8,128)(2,1)S(1)}) custom-call(s32[2]{0:T(128)S(1)} %pad_add_fusion.s_ref, f32[32,512]{1,0:T(8,128)S(1)} %get-tuple-element.52.refs_0_, f32[32,128]{1,0:T(8,128)S(1)} %get-tuple-element.53.refs_1_, ...), custom_call_target="tpu_custom_call" | custom-call | flops 5000000000 | bytes 1000 | tf_op jit(solution)/shard_map/pallas_call | solution.py:126
  124.4 10.1 %collective-permute-done.29.refs_3_ = bf16[512,128]{1,0:T(8,128)(2,1)S(1)} collective-permute-done((bf16[512,128]{1,0:T(8,128)(2,1)S(1)}, bf16[512,128]{1,0:T(8,128)(2,1)S(1)}, u32[]{:S(2)}, u32[]{:S(2)}) %collective-permute-start.29) | collective-permute-done | bytes 131104 | tf_op jit(solution)/shard_map/ppermute | solution.py:470
  134.5 1.3 collective-permute-done.25.refs_1_
  135.8 1.4 shard_map.74.refs_4_
  137.2 1.5 shard_map.75.refs_4_
  138.8 1.4 shard_map.76.refs_4_
  140.1 9.1 %collective-permute-done.26.refs_2_ = bf16[512,256]{1,0:T(8,128)(2,1)S(1)} collective-permute-done((bf16[512,256]{1,0:T(8,128)(2,1)S(1)}, bf16[512,256]{1,0:T(8,128)(2,1)S(1)}, u32[]{:S(2)}, u32[]{:S(2)}) %collective-permute-start.26) | collective-permute-done | bytes 262176 | tf_op jit(solution)/shard_map/ppermute | solution.py:470
  149.2 2.2 %collective-permute-done.27.refs_3_ = bf16[512,256]{1,0:T(8,128)(2,1)S(1)} collective-permute-done((bf16[512,256]{1,0:T(8,128)(2,1)S(1)}, bf16[512,256]{1,0:T(8,128)(2,1)S(1)}, u32[]{:S(2)}, u32[]{:S(2)}) %collective-permute-start.27) | collective-permute-done | bytes 262176 | tf_op jit(solution)/shard_map/ppermute | solution.py:470
  151.4 1.5 shard_map.77.refs_4_
  152.9 1.9 %collective-permute-done.22.refs_1_ = bf16[512,256]{1,0:T(8,128)(2,1)S(1)} collective-permute-done((bf16[512,256]{1,0:T(8,128)(2,1)S(1)}, bf16[512,256]{1,0:T(8,128)(2,1)S(1)}, u32[]{:S(2)}, u32[]{:S(2)}) %collective-permute-start.22) | collective-permute-done | bytes 262176 | tf_op jit(solution)/shard_map/ppermute | solution.py:470
  154.8 3.8 %collective-permute-done.23.refs_2_ = bf16[512,256]{1,0:T(8,128)(2,1)S(1)} collective-permute-done((bf16[512,256]{1,0:T(8,128)(2,1)S(1)}, bf16[512,256]{1,0:T(8,128)(2,1)S(1)}, u32[]{:S(2)}, u32[]{:S(2)}) %collective-permute-start.23) | collective-permute-done | bytes 262176 | tf_op jit(solution)/shard_map/ppermute | solution.py:470
  158.7 2.6 %collective-permute-done.24.refs_3_ = bf16[512,256]{1,0:T(8,128)(2,1)S(1)} collective-permute-done((bf16[512,256]{1,0:T(8,128)(2,1)S(1)}, bf16[512,256]{1,0:T(8,128)(2,1)S(1)}, u32[]{:S(2)}, u32[]{:S(2)}) %collective-permute-start.24) | collective-permute-done | bytes 262176 | tf_op jit(solution)/shard_map/ppermute | solution.py:470
  161.3 1.5 shard_map.78
  (47 shorter events, 17.7 us)
Async XLA Ops:
  0.1 0.8 copy-start.3
  0.9 0.7 copy-start.4
  2.2 4.6 %collective-permute-start = (f32[8,768]{1,0:T(8,128)S(1)}, f32[8,768]{1,0:T(8,128)S(1)}, u32[]{:S(2)}, u32[]{:S(2)}) collective-permute-start(f32[8,768]{1,0:T(8,128)S(1)} %get-tuple-element.49), channel_id=1, source_target_pairs={{0,8},{8,16},{16,24},{24,0},{1,9},{9,17},{17,25},{25,1},{2,10},{10... | collective-permute-start | bytes 73736 | tf_op jit(solution)/shard_map/ppermute | solution.py:470
  3.8 4.7 %collective-permute-start.1 = (f32[8,768]{1,0:T(8,128)S(1)}, f32[8,768]{1,0:T(8,128)S(1)}, u32[]{:S(2)}, u32[]{:S(2)}) collective-permute-start(f32[8,768]{1,0:T(8,128)S(1)} %get-tuple-element.50), channel_id=1, source_target_pairs={{0,16},{8,24},{16,0},{24,8},{1,17},{9,25},{17,1},{25,9},{2,18},{10... | collective-permute-start | bytes 73736 | tf_op jit(solution)/shard_map/ppermute | solution.py:470
  5.0 3.8 %collective-permute-start.2 = (f32[8,768]{1,0:T(8,128)S(1)}, f32[8,768]{1,0:T(8,128)S(1)}, u32[]{:S(2)}, u32[]{:S(2)}) collective-permute-start(f32[8,768]{1,0:T(8,128)S(1)} %get-tuple-element.51), channel_id=1, source_target_pairs={{0,24},{8,0},{16,8},{24,16},{1,25},{9,1},{17,9},{25,17},{2,26},{10... | collective-permute-start | bytes 73736 | tf_op jit(solution)/shard_map/ppermute | solution.py:470
  8.9 2.2 %copy-start = (bf16[512,4096]{1,0:T(8,128)(2,1)S(1)}, bf16[512,4096]{1,0:T(8,128)(2,1)}, u32[]{:S(2)}) copy-start(bf16[512,4096]{1,0:T(8,128)(2,1)} %refs_5_.9) | copy-start | bytes 12582916
  8.9 3.5 %copy-start.1 = (bf16[512,4096]{1,0:T(8,128)(2,1)S(1)}, bf16[512,4096]{1,0:T(8,128)(2,1)}, u32[]{:S(2)}) copy-start(bf16[512,4096]{1,0:T(8,128)(2,1)} %refs_6_.9) | copy-start | bytes 12582916
  15.1 6.0 %collective-permute-start.4 = (bf16[6,128,128]{2,1,0:T(8,128)(2,1)S(1)}, bf16[6,128,128]{2,1,0:T(8,128)(2,1)S(1)}, u32[]{:S(2)}, u32[]{:S(2)}) collective-permute-start(bf16[6,128,128]{2,1,0:T(8,128)(2,1)S(1)} %get-tuple-element.58), channel_id=1, source_target_pairs={{0,8},{8,0},{16,24},{24,16},{1,9},{9,1},{17,25},{25,17},{2,10},{10... | collective-permute-start | bytes 589832 | tf_op jit(solution)/shard_map/ppermute | solution.py:473
  21.8 37.8 %copy-start.2 = (bf16[512,4096]{1,0:T(8,128)(2,1)S(1)}, bf16[512,4096]{1,0:T(8,128)(2,1)}, u32[]{:S(2)}) copy-start(bf16[512,4096]{1,0:T(8,128)(2,1)} %refs_4_.9) | copy-start | bytes 12582916
  21.8 9.1 %collective-permute-start.5 = (bf16[6,128,128]{2,1,0:T(8,128)(2,1)S(1)}, bf16[6,128,128]{2,1,0:T(8,128)(2,1)S(1)}, u32[]{:S(2)}, u32[]{:S(2)}) collective-permute-start(bf16[6,128,128]{2,1,0:T(8,128)(2,1)S(1)} %shard_map.59.refs_0_.refs_5_), channel_id=1, source_target_pairs={{0,16},{8,24},{16,0},{24,8},{1,17},{9,25},{17,1},{25,9},{2,18},{10... | collective-permute-start | bytes 589832 | tf_op jit(solution)/shard_map/ppermute | solution.py:473
  25.0 10.2 %collective-permute-start.3 = (bf16[10,128,128]{2,1,0:T(8,128)(2,1)S(1)}, bf16[10,128,128]{2,1,0:T(8,128)(2,1)S(1)}, u32[]{:S(2)}, u32[]{:S(2)}) collective-permute-start(bf16[10,128,128]{2,1,0:T(8,128)(2,1)S(1)} %get-tuple-element.56), channel_id=1, source_target_pairs={{0,8},{8,0},{16,24},{24,16},{1,9},{9,1},{17,25},{25,17},{2,10},{10... | collective-permute-start | bytes 983048 | tf_op jit(solution)/shard_map/ppermute | solution.py:473
  31.5 5.9 %collective-permute-start.7 = (bf16[6,144,128]{2,1,0:T(8,128)(2,1)S(1)}, bf16[6,144,128]{2,1,0:T(8,128)(2,1)S(1)}, u32[]{:S(2)}, u32[]{:S(2)}) collective-permute-start(bf16[6,144,128]{2,1,0:T(8,128)(2,1)S(1)} %shard_map.60.refs_3_.refs_0_), channel_id=1, source_target_pairs={{0,1},{1,0},{2,3},{3,2},{4,5},{5,4},{6,7},{7,6},{8,9},{9,8},{10,11... | collective-permute-start | bytes 663560 | tf_op jit(solution)/shard_map/ppermute | solution.py:473
  36.0 14.0 %collective-permute-start.6 = (bf16[10,128,128]{2,1,0:T(8,128)(2,1)S(1)}, bf16[10,128,128]{2,1,0:T(8,128)(2,1)S(1)}, u32[]{:S(2)}, u32[]{:S(2)}) collective-permute-start(bf16[10,128,128]{2,1,0:T(8,128)(2,1)S(1)} %shard_map.61.refs_2_.refs_0_.refs_5_), channel_id=1, source_target_pairs={{0,16},{8,24},{16,0},{24,8},{1,17},{9,25},{17,1},{25,9},{2,18},{10... | collective-permute-start | bytes 983048 | tf_op jit(solution)/shard_map/ppermute | solution.py:473
  38.1 6.0 %collective-permute-start.8 = (bf16[6,144,128]{2,1,0:T(8,128)(2,1)S(1)}, bf16[6,144,128]{2,1,0:T(8,128)(2,1)S(1)}, u32[]{:S(2)}, u32[]{:S(2)}) collective-permute-start(bf16[6,144,128]{2,1,0:T(8,128)(2,1)S(1)} %get-tuple-element.59.refs_0_), channel_id=1, source_target_pairs={{0,2},{1,3},{2,0},{3,1},{4,6},{5,7},{6,4},{7,5},{8,10},{9,11},{10,... | collective-permute-start | bytes 663560 | tf_op jit(solution)/shard_map/ppermute | solution.py:473
  44.8 6.0 %collective-permute-start.10 = (bf16[6,144,128]{2,1,0:T(8,128)(2,1)S(1)}, bf16[6,144,128]{2,1,0:T(8,128)(2,1)S(1)}, u32[]{:S(2)}, u32[]{:S(2)}) collective-permute-start(bf16[6,144,128]{2,1,0:T(8,128)(2,1)S(1)} %get-tuple-element.62.refs_0_), channel_id=1, source_target_pairs={{0,4},{1,5},{2,6},{3,7},{4,0},{5,1},{6,2},{7,3},{8,12},{9,13},{10,... | collective-permute-start | bytes 663560 | tf_op jit(solution)/shard_map/ppermute | solution.py:473
  50.7 3.3 %collective-permute-start.9 = (bf16[10,144,128]{2,1,0:T(8,128)(2,1)S(1)}, bf16[10,144,128]{2,1,0:T(8,128)(2,1)S(1)}, u32[]{:S(2)}, u32[]{:S(2)}) collective-permute-start(bf16[10,144,128]{2,1,0:T(8,128)(2,1)S(1)} %shard_map.64.refs_8_.refs_0_), channel_id=1, source_target_pairs={{0,1},{1,0},{2,3},{3,2},{4,5},{5,4},{6,7},{7,6},{8,9},{9,8},{10,11... | collective-permute-start | bytes 1105928 | tf_op jit(solution)/shard_map/ppermute | solution.py:473
  51.6 8.0 %collective-permute-start.12 = (bf16[6,128,128]{2,1,0:T(8,128)(2,1)S(1)}, bf16[6,128,128]{2,1,0:T(8,128)(2,1)S(1)}, u32[]{:S(2)}, u32[]{:S(2)}) collective-permute-start(bf16[6,128,128]{2,1,0:T(8,128)(2,1)S(1)} %get-tuple-element.66), channel_id=1, source_target_pairs={{0,8},{8,0},{16,24},{24,16},{1,9},{9,1},{17,25},{25,17},{2,10},{10... | collective-permute-start | bytes 589832 | tf_op jit(solution)/shard_map/ppermute | solution.py:473
  54.8 12.7 %collective-permute-start.11 = (bf16[10,144,128]{2,1,0:T(8,128)(2,1)S(1)}, bf16[10,144,128]{2,1,0:T(8,128)(2,1)S(1)}, u32[]{:S(2)}, u32[]{:S(2)}) collective-permute-start(bf16[10,144,128]{2,1,0:T(8,128)(2,1)S(1)} %get-tuple-element.64.refs_0_), channel_id=1, source_target_pairs={{0,2},{1,3},{2,0},{3,1},{4,6},{5,7},{6,4},{7,5},{8,10},{9,11},{10,... | collective-permute-start | bytes 1105928 | tf_op jit(solution)/shard_map/ppermute | solution.py:473
  62.1 5.4 %collective-permute-start.13 = (bf16[512,128]{1,0:T(8,128)(2,1)S(1)}, bf16[512,128]{1,0:T(8,128)(2,1)S(1)}, u32[]{:S(2)}, u32[]{:S(2)}) collective-permute-start(bf16[512,128]{1,0:T(8,128)(2,1)S(1)} %get-tuple-element.68), channel_id=1, source_target_pairs={{0,8},{8,16},{16,24},{24,0},{1,9},{9,17},{17,25},{25,1},{2,10},{10... | collective-permute-start | bytes 393224 | tf_op jit(solution)/shard_map/ppermute | solution.py:470
  63.7 11.4 %collective-permute-start.15 = (bf16[512,128]{1,0:T(8,128)(2,1)S(1)}, bf16[512,128]{1,0:T(8,128)(2,1)S(1)}, u32[]{:S(2)}, u32[]{:S(2)}) collective-permute-start(bf16[512,128]{1,0:T(8,128)(2,1)S(1)} %get-tuple-element.71), channel_id=1, source_target_pairs={{0,24},{8,0},{16,8},{24,16},{1,25},{9,1},{17,9},{25,17},{2,26},{10... | collective-permute-start | bytes 393224 | tf_op jit(solution)/shard_map/ppermute | solution.py:470
  64.2 15.6 %collective-permute-start.16 = (bf16[512,128]{1,0:T(8,128)(2,1)S(1)}, bf16[512,128]{1,0:T(8,128)(2,1)S(1)}, u32[]{:S(2)}, u32[]{:S(2)}) collective-permute-start(bf16[512,128]{1,0:T(8,128)(2,1)S(1)} %get-tuple-element.73), channel_id=1, source_target_pairs={{0,16},{8,24},{16,0},{24,8},{1,17},{9,25},{17,1},{25,9},{2,18},{10... | collective-permute-start | bytes 393224 | tf_op jit(solution)/shard_map/ppermute | solution.py:470
  68.3 11.5 %collective-permute-start.14 = (bf16[10,144,128]{2,1,0:T(8,128)(2,1)S(1)}, bf16[10,144,128]{2,1,0:T(8,128)(2,1)S(1)}, u32[]{:S(2)}, u32[]{:S(2)}) collective-permute-start(bf16[10,144,128]{2,1,0:T(8,128)(2,1)S(1)} %get-tuple-element.69.refs_0_), channel_id=1, source_target_pairs={{0,4},{1,5},{2,6},{3,7},{4,0},{5,1},{6,2},{7,3},{8,12},{9,13},{10,... | collective-permute-start | bytes 1105928 | tf_op jit(solution)/shard_map/ppermute | solution.py:473
  80.8 20.6 %collective-permute-start.17 = (bf16[10,128,128]{2,1,0:T(8,128)(2,1)S(1)}, bf16[10,128,128]{2,1,0:T(8,128)(2,1)S(1)}, u32[]{:S(2)}, u32[]{:S(2)}) collective-permute-start(bf16[10,128,128]{2,1,0:T(8,128)(2,1)S(1)} %get-tuple-element.75), channel_id=1, source_target_pairs={{0,8},{8,0},{16,24},{24,16},{1,9},{9,1},{17,25},{25,17},{2,10},{10... | collective-permute-start | bytes 983048 | tf_op jit(solution)/shard_map/ppermute | solution.py:473
  82.1 15.0 %collective-permute-start.18 = (bf16[512,256]{1,0:T(8,128)(2,1)S(1)}, bf16[512,256]{1,0:T(8,128)(2,1)S(1)}, u32[]{:S(2)}, u32[]{:S(2)}) collective-permute-start(bf16[512,256]{1,0:T(8,128)(2,1)S(1)} %get-tuple-element.76), channel_id=1, source_target_pairs={{0,8},{8,16},{16,24},{24,0},{1,9},{9,17},{17,25},{25,1},{2,10},{10... | collective-permute-start | bytes 786440 | tf_op jit(solution)/shard_map/ppermute | solution.py:470
  84.5 24.7 %collective-permute-start.19 = (bf16[512,256]{1,0:T(8,128)(2,1)S(1)}, bf16[512,256]{1,0:T(8,128)(2,1)S(1)}, u32[]{:S(2)}, u32[]{:S(2)}) collective-permute-start(bf16[512,256]{1,0:T(8,128)(2,1)S(1)} %get-tuple-element.78), channel_id=1, source_target_pairs={{0,16},{8,24},{16,0},{24,8},{1,17},{9,25},{17,1},{25,9},{2,18},{10... | collective-permute-start | bytes 786440 | tf_op jit(solution)/shard_map/ppermute | solution.py:470
  85.9 31.8 %collective-permute-start.20 = (bf16[512,256]{1,0:T(8,128)(2,1)S(1)}, bf16[512,256]{1,0:T(8,128)(2,1)S(1)}, u32[]{:S(2)}, u32[]{:S(2)}) collective-permute-start(bf16[512,256]{1,0:T(8,128)(2,1)S(1)} %get-tuple-element.80), channel_id=1, source_target_pairs={{0,24},{8,0},{16,8},{24,16},{1,25},{9,1},{17,9},{25,17},{2,26},{10... | collective-permute-start | bytes 786440 | tf_op jit(solution)/shard_map/ppermute | solution.py:470
  103.9 13.8 %collective-permute-start.21 = (bf16[512,128]{1,0:T(8,128)(2,1)S(1)}, bf16[512,128]{1,0:T(8,128)(2,1)S(1)}, u32[]{:S(2)}, u32[]{:S(2)}) collective-permute-start(bf16[512,128]{1,0:T(8,128)(2,1)S(1)} %get-tuple-element.81), channel_id=1, source_target_pairs={{0,8},{8,16},{16,24},{24,0},{1,9},{9,17},{17,25},{25,1},{2,10},{10... | collective-permute-start | bytes 393224 | tf_op jit(solution)/shard_map/ppermute | solution.py:470
  105.3 17.9 %collective-permute-start.28 = (bf16[512,128]{1,0:T(8,128)(2,1)S(1)}, bf16[512,128]{1,0:T(8,128)(2,1)S(1)}, u32[]{:S(2)}, u32[]{:S(2)}) collective-permute-start(bf16[512,128]{1,0:T(8,128)(2,1)S(1)} %get-tuple-element.89), channel_id=1, source_target_pairs={{0,16},{8,24},{16,0},{24,8},{1,17},{9,25},{17,1},{25,9},{2,18},{10... | collective-permute-start | bytes 393224 | tf_op jit(solution)/shard_map/ppermute | solution.py:470
  108.8 25.7 %collective-permute-start.29 = (bf16[512,128]{1,0:T(8,128)(2,1)S(1)}, bf16[512,128]{1,0:T(8,128)(2,1)S(1)}, u32[]{:S(2)}, u32[]{:S(2)}) collective-permute-start(bf16[512,128]{1,0:T(8,128)(2,1)S(1)} %get-tuple-element.90), channel_id=1, source_target_pairs={{0,24},{8,0},{16,8},{24,16},{1,25},{9,1},{17,9},{25,17},{2,26},{10... | collective-permute-start | bytes 393224 | tf_op jit(solution)/shard_map/ppermute | solution.py:470
  113.9 22.0 %collective-permute-start.25 = (bf16[512,256]{1,0:T(8,128)(2,1)S(1)}, bf16[512,256]{1,0:T(8,128)(2,1)S(1)}, u32[]{:S(2)}, u32[]{:S(2)}) collective-permute-start(bf16[512,256]{1,0:T(8,128)(2,1)S(1)} %get-tuple-element.86), channel_id=1, source_target_pairs={{0,8},{8,16},{16,24},{24,0},{1,9},{9,17},{17,25},{25,1},{2,10},{10... | collective-permute-start | bytes 786440 | tf_op jit(solution)/shard_map/ppermute | solution.py:470
  117.7 31.6 %collective-permute-start.26 = (bf16[512,256]{1,0:T(8,128)(2,1)S(1)}, bf16[512,256]{1,0:T(8,128)(2,1)S(1)}, u32[]{:S(2)}, u32[]{:S(2)}) collective-permute-start(bf16[512,256]{1,0:T(8,128)(2,1)S(1)} %get-tuple-element.87), channel_id=1, source_target_pairs={{0,16},{8,24},{16,0},{24,8},{1,17},{9,25},{17,1},{25,9},{2,18},{10... | collective-permute-start | bytes 786440 | tf_op jit(solution)/shard_map/ppermute | solution.py:470
  117.7 33.7 %collective-permute-start.27 = (bf16[512,256]{1,0:T(8,128)(2,1)S(1)}, bf16[512,256]{1,0:T(8,128)(2,1)S(1)}, u32[]{:S(2)}, u32[]{:S(2)}) collective-permute-start(bf16[512,256]{1,0:T(8,128)(2,1)S(1)} %get-tuple-element.88), channel_id=1, source_target_pairs={{0,24},{8,0},{16,8},{24,16},{1,25},{9,1},{17,9},{25,17},{2,26},{10... | collective-permute-start | bytes 786440 | tf_op jit(solution)/shard_map/ppermute | solution.py:470
  123.2 31.6 %collective-permute-start.22 = (bf16[512,256]{1,0:T(8,128)(2,1)S(1)}, bf16[512,256]{1,0:T(8,128)(2,1)S(1)}, u32[]{:S(2)}, u32[]{:S(2)}) collective-permute-start(bf16[512,256]{1,0:T(8,128)(2,1)S(1)} %get-tuple-element.83), channel_id=1, source_target_pairs={{0,8},{8,16},{16,24},{24,0},{1,9},{9,17},{17,25},{25,1},{2,10},{10... | collective-permute-start | bytes 786440 | tf_op jit(solution)/shard_map/ppermute | solution.py:470
  134.5 24.2 %collective-permute-start.23 = (bf16[512,256]{1,0:T(8,128)(2,1)S(1)}, bf16[512,256]{1,0:T(8,128)(2,1)S(1)}, u32[]{:S(2)}, u32[]{:S(2)}) collective-permute-start(bf16[512,256]{1,0:T(8,128)(2,1)S(1)} %get-tuple-element.84), channel_id=1, source_target_pairs={{0,16},{8,24},{16,0},{24,8},{1,17},{9,25},{17,1},{25,9},{2,18},{10... | collective-permute-start | bytes 786440 | tf_op jit(solution)/shard_map/ppermute | solution.py:470
  135.8 25.5 %collective-permute-start.24 = (bf16[512,256]{1,0:T(8,128)(2,1)S(1)}, bf16[512,256]{1,0:T(8,128)(2,1)S(1)}, u32[]{:S(2)}, u32[]{:S(2)}) collective-permute-start(bf16[512,256]{1,0:T(8,128)(2,1)S(1)} %get-tuple-element.85), channel_id=1, source_target_pairs={{0,24},{8,0},{16,8},{24,16},{1,25},{9,1},{17,9},{25,17},{2,26},{10... | collective-permute-start | bytes 786440 | tf_op jit(solution)/shard_map/ppermute | solution.py:470

commit v3 on v2

--- a/solution.py
+++ b/solution.py
@@ -8,7 +8,7 @@
 from jax.sharding import PartitionSpec as P
 
 GROUPS = ((3, 0, (1, 2)), (5, 0, (1, 2, 2)))
-ORDER = ('k0', 'k1', 'k0', 'k0', 'k1', 'k0', 'k0', 'k1', 'k0', 'k1', 'k0', 'w001', 'k1', 'w003', 'k0', 'w002', 'k1', 'w011', 'k1', 'w012', 'k1', 'w013', 'w101', 'k1', 'p00', 'p01', 'p10', 'p11', 'p12')
+ORDER = ('k0', 'k1', 'k0', 'k0', 'k1', 'k0', 'k0', 'k1', 'k0', 'k1', 'k0', 'k1', 'w001', 'k0', 'w002', 'w003', 'k1', 'w011', 'k1', 'w012', 'w013', 'k1', 'w101', 'w103', 'k1', 'p00', 'p01', 'p10', 'p11', 'p12')
 CHUNK = 256
 VMEM_BYTES = 16 * 1024 * 1024
 SCALE = 1.0e9
@@ -482,7 +482,6 @@
         unpack_decays, got,
         [shape(heads * parts, rows, dtype=F32), shape(heads * parts, 8, 128, dtype=F32), shape(heads * parts, 128, dtype=F32)],
         scratch=[pltpu.VMEM((heads * parts, rows), F32)],
-        cost=cost_us(8),
     )
 
     def outputs(first, m, states, states_of):

time: 163 us -> 159 us (0.975)
  starting transfers between devices: 39.6 us -> 36.7 us
  local copies, waits for them, and re-layouts: 3.96 us -> 1.54 us
    ppermute x18, starting transfers between devices: 24.2 us -> 21.5 us  [shift(): return lax.ppermute(x, 'grp', [(i, (i + k) % parts) for i in range(parts)])]
    unnamed x10, local copies, waits for them, and re-layouts: 3.96 us -> 1.54 us
    ppermute x18, waiting for transfers between devices: 50.1 us -> 52 us  [shift(): return lax.ppermute(x, 'grp', [(i, (i + k) % parts) for i in range(parts)])]
  transfers between devices with their start and end apart: 30 -> 30, of which waited for: 19 -> 18; matrix products, arithmetic and copies ran while one was open for 0% -> 0% of each run, Pallas kernels for 21% -> 22%
where the time goes in v3:
time: 159 us
  waiting for transfers between devices  78 us (49%)
  Pallas kernels  42.5 us (27%)
  starting transfers between devices  36.7 us (23%)
    ppermute x18, waiting for transfers between devices, shift(): return lax.ppermute(x, 'grp', [(i, (i + k) % parts) for i in range(parts)])  52 us
    pallas_call x24, Pallas kernels, __call__(): pl.pallas_call(body, out_shape=outs, in_specs=[pl.BlockSpec(memory_space=...  42.5 us
    ppermute x12, waiting for transfers between devices, swap(): lax.ppermute(x, axis, [(i, i ^ bit) for i in range(lax.axis_size(axis))])  26 us
    ppermute x18, starting transfers between devices, shift(): return lax.ppermute(x, 'grp', [(i, (i + k) % parts) for i in range(parts)])  21.5 us
    ppermute x12, starting transfers between devices, swap(): lax.ppermute(x, axis, [(i, i ^ bit) for i in range(lax.axis_size(axis))])  15.2 us
  transfers between devices with their start and end apart: 30, of which 18 were waited for; matrix products, arithmetic and copies ran while one was open for 0% of the time, Pallas kernels for 22%

profile of v3, /device:TPU:10, one launch (start us, length us, event | category | flops | bytes accessed | tf_op | source)
XLA Modules:
  0.0 159.2 jit_solution(10669031240363828772)
XLA Ops:
  2.2 1.6 collective-permute-start
  3.8 1.2 collective-permute-start.1
  5.0 1.8 %collective-permute-start.2 = (f32[8,768]{1,0:T(8,128)S(1)}, f32[8,768]{1,0:T(8,128)S(1)}, u32[]{:S(2)}, u32[]{:S(2)}) collective-permute-start(f32[8,768]{1,0:T(8,128)S(1)} %get-tuple-element.51), channel_id=1, source_target_pairs={{0,24},{8,0},{16,8},{24,16},{1,25},{9,1},{17,9},{25,17},{2,26},{10... | collective-permute-start | bytes 73736 | tf_op jit(solution)/shard_map/ppermute | solution.py:470
  6.8 1.7 %collective-permute-done.1.refs_2_ = f32[8,768]{1,0:T(8,128)S(1)} collective-permute-done((f32[8,768]{1,0:T(8,128)S(1)}, f32[8,768]{1,0:T(8,128)S(1)}, u32[]{:S(2)}, u32[]{:S(2)}) %collective-permute-start.1) | collective-permute-done | bytes 24608 | tf_op jit(solution)/shard_map/ppermute | solution.py:470
  8.9 1.0 shard_map.56
  9.9 2.7 %shard_map.57 = (bf16[6,128,128]{2,1,0:T(8,128)(2,1)S(1)}, bf16[6,128,128]{2,1,0:T(8,128)(2,1)S(1)}) custom-call(s32[2]{0:T(128)S(1)} %pad_add_fusion.s_ref, f32[32,512]{1,0:T(8,128)S(1)} %get-tuple-element.52.refs_0_, bf16[512,4096]{1,0:T(8,128)(2,1)S(1)} %copy-done, bf16[512,4096]{1,0:T(8,128)(2,1)S(1)} %copy-done.1), custom_call_target="tpu_custom_call" | custom-call | flops 3000000000 | bytes 1000 | tf_op jit(solution)/shard_map/pallas_call | solution.py:126
  12.7 1.9 %collective-permute-start.4 = (bf16[6,128,128]{2,1,0:T(8,128)(2,1)S(1)}, bf16[6,128,128]{2,1,0:T(8,128)(2,1)S(1)}, u32[]{:S(2)}, u32[]{:S(2)}) collective-permute-start(bf16[6,128,128]{2,1,0:T(8,128)(2,1)S(1)} %get-tuple-element.58), channel_id=1, source_target_pairs={{0,8},{8,0},{16,24},{24,16},{1,9},{9,1},{17,25},{25,17},{2,10},{10... | collective-permute-start | bytes 589832 | tf_op jit(solution)/shard_map/ppermute | solution.py:473
  14.5 4.2 %shard_map.58 = (bf16[10,128,128]{2,1,0:T(8,128)(2,1)S(1)}, bf16[10,128,128]{2,1,0:T(8,128)(2,1)S(1)}) custom-call(s32[2]{0:T(128)S(1)} %pad_add_fusion.s_ref, f32[32,512]{1,0:T(8,128)S(1)} %get-tuple-element.52.refs_0_, bf16[512,4096]{1,0:T(8,128)(2,1)S(1)} %copy-done, bf16[512,4096]{1,0:T(8,128)(2,1)S(1)} %copy-done.1, ...), custom_call_target="tpu_custom_call" | custom-call | flops 5000000000 | bytes 1000 | tf_op jit(solution)/shard_map/pallas_call | solution.py:126
  19.4 3.2 %collective-permute-start.5 = (bf16[6,128,128]{2,1,0:T(8,128)(2,1)S(1)}, bf16[6,128,128]{2,1,0:T(8,128)(2,1)S(1)}, u32[]{:S(2)}, u32[]{:S(2)}) collective-permute-start(bf16[6,128,128]{2,1,0:T(8,128)(2,1)S(1)} %shard_map.59.refs_0_.refs_5_), channel_id=1, source_target_pairs={{0,16},{8,24},{16,0},{24,8},{1,17},{9,25},{17,1},{25,9},{2,18},{10... | collective-permute-start | bytes 589832 | tf_op jit(solution)/shard_map/ppermute | solution.py:473
  23.2 5.3 %collective-permute-done.5.refs_1_.refs_6_ = bf16[6,128,128]{2,1,0:T(8,128)(2,1)S(1)} collective-permute-done((bf16[6,128,128]{2,1,0:T(8,128)(2,1)S(1)}, bf16[6,128,128]{2,1,0:T(8,128)(2,1)S(1)}, u32[]{:S(2)}, u32[]{:S(2)}) %collective-permute-start.5) | collective-permute-done | bytes 196640 | tf_op jit(solution)/shard_map/ppermute | solution.py:473
  29.2 3.7 %collective-permute-done.3.refs_1_.refs_4_ = bf16[10,128,128]{2,1,0:T(8,128)(2,1)S(1)} collective-permute-done((bf16[10,128,128]{2,1,0:T(8,128)(2,1)S(1)}, bf16[10,128,128]{2,1,0:T(8,128)(2,1)S(1)}, u32[]{:S(2)}, u32[]{:S(2)}) %collective-permute-start.3) | collective-permute-done | bytes 327712 | tf_op jit(solution)/shard_map/ppermute | solution.py:473
  33.6 1.4 collective-permute-start.6
  36.3 5.4 %collective-permute-done.8.refs_1_ = bf16[6,144,128]{2,1,0:T(8,128)(2,1)S(1)} collective-permute-done((bf16[6,144,128]{2,1,0:T(8,128)(2,1)S(1)}, bf16[6,144,128]{2,1,0:T(8,128)(2,1)S(1)}, u32[]{:S(2)}, u32[]{:S(2)}) %collective-permute-start.8) | collective-permute-done | bytes 221216 | tf_op jit(solution)/shard_map/ppermute | solution.py:473
  42.4 1.6 collective-permute-start.10
  44.0 3.6 %collective-permute-done.6.refs_1_.refs_6_ = bf16[10,128,128]{2,1,0:T(8,128)(2,1)S(1)} collective-permute-done((bf16[10,128,128]{2,1,0:T(8,128)(2,1)S(1)}, bf16[10,128,128]{2,1,0:T(8,128)(2,1)S(1)}, u32[]{:S(2)}, u32[]{:S(2)}) %collective-permute-start.6) | collective-permute-done | bytes 327712 | tf_op jit(solution)/shard_map/ppermute | solution.py:473
  49.2 2.5 %collective-permute-start.12 = (bf16[6,128,128]{2,1,0:T(8,128)(2,1)S(1)}, bf16[6,128,128]{2,1,0:T(8,128)(2,1)S(1)}, u32[]{:S(2)}, u32[]{:S(2)}) collective-permute-start(bf16[6,128,128]{2,1,0:T(8,128)(2,1)S(1)} %get-tuple-element.66), channel_id=1, source_target_pairs={{0,8},{8,0},{16,24},{24,16},{1,9},{9,1},{17,25},{25,17},{2,10},{10... | collective-permute-start | bytes 589832 | tf_op jit(solution)/shard_map/ppermute | solution.py:473
  53.0 4.2 %collective-permute-done.12.refs_3_ = bf16[6,128,128]{2,1,0:T(8,128)(2,1)S(1)} collective-permute-done((bf16[6,128,128]{2,1,0:T(8,128)(2,1)S(1)}, bf16[6,128,128]{2,1,0:T(8,128)(2,1)S(1)}, u32[]{:S(2)}, u32[]{:S(2)}) %collective-permute-start.12) | collective-permute-done | bytes 196640 | tf_op jit(solution)/shard_map/ppermute | solution.py:473
  57.2 2.5 %shard_map.67 = (bf16[512,128]{1,0:T(8,128)(2,1)S(1)}, bf16[512,128]{1,0:T(8,128)(2,1)S(1)}, bf16[512,128]{1,0:T(8,128)(2,1)S(1)}, bf16[512,128]{1,0:T(8,128)(2,1)S(1)}) custom-call(s32[2]{0:T(128)S(1)} %pad_add_fusion.s_ref, f32[32,512]{1,0:T(8,128)S(1)} %get-tuple-element.52.refs_0_, f32[32,128]{1,0:T(8,128)S(1)} %get-tuple-element.53.refs_1_, ...), custom_call_target="tpu_custom_call" | custom-call | flops 2500000000 | bytes 1000 | tf_op jit(solution)/shard_map/pallas_call | solution.py:126
  59.7 1.6 %collective-permute-start.14 = (bf16[512,128]{1,0:T(8,128)(2,1)S(1)}, bf16[512,128]{1,0:T(8,128)(2,1)S(1)}, u32[]{:S(2)}, u32[]{:S(2)}) collective-permute-start(bf16[512,128]{1,0:T(8,128)(2,1)S(1)} %get-tuple-element.70), channel_id=1, source_target_pairs={{0,8},{8,16},{16,24},{24,0},{1,9},{9,17},{17,25},{25,1},{2,10},{10... | collective-permute-start | bytes 393224 | tf_op jit(solution)/shard_map/ppermute | solution.py:470
  61.3 2.5 %collective-permute-start.15 = (bf16[512,128]{1,0:T(8,128)(2,1)S(1)}, bf16[512,128]{1,0:T(8,128)(2,1)S(1)}, u32[]{:S(2)}, u32[]{:S(2)}) collective-permute-start(bf16[512,128]{1,0:T(8,128)(2,1)S(1)} %get-tuple-element.72), channel_id=1, source_target_pairs={{0,16},{8,24},{16,0},{24,8},{1,17},{9,25},{17,1},{25,9},{2,18},{10... | collective-permute-start | bytes 393224 | tf_op jit(solution)/shard_map/ppermute | solution.py:470
  65.4 1.6 collective-permute-start.13
  66.9 3.4 %collective-permute-done.14.refs_8_.refs_1_ = bf16[512,128]{1,0:T(8,128)(2,1)S(1)} collective-permute-done((bf16[512,128]{1,0:T(8,128)(2,1)S(1)}, bf16[512,128]{1,0:T(8,128)(2,1)S(1)}, u32[]{:S(2)}, u32[]{:S(2)}) %collective-permute-start.14) | collective-permute-done | bytes 131104 | tf_op jit(solution)/shard_map/ppermute | solution.py:470
  70.4 4.7 %shard_map.69 = (bf16[512,256]{1,0:T(8,128)(2,1)S(1)}, bf16[512,256]{1,0:T(8,128)(2,1)S(1)}, bf16[512,256]{1,0:T(8,128)(2,1)S(1)}, bf16[512,256]{1,0:T(8,128)(2,1)S(1)}) custom-call(s32[2]{0:T(128)S(1)} %pad_add_fusion.s_ref, f32[32,512]{1,0:T(8,128)S(1)} %get-tuple-element.52.refs_0_, f32[32,128]{1,0:T(8,128)S(1)} %get-tuple-element.53.refs_1_, ...), custom_call_target="tpu_custom_call" | custom-call | flops 5000000000 | bytes 1000 | tf_op jit(solution)/shard_map/pallas_call | solution.py:126
  75.1 1.0 shard_map.70
  76.0 1.2 collective-permute-start.17
  77.2 1.6 %collective-permute-start.18 = (bf16[512,256]{1,0:T(8,128)(2,1)S(1)}, bf16[512,256]{1,0:T(8,128)(2,1)S(1)}, u32[]{:S(2)}, u32[]{:S(2)}) collective-permute-start(bf16[512,256]{1,0:T(8,128)(2,1)S(1)} %get-tuple-element.76), channel_id=1, source_target_pairs={{0,8},{8,16},{16,24},{24,0},{1,9},{9,17},{17,25},{25,1},{2,10},{10... | collective-permute-start | bytes 786440 | tf_op jit(solution)/shard_map/ppermute | solution.py:470
  78.8 1.7 %collective-permute-start.19 = (bf16[512,256]{1,0:T(8,128)(2,1)S(1)}, bf16[512,256]{1,0:T(8,128)(2,1)S(1)}, u32[]{:S(2)}, u32[]{:S(2)}) collective-permute-start(bf16[512,256]{1,0:T(8,128)(2,1)S(1)} %get-tuple-element.78), channel_id=1, source_target_pairs={{0,16},{8,24},{16,0},{24,8},{1,17},{9,25},{17,1},{25,9},{2,18},{10... | collective-permute-start | bytes 786440 | tf_op jit(solution)/shard_map/ppermute | solution.py:470
  80.5 1.7 %collective-permute-start.20 = (bf16[512,256]{1,0:T(8,128)(2,1)S(1)}, bf16[512,256]{1,0:T(8,128)(2,1)S(1)}, u32[]{:S(2)}, u32[]{:S(2)}) collective-permute-start(bf16[512,256]{1,0:T(8,128)(2,1)S(1)} %get-tuple-element.79), channel_id=1, source_target_pairs={{0,24},{8,0},{16,8},{24,16},{1,25},{9,1},{17,9},{25,17},{2,26},{10... | collective-permute-start | bytes 786440 | tf_op jit(solution)/shard_map/ppermute | solution.py:470
  82.2 10.2 %collective-permute-done.18.refs_7_.refs_1_ = bf16[512,256]{1,0:T(8,128)(2,1)S(1)} collective-permute-done((bf16[512,256]{1,0:T(8,128)(2,1)S(1)}, bf16[512,256]{1,0:T(8,128)(2,1)S(1)}, u32[]{:S(2)}, u32[]{:S(2)}) %collective-permute-start.18) | collective-permute-done | bytes 262176 | tf_op jit(solution)/shard_map/ppermute | solution.py:470
  92.4 3.9 %collective-permute-done.17.refs_3_ = bf16[10,128,128]{2,1,0:T(8,128)(2,1)S(1)} collective-permute-done((bf16[10,128,128]{2,1,0:T(8,128)(2,1)S(1)}, bf16[10,128,128]{2,1,0:T(8,128)(2,1)S(1)}, u32[]{:S(2)}, u32[]{:S(2)}) %collective-permute-start.17) | collective-permute-done | bytes 327712 | tf_op jit(solution)/shard_map/ppermute | solution.py:473
  96.2 2.5 %shard_map.71 = (bf16[512,128]{1,0:T(8,128)(2,1)S(1)}, bf16[512,128]{1,0:T(8,128)(2,1)S(1)}, bf16[512,128]{1,0:T(8,128)(2,1)S(1)}, bf16[512,128]{1,0:T(8,128)(2,1)S(1)}) custom-call(s32[2]{0:T(128)S(1)} %pad_add_fusion.s_ref, f32[32,512]{1,0:T(8,128)S(1)} %get-tuple-element.52.refs_0_, f32[32,128]{1,0:T(8,128)S(1)} %get-tuple-element.53.refs_1_, ...), custom_call_target="tpu_custom_call" | custom-call | flops 2500000000 | bytes 1000 | tf_op jit(solution)/shard_map/pallas_call | solution.py:126
  98.9 2.5 %collective-permute-start.22 = (bf16[512,128]{1,0:T(8,128)(2,1)S(1)}, bf16[512,128]{1,0:T(8,128)(2,1)S(1)}, u32[]{:S(2)}, u32[]{:S(2)}) collective-permute-start(bf16[512,128]{1,0:T(8,128)(2,1)S(1)} %get-tuple-element.82), channel_id=1, source_target_pairs={{0,24},{8,0},{16,8},{24,16},{1,25},{9,1},{17,9},{25,17},{2,26},{10... | collective-permute-start | bytes 393224 | tf_op jit(solution)/shard_map/ppermute | solution.py:470
  101.4 2.3 %collective-permute-start.29 = (bf16[512,128]{1,0:T(8,128)(2,1)S(1)}, bf16[512,128]{1,0:T(8,128)(2,1)S(1)}, u32[]{:S(2)}, u32[]{:S(2)}) collective-permute-start(bf16[512,128]{1,0:T(8,128)(2,1)S(1)} %get-tuple-element.90), channel_id=1, source_target_pairs={{0,16},{8,24},{16,0},{24,8},{1,17},{9,25},{17,1},{25,9},{2,18},{10... | collective-permute-start | bytes 393224 | tf_op jit(solution)/shard_map/ppermute | solution.py:470
  103.7 4.4 %collective-permute-done.20.refs_9_.refs_3_ = bf16[512,256]{1,0:T(8,128)(2,1)S(1)} collective-permute-done((bf16[512,256]{1,0:T(8,128)(2,1)S(1)}, bf16[512,256]{1,0:T(8,128)(2,1)S(1)}, u32[]{:S(2)}, u32[]{:S(2)}) %collective-permute-start.20) | collective-permute-done | bytes 262176 | tf_op jit(solution)/shard_map/ppermute | solution.py:470
  108.0 4.7 %shard_map.72 = (bf16[512,256]{1,0:T(8,128)(2,1)S(1)}, bf16[512,256]{1,0:T(8,128)(2,1)S(1)}, bf16[512,256]{1,0:T(8,128)(2,1)S(1)}, bf16[512,256]{1,0:T(8,128)(2,1)S(1)}) custom-call(s32[2]{0:T(128)S(1)} %pad_add_fusion.s_ref, f32[32,512]{1,0:T(8,128)S(1)} %get-tuple-element.52.refs_0_, f32[32,128]{1,0:T(8,128)S(1)} %get-tuple-element.53.refs_1_, ...), custom_call_target="tpu_custom_call" | custom-call | flops 5000000000 | bytes 1000 | tf_op jit(solution)/shard_map/pallas_call | solution.py:126
  112.9 1.9 %collective-permute-start.28 = (bf16[512,256]{1,0:T(8,128)(2,1)S(1)}, bf16[512,256]{1,0:T(8,128)(2,1)S(1)}, u32[]{:S(2)}, u32[]{:S(2)}) collective-permute-start(bf16[512,256]{1,0:T(8,128)(2,1)S(1)} %get-tuple-element.89), channel_id=1, source_target_pairs={{0,24},{8,0},{16,8},{24,16},{1,25},{9,1},{17,9},{25,17},{2,26},{10... | collective-permute-start | bytes 786440 | tf_op jit(solution)/shard_map/ppermute | solution.py:470
  114.8 6.5 %collective-permute-done.22.refs_9_.refs_3_ = bf16[512,128]{1,0:T(8,128)(2,1)S(1)} collective-permute-done((bf16[512,128]{1,0:T(8,128)(2,1)S(1)}, bf16[512,128]{1,0:T(8,128)(2,1)S(1)}, u32[]{:S(2)}, u32[]{:S(2)}) %collective-permute-start.22) | collective-permute-done | bytes 131104 | tf_op jit(solution)/shard_map/ppermute | solution.py:470
  121.3 4.7 %shard_map.73 = (bf16[512,256]{1,0:T(8,128)(2,1)S(1)}, bf16[512,256]{1,0:T(8,128)(2,1)S(1)}, bf16[512,256]{1,0:T(8,128)(2,1)S(1)}, bf16[512,256]{1,0:T(8,128)(2,1)S(1)}) custom-call(s32[2]{0:T(128)S(1)} %pad_add_fusion.s_ref, f32[32,512]{1,0:T(8,128)S(1)} %get-tuple-element.52.refs_0_, f32[32,128]{1,0:T(8,128)S(1)} %get-tuple-element.53.refs_1_, ...), custom_call_target="tpu_custom_call" | custom-call | flops 5000000000 | bytes 1000 | tf_op jit(solution)/shard_map/pallas_call | solution.py:126
  126.2 7.2 %collective-permute-done.26.refs_1_ = bf16[512,256]{1,0:T(8,128)(2,1)S(1)} collective-permute-done((bf16[512,256]{1,0:T(8,128)(2,1)S(1)}, bf16[512,256]{1,0:T(8,128)(2,1)S(1)}, u32[]{:S(2)}, u32[]{:S(2)}) %collective-permute-start.26) | collective-permute-done | bytes 262176 | tf_op jit(solution)/shard_map/ppermute | solution.py:470
  133.4 1.4 shard_map.74.refs_4_
  134.8 1.5 shard_map.75.refs_4_
  136.3 1.4 shard_map.76.refs_4_
  137.7 8.6 %collective-permute-done.27.refs_2_ = bf16[512,256]{1,0:T(8,128)(2,1)S(1)} collective-permute-done((bf16[512,256]{1,0:T(8,128)(2,1)S(1)}, bf16[512,256]{1,0:T(8,128)(2,1)S(1)}, u32[]{:S(2)}, u32[]{:S(2)}) %collective-permute-start.27) | collective-permute-done | bytes 262176 | tf_op jit(solution)/shard_map/ppermute | solution.py:470
  146.3 2.2 %collective-permute-done.28.refs_3_ = bf16[512,256]{1,0:T(8,128)(2,1)S(1)} collective-permute-done((bf16[512,256]{1,0:T(8,128)(2,1)S(1)}, bf16[512,256]{1,0:T(8,128)(2,1)S(1)}, u32[]{:S(2)}, u32[]{:S(2)}) %collective-permute-start.28) | collective-permute-done | bytes 262176 | tf_op jit(solution)/shard_map/ppermute | solution.py:470
  148.5 1.5 shard_map.77.refs_4_
  150.0 1.9 %collective-permute-done.23.refs_1_ = bf16[512,256]{1,0:T(8,128)(2,1)S(1)} collective-permute-done((bf16[512,256]{1,0:T(8,128)(2,1)S(1)}, bf16[512,256]{1,0:T(8,128)(2,1)S(1)}, u32[]{:S(2)}, u32[]{:S(2)}) %collective-permute-start.23) | collective-permute-done | bytes 262176 | tf_op jit(solution)/shard_map/ppermute | solution.py:470
  151.9 4.7 %collective-permute-done.24.refs_2_ = bf16[512,256]{1,0:T(8,128)(2,1)S(1)} collective-permute-done((bf16[512,256]{1,0:T(8,128)(2,1)S(1)}, bf16[512,256]{1,0:T(8,128)(2,1)S(1)}, u32[]{:S(2)}, u32[]{:S(2)}) %collective-permute-start.24) | collective-permute-done | bytes 262176 | tf_op jit(solution)/shard_map/ppermute | solution.py:470
  157.5 1.5 shard_map.78
  (47 shorter events, 13.0 us)
Async XLA Ops:
  0.1 0.8 copy-start.3
  0.9 0.7 copy-start.4
  1.6 8.3 %copy-start = (bf16[512,4096]{1,0:T(8,128)(2,1)S(1)}, bf16[512,4096]{1,0:T(8,128)(2,1)}, u32[]{:S(2)}) copy-start(bf16[512,4096]{1,0:T(8,128)(2,1)} %refs_5_.9) | copy-start | bytes 12582916
  1.6 8.3 %copy-start.1 = (bf16[512,4096]{1,0:T(8,128)(2,1)S(1)}, bf16[512,4096]{1,0:T(8,128)(2,1)}, u32[]{:S(2)}) copy-start(bf16[512,4096]{1,0:T(8,128)(2,1)} %refs_6_.9) | copy-start | bytes 12582916
  2.2 4.6 %collective-permute-start = (f32[8,768]{1,0:T(8,128)S(1)}, f32[8,768]{1,0:T(8,128)S(1)}, u32[]{:S(2)}, u32[]{:S(2)}) collective-permute-start(f32[8,768]{1,0:T(8,128)S(1)} %get-tuple-element.49), channel_id=1, source_target_pairs={{0,8},{8,16},{16,24},{24,0},{1,9},{9,17},{17,25},{25,1},{2,10},{10... | collective-permute-start | bytes 73736 | tf_op jit(solution)/shard_map/ppermute | solution.py:470
  3.8 4.7 %collective-permute-start.1 = (f32[8,768]{1,0:T(8,128)S(1)}, f32[8,768]{1,0:T(8,128)S(1)}, u32[]{:S(2)}, u32[]{:S(2)}) collective-permute-start(f32[8,768]{1,0:T(8,128)S(1)} %get-tuple-element.50), channel_id=1, source_target_pairs={{0,16},{8,24},{16,0},{24,8},{1,17},{9,25},{17,1},{25,9},{2,18},{10... | collective-permute-start | bytes 73736 | tf_op jit(solution)/shard_map/ppermute | solution.py:470
  5.0 3.8 %collective-permute-start.2 = (f32[8,768]{1,0:T(8,128)S(1)}, f32[8,768]{1,0:T(8,128)S(1)}, u32[]{:S(2)}, u32[]{:S(2)}) collective-permute-start(f32[8,768]{1,0:T(8,128)S(1)} %get-tuple-element.51), channel_id=1, source_target_pairs={{0,24},{8,0},{16,8},{24,16},{1,25},{9,1},{17,9},{25,17},{2,26},{10... | collective-permute-start | bytes 73736 | tf_op jit(solution)/shard_map/ppermute | solution.py:470
  12.7 6.1 %collective-permute-start.4 = (bf16[6,128,128]{2,1,0:T(8,128)(2,1)S(1)}, bf16[6,128,128]{2,1,0:T(8,128)(2,1)S(1)}, u32[]{:S(2)}, u32[]{:S(2)}) collective-permute-start(bf16[6,128,128]{2,1,0:T(8,128)(2,1)S(1)} %get-tuple-element.58), channel_id=1, source_target_pairs={{0,8},{8,0},{16,24},{24,16},{1,9},{9,1},{17,25},{25,17},{2,10},{10... | collective-permute-start | bytes 589832 | tf_op jit(solution)/shard_map/ppermute | solution.py:473
  19.4 37.8 %copy-start.2 = (bf16[512,4096]{1,0:T(8,128)(2,1)S(1)}, bf16[512,4096]{1,0:T(8,128)(2,1)}, u32[]{:S(2)}) copy-start(bf16[512,4096]{1,0:T(8,128)(2,1)} %refs_4_.9) | copy-start | bytes 12582916
  19.4 9.0 %collective-permute-start.5 = (bf16[6,128,128]{2,1,0:T(8,128)(2,1)S(1)}, bf16[6,128,128]{2,1,0:T(8,128)(2,1)S(1)}, u32[]{:S(2)}, u32[]{:S(2)}) collective-permute-start(bf16[6,128,128]{2,1,0:T(8,128)(2,1)S(1)} %shard_map.59.refs_0_.refs_5_), channel_id=1, source_target_pairs={{0,16},{8,24},{16,0},{24,8},{1,17},{9,25},{17,1},{25,9},{2,18},{10... | collective-permute-start | bytes 589832 | tf_op jit(solution)/shard_map/ppermute | solution.py:473
  22.6 10.2 %collective-permute-start.3 = (bf16[10,128,128]{2,1,0:T(8,128)(2,1)S(1)}, bf16[10,128,128]{2,1,0:T(8,128)(2,1)S(1)}, u32[]{:S(2)}, u32[]{:S(2)}) collective-permute-start(bf16[10,128,128]{2,1,0:T(8,128)(2,1)S(1)} %get-tuple-element.56), channel_id=1, source_target_pairs={{0,8},{8,0},{16,24},{24,16},{1,9},{9,1},{17,25},{25,17},{2,10},{10... | collective-permute-start | bytes 983048 | tf_op jit(solution)/shard_map/ppermute | solution.py:473
  29.1 5.9 %collective-permute-start.7 = (bf16[6,144,128]{2,1,0:T(8,128)(2,1)S(1)}, bf16[6,144,128]{2,1,0:T(8,128)(2,1)S(1)}, u32[]{:S(2)}, u32[]{:S(2)}) collective-permute-start(bf16[6,144,128]{2,1,0:T(8,128)(2,1)S(1)} %shard_map.60.refs_3_.refs_0_), channel_id=1, source_target_pairs={{0,1},{1,0},{2,3},{3,2},{4,5},{5,4},{6,7},{7,6},{8,9},{9,8},{10,11... | collective-permute-start | bytes 663560 | tf_op jit(solution)/shard_map/ppermute | solution.py:473
  33.6 14.0 %collective-permute-start.6 = (bf16[10,128,128]{2,1,0:T(8,128)(2,1)S(1)}, bf16[10,128,128]{2,1,0:T(8,128)(2,1)S(1)}, u32[]{:S(2)}, u32[]{:S(2)}) collective-permute-start(bf16[10,128,128]{2,1,0:T(8,128)(2,1)S(1)} %shard_map.61.refs_2_.refs_0_.refs_5_), channel_id=1, source_target_pairs={{0,16},{8,24},{16,0},{24,8},{1,17},{9,25},{17,1},{25,9},{2,18},{10... | collective-permute-start | bytes 983048 | tf_op jit(solution)/shard_map/ppermute | solution.py:473
  35.7 6.0 %collective-permute-start.8 = (bf16[6,144,128]{2,1,0:T(8,128)(2,1)S(1)}, bf16[6,144,128]{2,1,0:T(8,128)(2,1)S(1)}, u32[]{:S(2)}, u32[]{:S(2)}) collective-permute-start(bf16[6,144,128]{2,1,0:T(8,128)(2,1)S(1)} %get-tuple-element.59.refs_0_), channel_id=1, source_target_pairs={{0,2},{1,3},{2,0},{3,1},{4,6},{5,7},{6,4},{7,5},{8,10},{9,11},{10,... | collective-permute-start | bytes 663560 | tf_op jit(solution)/shard_map/ppermute | solution.py:473
  42.4 6.0 %collective-permute-start.10 = (bf16[6,144,128]{2,1,0:T(8,128)(2,1)S(1)}, bf16[6,144,128]{2,1,0:T(8,128)(2,1)S(1)}, u32[]{:S(2)}, u32[]{:S(2)}) collective-permute-start(bf16[6,144,128]{2,1,0:T(8,128)(2,1)S(1)} %get-tuple-element.62.refs_0_), channel_id=1, source_target_pairs={{0,4},{1,5},{2,6},{3,7},{4,0},{5,1},{6,2},{7,3},{8,12},{9,13},{10,... | collective-permute-start | bytes 663560 | tf_op jit(solution)/shard_map/ppermute | solution.py:473
  48.3 3.3 %collective-permute-start.9 = (bf16[10,144,128]{2,1,0:T(8,128)(2,1)S(1)}, bf16[10,144,128]{2,1,0:T(8,128)(2,1)S(1)}, u32[]{:S(2)}, u32[]{:S(2)}) collective-permute-start(bf16[10,144,128]{2,1,0:T(8,128)(2,1)S(1)} %shard_map.64.refs_8_.refs_0_), channel_id=1, source_target_pairs={{0,1},{1,0},{2,3},{3,2},{4,5},{5,4},{6,7},{7,6},{8,9},{9,8},{10,11... | collective-permute-start | bytes 1105928 | tf_op jit(solution)/shard_map/ppermute | solution.py:473
  49.2 8.0 %collective-permute-start.12 = (bf16[6,128,128]{2,1,0:T(8,128)(2,1)S(1)}, bf16[6,128,128]{2,1,0:T(8,128)(2,1)S(1)}, u32[]{:S(2)}, u32[]{:S(2)}) collective-permute-start(bf16[6,128,128]{2,1,0:T(8,128)(2,1)S(1)} %get-tuple-element.66), channel_id=1, source_target_pairs={{0,8},{8,0},{16,24},{24,16},{1,9},{9,1},{17,25},{25,17},{2,10},{10... | collective-permute-start | bytes 589832 | tf_op jit(solution)/shard_map/ppermute | solution.py:473
  52.4 12.1 %collective-permute-start.11 = (bf16[10,144,128]{2,1,0:T(8,128)(2,1)S(1)}, bf16[10,144,128]{2,1,0:T(8,128)(2,1)S(1)}, u32[]{:S(2)}, u32[]{:S(2)}) collective-permute-start(bf16[10,144,128]{2,1,0:T(8,128)(2,1)S(1)} %get-tuple-element.64.refs_0_), channel_id=1, source_target_pairs={{0,2},{1,3},{2,0},{3,1},{4,6},{5,7},{6,4},{7,5},{8,10},{9,11},{10,... | collective-permute-start | bytes 1105928 | tf_op jit(solution)/shard_map/ppermute | solution.py:473
  59.7 10.6 %collective-permute-start.14 = (bf16[512,128]{1,0:T(8,128)(2,1)S(1)}, bf16[512,128]{1,0:T(8,128)(2,1)S(1)}, u32[]{:S(2)}, u32[]{:S(2)}) collective-permute-start(bf16[512,128]{1,0:T(8,128)(2,1)S(1)} %get-tuple-element.70), channel_id=1, source_target_pairs={{0,8},{8,16},{16,24},{24,0},{1,9},{9,17},{17,25},{25,1},{2,10},{10... | collective-permute-start | bytes 393224 | tf_op jit(solution)/shard_map/ppermute | solution.py:470
  61.3 13.7 %collective-permute-start.15 = (bf16[512,128]{1,0:T(8,128)(2,1)S(1)}, bf16[512,128]{1,0:T(8,128)(2,1)S(1)}, u32[]{:S(2)}, u32[]{:S(2)}) collective-permute-start(bf16[512,128]{1,0:T(8,128)(2,1)S(1)} %get-tuple-element.72), channel_id=1, source_target_pairs={{0,16},{8,24},{16,0},{24,8},{1,17},{9,25},{17,1},{25,9},{2,18},{10... | collective-permute-start | bytes 393224 | tf_op jit(solution)/shard_map/ppermute | solution.py:470
  63.9 11.2 %collective-permute-start.16 = (bf16[512,128]{1,0:T(8,128)(2,1)S(1)}, bf16[512,128]{1,0:T(8,128)(2,1)S(1)}, u32[]{:S(2)}, u32[]{:S(2)}) collective-permute-start(bf16[512,128]{1,0:T(8,128)(2,1)S(1)} %get-tuple-element.73), channel_id=1, source_target_pairs={{0,24},{8,0},{16,8},{24,16},{1,25},{9,1},{17,9},{25,17},{2,26},{10... | collective-permute-start | bytes 393224 | tf_op jit(solution)/shard_map/ppermute | solution.py:470
  65.4 9.7 %collective-permute-start.13 = (bf16[10,144,128]{2,1,0:T(8,128)(2,1)S(1)}, bf16[10,144,128]{2,1,0:T(8,128)(2,1)S(1)}, u32[]{:S(2)}, u32[]{:S(2)}) collective-permute-start(bf16[10,144,128]{2,1,0:T(8,128)(2,1)S(1)} %get-tuple-element.68.refs_0_), channel_id=1, source_target_pairs={{0,4},{1,5},{2,6},{3,7},{4,0},{5,1},{6,2},{7,3},{8,12},{9,13},{10,... | collective-permute-start | bytes 1105928 | tf_op jit(solution)/shard_map/ppermute | solution.py:473
  76.0 20.2 %collective-permute-start.17 = (bf16[10,128,128]{2,1,0:T(8,128)(2,1)S(1)}, bf16[10,128,128]{2,1,0:T(8,128)(2,1)S(1)}, u32[]{:S(2)}, u32[]{:S(2)}) collective-permute-start(bf16[10,128,128]{2,1,0:T(8,128)(2,1)S(1)} %get-tuple-element.75), channel_id=1, source_target_pairs={{0,8},{8,0},{16,24},{24,16},{1,9},{9,1},{17,25},{25,17},{2,10},{10... | collective-permute-start | bytes 983048 | tf_op jit(solution)/shard_map/ppermute | solution.py:473
  77.2 15.2 %collective-permute-start.18 = (bf16[512,256]{1,0:T(8,128)(2,1)S(1)}, bf16[512,256]{1,0:T(8,128)(2,1)S(1)}, u32[]{:S(2)}, u32[]{:S(2)}) collective-permute-start(bf16[512,256]{1,0:T(8,128)(2,1)S(1)} %get-tuple-element.76), channel_id=1, source_target_pairs={{0,8},{8,16},{16,24},{24,0},{1,9},{9,17},{17,25},{25,1},{2,10},{10... | collective-permute-start | bytes 786440 | tf_op jit(solution)/shard_map/ppermute | solution.py:470
  78.8 24.9 %collective-permute-start.19 = (bf16[512,256]{1,0:T(8,128)(2,1)S(1)}, bf16[512,256]{1,0:T(8,128)(2,1)S(1)}, u32[]{:S(2)}, u32[]{:S(2)}) collective-permute-start(bf16[512,256]{1,0:T(8,128)(2,1)S(1)} %get-tuple-element.78), channel_id=1, source_target_pairs={{0,16},{8,24},{16,0},{24,8},{1,17},{9,25},{17,1},{25,9},{2,18},{10... | collective-permute-start | bytes 786440 | tf_op jit(solution)/shard_map/ppermute | solution.py:470
  80.5 27.6 %collective-permute-start.20 = (bf16[512,256]{1,0:T(8,128)(2,1)S(1)}, bf16[512,256]{1,0:T(8,128)(2,1)S(1)}, u32[]{:S(2)}, u32[]{:S(2)}) collective-permute-start(bf16[512,256]{1,0:T(8,128)(2,1)S(1)} %get-tuple-element.79), channel_id=1, source_target_pairs={{0,24},{8,0},{16,8},{24,16},{1,25},{9,1},{17,9},{25,17},{2,26},{10... | collective-permute-start | bytes 786440 | tf_op jit(solution)/shard_map/ppermute | solution.py:470
  98.8 14.1 %collective-permute-start.21 = (bf16[512,128]{1,0:T(8,128)(2,1)S(1)}, bf16[512,128]{1,0:T(8,128)(2,1)S(1)}, u32[]{:S(2)}, u32[]{:S(2)}) collective-permute-start(bf16[512,128]{1,0:T(8,128)(2,1)S(1)} %get-tuple-element.81), channel_id=1, source_target_pairs={{0,8},{8,16},{16,24},{24,0},{1,9},{9,17},{17,25},{25,1},{2,10},{10... | collective-permute-start | bytes 393224 | tf_op jit(solution)/shard_map/ppermute | solution.py:470
  98.9 22.4 %collective-permute-start.22 = (bf16[512,128]{1,0:T(8,128)(2,1)S(1)}, bf16[512,128]{1,0:T(8,128)(2,1)S(1)}, u32[]{:S(2)}, u32[]{:S(2)}) collective-permute-start(bf16[512,128]{1,0:T(8,128)(2,1)S(1)} %get-tuple-element.82), channel_id=1, source_target_pairs={{0,24},{8,0},{16,8},{24,16},{1,25},{9,1},{17,9},{25,17},{2,26},{10... | collective-permute-start | bytes 393224 | tf_op jit(solution)/shard_map/ppermute | solution.py:470
  101.4 24.7 %collective-permute-start.29 = (bf16[512,128]{1,0:T(8,128)(2,1)S(1)}, bf16[512,128]{1,0:T(8,128)(2,1)S(1)}, u32[]{:S(2)}, u32[]{:S(2)}) collective-permute-start(bf16[512,128]{1,0:T(8,128)(2,1)S(1)} %get-tuple-element.90), channel_id=1, source_target_pairs={{0,16},{8,24},{16,0},{24,8},{1,17},{9,25},{17,1},{25,9},{2,18},{10... | collective-permute-start | bytes 393224 | tf_op jit(solution)/shard_map/ppermute | solution.py:470
  112.7 20.7 %collective-permute-start.26 = (bf16[512,256]{1,0:T(8,128)(2,1)S(1)}, bf16[512,256]{1,0:T(8,128)(2,1)S(1)}, u32[]{:S(2)}, u32[]{:S(2)}) collective-permute-start(bf16[512,256]{1,0:T(8,128)(2,1)S(1)} %get-tuple-element.87), channel_id=1, source_target_pairs={{0,8},{8,16},{16,24},{24,0},{1,9},{9,17},{17,25},{25,1},{2,10},{10... | collective-permute-start | bytes 786440 | tf_op jit(solution)/shard_map/ppermute | solution.py:470
  112.8 33.5 %collective-permute-start.27 = (bf16[512,256]{1,0:T(8,128)(2,1)S(1)}, bf16[512,256]{1,0:T(8,128)(2,1)S(1)}, u32[]{:S(2)}, u32[]{:S(2)}) collective-permute-start(bf16[512,256]{1,0:T(8,128)(2,1)S(1)} %get-tuple-element.88), channel_id=1, source_target_pairs={{0,16},{8,24},{16,0},{24,8},{1,17},{9,25},{17,1},{25,9},{2,18},{10... | collective-permute-start | bytes 786440 | tf_op jit(solution)/shard_map/ppermute | solution.py:470
  112.9 35.6 %collective-permute-start.28 = (bf16[512,256]{1,0:T(8,128)(2,1)S(1)}, bf16[512,256]{1,0:T(8,128)(2,1)S(1)}, u32[]{:S(2)}, u32[]{:S(2)}) collective-permute-start(bf16[512,256]{1,0:T(8,128)(2,1)S(1)} %get-tuple-element.89), channel_id=1, source_target_pairs={{0,24},{8,0},{16,8},{24,16},{1,25},{9,1},{17,9},{25,17},{2,26},{10... | collective-permute-start | bytes 786440 | tf_op jit(solution)/shard_map/ppermute | solution.py:470
  126.0 25.9 %collective-permute-start.23 = (bf16[512,256]{1,0:T(8,128)(2,1)S(1)}, bf16[512,256]{1,0:T(8,128)(2,1)S(1)}, u32[]{:S(2)}, u32[]{:S(2)}) collective-permute-start(bf16[512,256]{1,0:T(8,128)(2,1)S(1)} %get-tuple-element.84), channel_id=1, source_target_pairs={{0,8},{8,16},{16,24},{24,0},{1,9},{9,17},{17,25},{25,1},{2,10},{10... | collective-permute-start | bytes 786440 | tf_op jit(solution)/shard_map/ppermute | solution.py:470
  126.1 30.5 %collective-permute-start.24 = (bf16[512,256]{1,0:T(8,128)(2,1)S(1)}, bf16[512,256]{1,0:T(8,128)(2,1)S(1)}, u32[]{:S(2)}, u32[]{:S(2)}) collective-permute-start(bf16[512,256]{1,0:T(8,128)(2,1)S(1)} %get-tuple-element.85), channel_id=1, source_target_pairs={{0,16},{8,24},{16,0},{24,8},{1,17},{9,25},{17,1},{25,9},{2,18},{10... | collective-permute-start | bytes 786440 | tf_op jit(solution)/shard_map/ppermute | solution.py:470
  133.4 24.1 %collective-permute-start.25 = (bf16[512,256]{1,0:T(8,128)(2,1)S(1)}, bf16[512,256]{1,0:T(8,128)(2,1)S(1)}, u32[]{:S(2)}, u32[]{:S(2)}) collective-permute-start(bf16[512,256]{1,0:T(8,128)(2,1)S(1)} %get-tuple-element.86), channel_id=1, source_target_pairs={{0,24},{8,0},{16,8},{24,16},{1,25},{9,1},{17,9},{25,17},{2,26},{10... | collective-permute-start | bytes 786440 | tf_op jit(solution)/shard_map/ppermute | solution.py:470

commit v4 on v3

--- a/solution.py
+++ b/solution.py
@@ -201,17 +201,29 @@
     )
 
 
-def put_log(ref, i, log):
+def add_log(rows, i, log):
     high = log.astype(BF16).astype(F32)
     middle = (log - high).astype(BF16).astype(F32)
     low = log - high - middle
-    row = lax.broadcasted_iota(jnp.int32, (16, 128), 0)
-    rows = jnp.where(row == 0, high, jnp.where(row == 1, middle, jnp.where(row == 2, low, 0.0)))
-    ref[(*i, pl.ds(ref.shape[-2] - 16, 16))] = rows.astype(BF16)
-
-
-def get_log(ref, i):
-    return jnp.sum(ref[(*i, pl.ds(ref.shape[-2] - 16, 16))].astype(F32), axis=0, keepdims=True)
+    at = lax.broadcasted_iota(jnp.int32, rows.shape, 0)
+    for n, part in enumerate((high, middle, low)):
+        rows = jnp.where(at == 3 * i + n, part, rows)
+    return rows
+
+
+def log_rows(n):
+    return -(-3 * n // 16) * 16
+
+
+def get_log(ref, i, count):
+    rows = ref[pl.ds(count * 128, ref.shape[0] - count * 128), :].astype(F32)
+    at = lax.broadcasted_iota(jnp.int32, rows.shape, 0)
+    mine = (at >= 3 * i) & (at < 3 * i + 3)
+    return jnp.sum(jnp.where(mine, rows, 0.0), axis=0, keepdims=True)
+
+
+def get_state(ref, i):
+    return ref[pl.ds(i * 128, 128), :].astype(F32)
 
 
 def state_of(key, value, row, end):
@@ -255,19 +267,22 @@
 def block_states(head_of, z_ref, pair_ref, got_ref, totals_ref, out_ref):
     z = z_ref[0]
     upper = z >= 2
-    for i in range(out_ref.shape[0]):
+    count = out_ref.shape[0] // 128
+    logs = jnp.zeros((log_rows(count), 128), F32)
+    for i in range(count):
         totals = totals_ref[head_of(i, z, 0)]
         mine, got = pair_ref[i].astype(F32), got_ref[i].astype(F32)
         decay = jnp.exp(pick(totals, 2) + pick(totals, 3))
         state = decay * jnp.where(upper, got, mine) + jnp.where(upper, mine, got)
-        out_ref[i, :128, :] = state.astype(BF16)
-        put_log(out_ref, (i,), jnp.sum(totals, axis=0, keepdims=True))
-
-
-def scan_step(bit, s_ref, i, own_ref, got_ref, before, before_log):
+        out_ref[i * 128 : (i + 1) * 128, :] = state.astype(BF16)
+        logs = add_log(logs, i, jnp.sum(totals, axis=0, keepdims=True))
+    out_ref[count * 128 :, :] = logs.astype(BF16)
+
+
+def scan_step(bit, s_ref, i, count, own_ref, got_ref, before, before_log):
     upper = (s_ref[1] >> bit) & 1 == 1
-    own, got = own_ref[i, :128, :].astype(F32), got_ref[i, :128, :].astype(F32)
-    own_log, got_log = get_log(own_ref, (i,)), get_log(got_ref, (i,))
+    own, got = get_state(own_ref, i), get_state(got_ref, i)
+    own_log, got_log = get_log(own_ref, i, count), get_log(got_ref, i, count)
     if before is None:
         after = jnp.where(upper, got, 0.0)
         after_log = jnp.where(upper, got_log, 0.0)
@@ -281,26 +296,29 @@
 def scan_blocks(bit, s_ref, own_ref, got_ref, *refs):
     before_ref = refs[0] if bit else None
     after_ref, total_ref = refs[-2:]
-    for i in range(own_ref.shape[0]):
+    count = after_ref.shape[0]
+    logs = jnp.zeros((log_rows(count), 128), F32)
+    for i in range(count):
         before = before_ref[i, :128, :] if bit else None
         before_log = before_ref[i, 128:129, :] if bit else None
-        after, after_log, total, total_log = scan_step(bit, s_ref, i, own_ref, got_ref, before, before_log)
+        after, after_log, total, total_log = scan_step(bit, s_ref, i, count, own_ref, got_ref, before, before_log)
         after_ref[i, :128, :] = after
         after_ref[i, 128:, :] = jnp.broadcast_to(after_log, (8, 128))
-        total_ref[i, :128, :] = total.astype(BF16)
-        put_log(total_ref, (i,), total_log)
+        total_ref[i * 128 : (i + 1) * 128, :] = total.astype(BF16)
+        logs = add_log(logs, i, total_log)
+    total_ref[count * 128 :, :] = logs.astype(BF16)
 
 
 def entering_states(first, heads, done, bit, s_ref, own_ref, got_ref, before_ref, keep_ref, keep_got_ref, pair_ref, pair_got_ref, totals_ref, *outs):
     z = s_ref[0]
     odd, upper = lax.rem(z, 2) == 1, z >= 2
-    count = own_ref.shape[0]
+    count = before_ref.shape[0]
     m = count // 2
 
     def parts_of(i, head):
         totals = totals_ref[head]
         state = scan_step(
-            bit, s_ref, i, own_ref, got_ref, before_ref[i, :128, :], before_ref[i, 128:129, :]
+            bit, s_ref, i, count, own_ref, got_ref, before_ref[i, :128, :], before_ref[i, 128:129, :]
         )[0]
         low = jnp.where(upper, pair_got_ref[i], pair_ref[i]).astype(F32)
         even_part = jnp.where(odd, keep_got_ref[i], keep_ref[i]).astype(F32)
@@ -510,7 +528,7 @@
         pair, = call(functools.partial(pair_states, head_of), [keep, got, totals], [shape(n + done, 128, 128)])
         pair_got = swap(pair, "grp", 2)
         yield
-        total, = call(functools.partial(block_states, head_of), [pair, pair_got, totals], [shape(n, 144, 128)])
+        total, = call(functools.partial(block_states, head_of), [pair, pair_got, totals], [shape(n * 128 + log_rows(n), 128)])
         before = []
         bits = blocks.bit_length() - 1
         for bit in range(bits - 1):
@@ -518,7 +536,7 @@
             yield
             after, total = call(
                 functools.partial(scan_blocks, bit), [total, other, *before],
-                [shape(n, 136, 128, dtype=F32), shape(n, 144, 128)],
+                [shape(n, 136, 128, dtype=F32), shape(n * 128 + log_rows(n), 128)],
             )
             before = [after]
         other = swap(total, "seq", 1 << (bits - 1))

time: 159 us -> 159 us (level)
  no operation moved by 1% of the time
where the time goes in v4:
time: 159 us
  waiting for transfers between devices  78 us (49%)
  Pallas kernels  42.5 us (27%)
  starting transfers between devices  36.7 us (23%)
    ppermute x18, waiting for transfers between devices, shift(): return lax.ppermute(x, 'grp', [(i, (i + k) % parts) for i in range(parts)])  52.3 us
    pallas_call x24, Pallas kernels, __call__(): pl.pallas_call(body, out_shape=outs, in_specs=[pl.BlockSpec(memory_space=...  42.5 us
    ppermute x12, waiting for transfers between devices, swap(): lax.ppermute(x, axis, [(i, i ^ bit) for i in range(lax.axis_size(axis))])  25.7 us
    ppermute x18, starting transfers between devices, shift(): return lax.ppermute(x, 'grp', [(i, (i + k) % parts) for i in range(parts)])  22.2 us
    ppermute x12, starting transfers between devices, swap(): lax.ppermute(x, axis, [(i, i ^ bit) for i in range(lax.axis_size(axis))])  14.5 us
  transfers between devices with their start and end apart: 30, of which 18 were waited for; matrix products, arithmetic and copies ran while one was open for 0% of the time, Pallas kernels for 22%

profile of v4, /device:TPU:10, one launch (start us, length us, event | category | flops | bytes accessed | tf_op | source)
XLA Modules:
  0.0 159.2 jit_solution(14975311984786804970)
XLA Ops:
  2.2 1.6 collective-permute-start
  3.8 1.2 collective-permute-start.1
  5.0 1.8 %collective-permute-start.2 = (f32[8,768]{1,0:T(8,128)S(1)}, f32[8,768]{1,0:T(8,128)S(1)}, u32[]{:S(2)}, u32[]{:S(2)}) collective-permute-start(f32[8,768]{1,0:T(8,128)S(1)} %get-tuple-element.51), channel_id=1, source_target_pairs={{0,24},{8,0},{16,8},{24,16},{1,25},{9,1},{17,9},{25,17},{2,26},{10... | collective-permute-start | bytes 73736 | tf_op jit(solution)/shard_map/ppermute | solution.py:488
  6.8 1.7 %collective-permute-done.1.refs_2_ = f32[8,768]{1,0:T(8,128)S(1)} collective-permute-done((f32[8,768]{1,0:T(8,128)S(1)}, f32[8,768]{1,0:T(8,128)S(1)}, u32[]{:S(2)}, u32[]{:S(2)}) %collective-permute-start.1) | collective-permute-done | bytes 24608 | tf_op jit(solution)/shard_map/ppermute | solution.py:488
  8.9 1.0 shard_map.56
  9.9 2.7 %shard_map.57 = (bf16[6,128,128]{2,1,0:T(8,128)(2,1)S(1)}, bf16[6,128,128]{2,1,0:T(8,128)(2,1)S(1)}) custom-call(s32[2]{0:T(128)S(1)} %pad_add_fusion.s_ref, f32[32,512]{1,0:T(8,128)S(1)} %get-tuple-element.52.refs_0_, bf16[512,4096]{1,0:T(8,128)(2,1)S(1)} %copy-done, bf16[512,4096]{1,0:T(8,128)(2,1)S(1)} %copy-done.1), custom_call_target="tpu_custom_call" | custom-call | flops 3000000000 | bytes 1000 | tf_op jit(solution)/shard_map/pallas_call | solution.py:126
  12.7 1.9 %collective-permute-start.4 = (bf16[6,128,128]{2,1,0:T(8,128)(2,1)S(1)}, bf16[6,128,128]{2,1,0:T(8,128)(2,1)S(1)}, u32[]{:S(2)}, u32[]{:S(2)}) collective-permute-start(bf16[6,128,128]{2,1,0:T(8,128)(2,1)S(1)} %get-tuple-element.58), channel_id=1, source_target_pairs={{0,8},{8,0},{16,24},{24,16},{1,9},{9,1},{17,25},{25,17},{2,10},{10... | collective-permute-start | bytes 589832 | tf_op jit(solution)/shard_map/ppermute | solution.py:491
  14.5 4.2 %shard_map.58 = (bf16[10,128,128]{2,1,0:T(8,128)(2,1)S(1)}, bf16[10,128,128]{2,1,0:T(8,128)(2,1)S(1)}) custom-call(s32[2]{0:T(128)S(1)} %pad_add_fusion.s_ref, f32[32,512]{1,0:T(8,128)S(1)} %get-tuple-element.52.refs_0_, bf16[512,4096]{1,0:T(8,128)(2,1)S(1)} %copy-done, bf16[512,4096]{1,0:T(8,128)(2,1)S(1)} %copy-done.1, ...), custom_call_target="tpu_custom_call" | custom-call | flops 5000000000 | bytes 1000 | tf_op jit(solution)/shard_map/pallas_call | solution.py:126
  19.4 3.2 %collective-permute-start.5 = (bf16[6,128,128]{2,1,0:T(8,128)(2,1)S(1)}, bf16[6,128,128]{2,1,0:T(8,128)(2,1)S(1)}, u32[]{:S(2)}, u32[]{:S(2)}) collective-permute-start(bf16[6,128,128]{2,1,0:T(8,128)(2,1)S(1)} %shard_map.59.refs_0_.refs_5_), channel_id=1, source_target_pairs={{0,16},{8,24},{16,0},{24,8},{1,17},{9,25},{17,1},{25,9},{2,18},{10... | collective-permute-start | bytes 589832 | tf_op jit(solution)/shard_map/ppermute | solution.py:491
  23.2 5.3 %collective-permute-done.5.refs_1_.refs_6_ = bf16[6,128,128]{2,1,0:T(8,128)(2,1)S(1)} collective-permute-done((bf16[6,128,128]{2,1,0:T(8,128)(2,1)S(1)}, bf16[6,128,128]{2,1,0:T(8,128)(2,1)S(1)}, u32[]{:S(2)}, u32[]{:S(2)}) %collective-permute-start.5) | collective-permute-done | bytes 196640 | tf_op jit(solution)/shard_map/ppermute | solution.py:491
  29.2 3.7 %collective-permute-done.3.refs_1_.refs_4_ = bf16[10,128,128]{2,1,0:T(8,128)(2,1)S(1)} collective-permute-done((bf16[10,128,128]{2,1,0:T(8,128)(2,1)S(1)}, bf16[10,128,128]{2,1,0:T(8,128)(2,1)S(1)}, u32[]{:S(2)}, u32[]{:S(2)}) %collective-permute-start.3) | collective-permute-done | bytes 327712 | tf_op jit(solution)/shard_map/ppermute | solution.py:491
  33.6 1.4 collective-permute-start.6
  36.3 5.2 %collective-permute-done.8.refs_1_ = bf16[800,128]{1,0:T(8,128)(2,1)S(1)} collective-permute-done((bf16[800,128]{1,0:T(8,128)(2,1)S(1)}, bf16[800,128]{1,0:T(8,128)(2,1)S(1)}, u32[]{:S(2)}, u32[]{:S(2)}) %collective-permute-start.8) | collective-permute-done | bytes 204832 | tf_op jit(solution)/shard_map/ppermute | solution.py:491
  42.2 1.6 collective-permute-start.10
  43.8 3.7 %collective-permute-done.6.refs_1_.refs_6_ = bf16[10,128,128]{2,1,0:T(8,128)(2,1)S(1)} collective-permute-done((bf16[10,128,128]{2,1,0:T(8,128)(2,1)S(1)}, bf16[10,128,128]{2,1,0:T(8,128)(2,1)S(1)}, u32[]{:S(2)}, u32[]{:S(2)}) %collective-permute-start.6) | collective-permute-done | bytes 327712 | tf_op jit(solution)/shard_map/ppermute | solution.py:491
  49.2 2.5 %collective-permute-start.12 = (bf16[6,128,128]{2,1,0:T(8,128)(2,1)S(1)}, bf16[6,128,128]{2,1,0:T(8,128)(2,1)S(1)}, u32[]{:S(2)}, u32[]{:S(2)}) collective-permute-start(bf16[6,128,128]{2,1,0:T(8,128)(2,1)S(1)} %get-tuple-element.66), channel_id=1, source_target_pairs={{0,8},{8,0},{16,24},{24,16},{1,9},{9,1},{17,25},{25,17},{2,10},{10... | collective-permute-start | bytes 589832 | tf_op jit(solution)/shard_map/ppermute | solution.py:491
  53.0 4.2 %collective-permute-done.12.refs_3_ = bf16[6,128,128]{2,1,0:T(8,128)(2,1)S(1)} collective-permute-done((bf16[6,128,128]{2,1,0:T(8,128)(2,1)S(1)}, bf16[6,128,128]{2,1,0:T(8,128)(2,1)S(1)}, u32[]{:S(2)}, u32[]{:S(2)}) %collective-permute-start.12) | collective-permute-done | bytes 196640 | tf_op jit(solution)/shard_map/ppermute | solution.py:491
  57.2 2.5 %shard_map.67 = (bf16[512,128]{1,0:T(8,128)(2,1)S(1)}, bf16[512,128]{1,0:T(8,128)(2,1)S(1)}, bf16[512,128]{1,0:T(8,128)(2,1)S(1)}, bf16[512,128]{1,0:T(8,128)(2,1)S(1)}) custom-call(s32[2]{0:T(128)S(1)} %pad_add_fusion.s_ref, f32[32,512]{1,0:T(8,128)S(1)} %get-tuple-element.52.refs_0_, f32[32,128]{1,0:T(8,128)S(1)} %get-tuple-element.53.refs_1_, ...), custom_call_target="tpu_custom_call" | custom-call | flops 2500000000 | bytes 1000 | tf_op jit(solution)/shard_map/pallas_call | solution.py:126
  59.7 1.6 collective-permute-start.14
  61.3 2.6 %collective-permute-start.15 = (bf16[512,128]{1,0:T(8,128)(2,1)S(1)}, bf16[512,128]{1,0:T(8,128)(2,1)S(1)}, u32[]{:S(2)}, u32[]{:S(2)}) collective-permute-start(bf16[512,128]{1,0:T(8,128)(2,1)S(1)} %get-tuple-element.72), channel_id=1, source_target_pairs={{0,16},{8,24},{16,0},{24,8},{1,17},{9,25},{17,1},{25,9},{2,18},{10... | collective-permute-start | bytes 393224 | tf_op jit(solution)/shard_map/ppermute | solution.py:488
  65.4 1.6 %collective-permute-start.13 = (bf16[1312,128]{1,0:T(8,128)(2,1)S(1)}, bf16[1312,128]{1,0:T(8,128)(2,1)S(1)}, u32[]{:S(2)}, u32[]{:S(2)}) collective-permute-start(bf16[1312,128]{1,0:T(8,128)(2,1)S(1)} %get-tuple-element.68.refs_0_), channel_id=1, source_target_pairs={{0,4},{1,5},{2,6},{3,7},{4,0},{5,1},{6,2},{7,3},{8,12},{9,13},{10,... | collective-permute-start | bytes 1007624 | tf_op jit(solution)/shard_map/ppermute | solution.py:491
  66.9 3.4 %collective-permute-done.14.refs_8_.refs_1_ = bf16[512,128]{1,0:T(8,128)(2,1)S(1)} collective-permute-done((bf16[512,128]{1,0:T(8,128)(2,1)S(1)}, bf16[512,128]{1,0:T(8,128)(2,1)S(1)}, u32[]{:S(2)}, u32[]{:S(2)}) %collective-permute-start.14) | collective-permute-done | bytes 131104 | tf_op jit(solution)/shard_map/ppermute | solution.py:488
  70.3 4.7 %shard_map.69 = (bf16[512,256]{1,0:T(8,128)(2,1)S(1)}, bf16[512,256]{1,0:T(8,128)(2,1)S(1)}, bf16[512,256]{1,0:T(8,128)(2,1)S(1)}, bf16[512,256]{1,0:T(8,128)(2,1)S(1)}) custom-call(s32[2]{0:T(128)S(1)} %pad_add_fusion.s_ref, f32[32,512]{1,0:T(8,128)S(1)} %get-tuple-element.52.refs_0_, f32[32,128]{1,0:T(8,128)S(1)} %get-tuple-element.53.refs_1_, ...), custom_call_target="tpu_custom_call" | custom-call | flops 5000000000 | bytes 1000 | tf_op jit(solution)/shard_map/pallas_call | solution.py:126
  75.1 0.9 shard_map.70
  76.5 2.3 %collective-permute-start.18 = (bf16[512,256]{1,0:T(8,128)(2,1)S(1)}, bf16[512,256]{1,0:T(8,128)(2,1)S(1)}, u32[]{:S(2)}, u32[]{:S(2)}) collective-permute-start(bf16[512,256]{1,0:T(8,128)(2,1)S(1)} %get-tuple-element.76), channel_id=1, source_target_pairs={{0,8},{8,16},{16,24},{24,0},{1,9},{9,17},{17,25},{25,1},{2,10},{10... | collective-permute-start | bytes 786440 | tf_op jit(solution)/shard_map/ppermute | solution.py:488
  78.8 1.7 %collective-permute-start.19 = (bf16[512,256]{1,0:T(8,128)(2,1)S(1)}, bf16[512,256]{1,0:T(8,128)(2,1)S(1)}, u32[]{:S(2)}, u32[]{:S(2)}) collective-permute-start(bf16[512,256]{1,0:T(8,128)(2,1)S(1)} %get-tuple-element.78), channel_id=1, source_target_pairs={{0,16},{8,24},{16,0},{24,8},{1,17},{9,25},{17,1},{25,9},{2,18},{10... | collective-permute-start | bytes 786440 | tf_op jit(solution)/shard_map/ppermute | solution.py:488
  80.4 1.7 %collective-permute-start.20 = (bf16[512,256]{1,0:T(8,128)(2,1)S(1)}, bf16[512,256]{1,0:T(8,128)(2,1)S(1)}, u32[]{:S(2)}, u32[]{:S(2)}) collective-permute-start(bf16[512,256]{1,0:T(8,128)(2,1)S(1)} %get-tuple-element.79), channel_id=1, source_target_pairs={{0,24},{8,0},{16,8},{24,16},{1,25},{9,1},{17,9},{25,17},{2,26},{10... | collective-permute-start | bytes 786440 | tf_op jit(solution)/shard_map/ppermute | solution.py:488
  82.2 10.1 %collective-permute-done.18.refs_7_.refs_1_ = bf16[512,256]{1,0:T(8,128)(2,1)S(1)} collective-permute-done((bf16[512,256]{1,0:T(8,128)(2,1)S(1)}, bf16[512,256]{1,0:T(8,128)(2,1)S(1)}, u32[]{:S(2)}, u32[]{:S(2)}) %collective-permute-start.18) | collective-permute-done | bytes 262176 | tf_op jit(solution)/shard_map/ppermute | solution.py:488
  92.3 3.5 %collective-permute-done.17.refs_3_ = bf16[10,128,128]{2,1,0:T(8,128)(2,1)S(1)} collective-permute-done((bf16[10,128,128]{2,1,0:T(8,128)(2,1)S(1)}, bf16[10,128,128]{2,1,0:T(8,128)(2,1)S(1)}, u32[]{:S(2)}, u32[]{:S(2)}) %collective-permute-start.17) | collective-permute-done | bytes 327712 | tf_op jit(solution)/shard_map/ppermute | solution.py:491
  95.9 2.5 %shard_map.71 = (bf16[512,128]{1,0:T(8,128)(2,1)S(1)}, bf16[512,128]{1,0:T(8,128)(2,1)S(1)}, bf16[512,128]{1,0:T(8,128)(2,1)S(1)}, bf16[512,128]{1,0:T(8,128)(2,1)S(1)}) custom-call(s32[2]{0:T(128)S(1)} %pad_add_fusion.s_ref, f32[32,512]{1,0:T(8,128)S(1)} %get-tuple-element.52.refs_0_, f32[32,128]{1,0:T(8,128)S(1)} %get-tuple-element.53.refs_1_, ...), custom_call_target="tpu_custom_call" | custom-call | flops 2500000000 | bytes 1000 | tf_op jit(solution)/shard_map/pallas_call | solution.py:126
  98.8 2.2 %collective-permute-start.22 = (bf16[512,128]{1,0:T(8,128)(2,1)S(1)}, bf16[512,128]{1,0:T(8,128)(2,1)S(1)}, u32[]{:S(2)}, u32[]{:S(2)}) collective-permute-start(bf16[512,128]{1,0:T(8,128)(2,1)S(1)} %get-tuple-element.82), channel_id=1, source_target_pairs={{0,24},{8,0},{16,8},{24,16},{1,25},{9,1},{17,9},{25,17},{2,26},{10... | collective-permute-start | bytes 393224 | tf_op jit(solution)/shard_map/ppermute | solution.py:488
  101.0 2.3 %collective-permute-start.29 = (bf16[512,128]{1,0:T(8,128)(2,1)S(1)}, bf16[512,128]{1,0:T(8,128)(2,1)S(1)}, u32[]{:S(2)}, u32[]{:S(2)}) collective-permute-start(bf16[512,128]{1,0:T(8,128)(2,1)S(1)} %get-tuple-element.90), channel_id=1, source_target_pairs={{0,16},{8,24},{16,0},{24,8},{1,17},{9,25},{17,1},{25,9},{2,18},{10... | collective-permute-start | bytes 393224 | tf_op jit(solution)/shard_map/ppermute | solution.py:488
  103.3 4.6 %collective-permute-done.20.refs_9_.refs_3_ = bf16[512,256]{1,0:T(8,128)(2,1)S(1)} collective-permute-done((bf16[512,256]{1,0:T(8,128)(2,1)S(1)}, bf16[512,256]{1,0:T(8,128)(2,1)S(1)}, u32[]{:S(2)}, u32[]{:S(2)}) %collective-permute-start.20) | collective-permute-done | bytes 262176 | tf_op jit(solution)/shard_map/ppermute | solution.py:488
  107.9 4.7 %shard_map.72 = (bf16[512,256]{1,0:T(8,128)(2,1)S(1)}, bf16[512,256]{1,0:T(8,128)(2,1)S(1)}, bf16[512,256]{1,0:T(8,128)(2,1)S(1)}, bf16[512,256]{1,0:T(8,128)(2,1)S(1)}) custom-call(s32[2]{0:T(128)S(1)} %pad_add_fusion.s_ref, f32[32,512]{1,0:T(8,128)S(1)} %get-tuple-element.52.refs_0_, f32[32,128]{1,0:T(8,128)S(1)} %get-tuple-element.53.refs_1_, ...), custom_call_target="tpu_custom_call" | custom-call | flops 5000000000 | bytes 1000 | tf_op jit(solution)/shard_map/pallas_call | solution.py:126
  112.8 1.9 %collective-permute-start.28 = (bf16[512,256]{1,0:T(8,128)(2,1)S(1)}, bf16[512,256]{1,0:T(8,128)(2,1)S(1)}, u32[]{:S(2)}, u32[]{:S(2)}) collective-permute-start(bf16[512,256]{1,0:T(8,128)(2,1)S(1)} %get-tuple-element.89), channel_id=1, source_target_pairs={{0,24},{8,0},{16,8},{24,16},{1,25},{9,1},{17,9},{25,17},{2,26},{10... | collective-permute-start | bytes 786440 | tf_op jit(solution)/shard_map/ppermute | solution.py:488
  114.7 7.0 %collective-permute-done.22.refs_9_.refs_3_ = bf16[512,128]{1,0:T(8,128)(2,1)S(1)} collective-permute-done((bf16[512,128]{1,0:T(8,128)(2,1)S(1)}, bf16[512,128]{1,0:T(8,128)(2,1)S(1)}, u32[]{:S(2)}, u32[]{:S(2)}) %collective-permute-start.22) | collective-permute-done | bytes 131104 | tf_op jit(solution)/shard_map/ppermute | solution.py:488
  121.7 4.7 %shard_map.73 = (bf16[512,256]{1,0:T(8,128)(2,1)S(1)}, bf16[512,256]{1,0:T(8,128)(2,1)S(1)}, bf16[512,256]{1,0:T(8,128)(2,1)S(1)}, bf16[512,256]{1,0:T(8,128)(2,1)S(1)}) custom-call(s32[2]{0:T(128)S(1)} %pad_add_fusion.s_ref, f32[32,512]{1,0:T(8,128)S(1)} %get-tuple-element.52.refs_0_, f32[32,128]{1,0:T(8,128)S(1)} %get-tuple-element.53.refs_1_, ...), custom_call_target="tpu_custom_call" | custom-call | flops 5000000000 | bytes 1000 | tf_op jit(solution)/shard_map/pallas_call | solution.py:126
  126.5 6.7 %collective-permute-done.26.refs_1_ = bf16[512,256]{1,0:T(8,128)(2,1)S(1)} collective-permute-done((bf16[512,256]{1,0:T(8,128)(2,1)S(1)}, bf16[512,256]{1,0:T(8,128)(2,1)S(1)}, u32[]{:S(2)}, u32[]{:S(2)}) %collective-permute-start.26) | collective-permute-done | bytes 262176 | tf_op jit(solution)/shard_map/ppermute | solution.py:488
  133.2 1.4 shard_map.74.refs_4_
  134.6 1.5 shard_map.75.refs_4_
  136.1 1.4 shard_map.76.refs_4_
  137.5 8.8 %collective-permute-done.27.refs_2_ = bf16[512,256]{1,0:T(8,128)(2,1)S(1)} collective-permute-done((bf16[512,256]{1,0:T(8,128)(2,1)S(1)}, bf16[512,256]{1,0:T(8,128)(2,1)S(1)}, u32[]{:S(2)}, u32[]{:S(2)}) %collective-permute-start.27) | collective-permute-done | bytes 262176 | tf_op jit(solution)/shard_map/ppermute | solution.py:488
  146.3 2.2 %collective-permute-done.28.refs_3_ = bf16[512,256]{1,0:T(8,128)(2,1)S(1)} collective-permute-done((bf16[512,256]{1,0:T(8,128)(2,1)S(1)}, bf16[512,256]{1,0:T(8,128)(2,1)S(1)}, u32[]{:S(2)}, u32[]{:S(2)}) %collective-permute-start.28) | collective-permute-done | bytes 262176 | tf_op jit(solution)/shard_map/ppermute | solution.py:488
  148.5 1.5 shard_map.77.refs_4_
  150.0 1.9 %collective-permute-done.23.refs_1_ = bf16[512,256]{1,0:T(8,128)(2,1)S(1)} collective-permute-done((bf16[512,256]{1,0:T(8,128)(2,1)S(1)}, bf16[512,256]{1,0:T(8,128)(2,1)S(1)}, u32[]{:S(2)}, u32[]{:S(2)}) %collective-permute-start.23) | collective-permute-done | bytes 262176 | tf_op jit(solution)/shard_map/ppermute | solution.py:488
  151.9 4.7 %collective-permute-done.24.refs_2_ = bf16[512,256]{1,0:T(8,128)(2,1)S(1)} collective-permute-done((bf16[512,256]{1,0:T(8,128)(2,1)S(1)}, bf16[512,256]{1,0:T(8,128)(2,1)S(1)}, u32[]{:S(2)}, u32[]{:S(2)}) %collective-permute-start.24) | collective-permute-done | bytes 262176 | tf_op jit(solution)/shard_map/ppermute | solution.py:488
  156.6 0.9 collective-permute-done.25.refs_3_
  157.5 1.5 shard_map.78
  (47 shorter events, 12.8 us)
Async XLA Ops:
  0.1 0.8 copy-start.3
  0.9 0.7 copy-start.4
  1.6 8.3 %copy-start = (bf16[512,4096]{1,0:T(8,128)(2,1)S(1)}, bf16[512,4096]{1,0:T(8,128)(2,1)}, u32[]{:S(2)}) copy-start(bf16[512,4096]{1,0:T(8,128)(2,1)} %refs_5_.9) | copy-start | bytes 12582916
  1.6 8.3 %copy-start.1 = (bf16[512,4096]{1,0:T(8,128)(2,1)S(1)}, bf16[512,4096]{1,0:T(8,128)(2,1)}, u32[]{:S(2)}) copy-start(bf16[512,4096]{1,0:T(8,128)(2,1)} %refs_6_.9) | copy-start | bytes 12582916
  2.2 4.6 %collective-permute-start = (f32[8,768]{1,0:T(8,128)S(1)}, f32[8,768]{1,0:T(8,128)S(1)}, u32[]{:S(2)}, u32[]{:S(2)}) collective-permute-start(f32[8,768]{1,0:T(8,128)S(1)} %get-tuple-element.49), channel_id=1, source_target_pairs={{0,8},{8,16},{16,24},{24,0},{1,9},{9,17},{17,25},{25,1},{2,10},{10... | collective-permute-start | bytes 73736 | tf_op jit(solution)/shard_map/ppermute | solution.py:488
  3.8 4.7 %collective-permute-start.1 = (f32[8,768]{1,0:T(8,128)S(1)}, f32[8,768]{1,0:T(8,128)S(1)}, u32[]{:S(2)}, u32[]{:S(2)}) collective-permute-start(f32[8,768]{1,0:T(8,128)S(1)} %get-tuple-element.50), channel_id=1, source_target_pairs={{0,16},{8,24},{16,0},{24,8},{1,17},{9,25},{17,1},{25,9},{2,18},{10... | collective-permute-start | bytes 73736 | tf_op jit(solution)/shard_map/ppermute | solution.py:488
  5.0 3.8 %collective-permute-start.2 = (f32[8,768]{1,0:T(8,128)S(1)}, f32[8,768]{1,0:T(8,128)S(1)}, u32[]{:S(2)}, u32[]{:S(2)}) collective-permute-start(f32[8,768]{1,0:T(8,128)S(1)} %get-tuple-element.51), channel_id=1, source_target_pairs={{0,24},{8,0},{16,8},{24,16},{1,25},{9,1},{17,9},{25,17},{2,26},{10... | collective-permute-start | bytes 73736 | tf_op jit(solution)/shard_map/ppermute | solution.py:488
  12.7 6.1 %collective-permute-start.4 = (bf16[6,128,128]{2,1,0:T(8,128)(2,1)S(1)}, bf16[6,128,128]{2,1,0:T(8,128)(2,1)S(1)}, u32[]{:S(2)}, u32[]{:S(2)}) collective-permute-start(bf16[6,128,128]{2,1,0:T(8,128)(2,1)S(1)} %get-tuple-element.58), channel_id=1, source_target_pairs={{0,8},{8,0},{16,24},{24,16},{1,9},{9,1},{17,25},{25,17},{2,10},{10... | collective-permute-start | bytes 589832 | tf_op jit(solution)/shard_map/ppermute | solution.py:491
  19.4 37.8 %copy-start.2 = (bf16[512,4096]{1,0:T(8,128)(2,1)S(1)}, bf16[512,4096]{1,0:T(8,128)(2,1)}, u32[]{:S(2)}) copy-start(bf16[512,4096]{1,0:T(8,128)(2,1)} %refs_4_.9) | copy-start | bytes 12582916
  19.4 9.0 %collective-permute-start.5 = (bf16[6,128,128]{2,1,0:T(8,128)(2,1)S(1)}, bf16[6,128,128]{2,1,0:T(8,128)(2,1)S(1)}, u32[]{:S(2)}, u32[]{:S(2)}) collective-permute-start(bf16[6,128,128]{2,1,0:T(8,128)(2,1)S(1)} %shard_map.59.refs_0_.refs_5_), channel_id=1, source_target_pairs={{0,16},{8,24},{16,0},{24,8},{1,17},{9,25},{17,1},{25,9},{2,18},{10... | collective-permute-start | bytes 589832 | tf_op jit(solution)/shard_map/ppermute | solution.py:491
  22.6 10.2 %collective-permute-start.3 = (bf16[10,128,128]{2,1,0:T(8,128)(2,1)S(1)}, bf16[10,128,128]{2,1,0:T(8,128)(2,1)S(1)}, u32[]{:S(2)}, u32[]{:S(2)}) collective-permute-start(bf16[10,128,128]{2,1,0:T(8,128)(2,1)S(1)} %get-tuple-element.56), channel_id=1, source_target_pairs={{0,8},{8,0},{16,24},{24,16},{1,9},{9,1},{17,25},{25,17},{2,10},{10... | collective-permute-start | bytes 983048 | tf_op jit(solution)/shard_map/ppermute | solution.py:491
  29.1 5.9 %collective-permute-start.7 = (bf16[800,128]{1,0:T(8,128)(2,1)S(1)}, bf16[800,128]{1,0:T(8,128)(2,1)S(1)}, u32[]{:S(2)}, u32[]{:S(2)}) collective-permute-start(bf16[800,128]{1,0:T(8,128)(2,1)S(1)} %shard_map.60.refs_3_.refs_0_), channel_id=1, source_target_pairs={{0,1},{1,0},{2,3},{3,2},{4,5},{5,4},{6,7},{7,6},{8,9},{9,8},{10,11... | collective-permute-start | bytes 614408 | tf_op jit(solution)/shard_map/ppermute | solution.py:491
  33.6 14.0 %collective-permute-start.6 = (bf16[10,128,128]{2,1,0:T(8,128)(2,1)S(1)}, bf16[10,128,128]{2,1,0:T(8,128)(2,1)S(1)}, u32[]{:S(2)}, u32[]{:S(2)}) collective-permute-start(bf16[10,128,128]{2,1,0:T(8,128)(2,1)S(1)} %shard_map.61.refs_2_.refs_0_.refs_5_), channel_id=1, source_target_pairs={{0,16},{8,24},{16,0},{24,8},{1,17},{9,25},{17,1},{25,9},{2,18},{10... | collective-permute-start | bytes 983048 | tf_op jit(solution)/shard_map/ppermute | solution.py:491
  35.7 5.8 %collective-permute-start.8 = (bf16[800,128]{1,0:T(8,128)(2,1)S(1)}, bf16[800,128]{1,0:T(8,128)(2,1)S(1)}, u32[]{:S(2)}, u32[]{:S(2)}) collective-permute-start(bf16[800,128]{1,0:T(8,128)(2,1)S(1)} %get-tuple-element.59.refs_0_), channel_id=1, source_target_pairs={{0,2},{1,3},{2,0},{3,1},{4,6},{5,7},{6,4},{7,5},{8,10},{9,11},{10,... | collective-permute-start | bytes 614408 | tf_op jit(solution)/shard_map/ppermute | solution.py:491
  42.2 6.2 %collective-permute-start.10 = (bf16[800,128]{1,0:T(8,128)(2,1)S(1)}, bf16[800,128]{1,0:T(8,128)(2,1)S(1)}, u32[]{:S(2)}, u32[]{:S(2)}) collective-permute-start(bf16[800,128]{1,0:T(8,128)(2,1)S(1)} %get-tuple-element.62.refs_0_), channel_id=1, source_target_pairs={{0,4},{1,5},{2,6},{3,7},{4,0},{5,1},{6,2},{7,3},{8,12},{9,13},{10,... | collective-permute-start | bytes 614408 | tf_op jit(solution)/shard_map/ppermute | solution.py:491
  48.3 3.4 %collective-permute-start.9 = (bf16[1312,128]{1,0:T(8,128)(2,1)S(1)}, bf16[1312,128]{1,0:T(8,128)(2,1)S(1)}, u32[]{:S(2)}, u32[]{:S(2)}) collective-permute-start(bf16[1312,128]{1,0:T(8,128)(2,1)S(1)} %shard_map.64.refs_8_.refs_0_), channel_id=1, source_target_pairs={{0,1},{1,0},{2,3},{3,2},{4,5},{5,4},{6,7},{7,6},{8,9},{9,8},{10,11... | collective-permute-start | bytes 1007624 | tf_op jit(solution)/shard_map/ppermute | solution.py:491
  49.2 8.0 %collective-permute-start.12 = (bf16[6,128,128]{2,1,0:T(8,128)(2,1)S(1)}, bf16[6,128,128]{2,1,0:T(8,128)(2,1)S(1)}, u32[]{:S(2)}, u32[]{:S(2)}) collective-permute-start(bf16[6,128,128]{2,1,0:T(8,128)(2,1)S(1)} %get-tuple-element.66), channel_id=1, source_target_pairs={{0,8},{8,0},{16,24},{24,16},{1,9},{9,1},{17,25},{25,17},{2,10},{10... | collective-permute-start | bytes 589832 | tf_op jit(solution)/shard_map/ppermute | solution.py:491
  52.4 12.1 %collective-permute-start.11 = (bf16[1312,128]{1,0:T(8,128)(2,1)S(1)}, bf16[1312,128]{1,0:T(8,128)(2,1)S(1)}, u32[]{:S(2)}, u32[]{:S(2)}) collective-permute-start(bf16[1312,128]{1,0:T(8,128)(2,1)S(1)} %get-tuple-element.64.refs_0_), channel_id=1, source_target_pairs={{0,2},{1,3},{2,0},{3,1},{4,6},{5,7},{6,4},{7,5},{8,10},{9,11},{10,... | collective-permute-start | bytes 1007624 | tf_op jit(solution)/shard_map/ppermute | solution.py:491
  59.7 10.6 %collective-permute-start.14 = (bf16[512,128]{1,0:T(8,128)(2,1)S(1)}, bf16[512,128]{1,0:T(8,128)(2,1)S(1)}, u32[]{:S(2)}, u32[]{:S(2)}) collective-permute-start(bf16[512,128]{1,0:T(8,128)(2,1)S(1)} %get-tuple-element.70), channel_id=1, source_target_pairs={{0,8},{8,16},{16,24},{24,0},{1,9},{9,17},{17,25},{25,1},{2,10},{10... | collective-permute-start | bytes 393224 | tf_op jit(solution)/shard_map/ppermute | solution.py:488
  61.3 13.7 %collective-permute-start.15 = (bf16[512,128]{1,0:T(8,128)(2,1)S(1)}, bf16[512,128]{1,0:T(8,128)(2,1)S(1)}, u32[]{:S(2)}, u32[]{:S(2)}) collective-permute-start(bf16[512,128]{1,0:T(8,128)(2,1)S(1)} %get-tuple-element.72), channel_id=1, source_target_pairs={{0,16},{8,24},{16,0},{24,8},{1,17},{9,25},{17,1},{25,9},{2,18},{10... | collective-permute-start | bytes 393224 | tf_op jit(solution)/shard_map/ppermute | solution.py:488
  63.9 11.1 %collective-permute-start.16 = (bf16[512,128]{1,0:T(8,128)(2,1)S(1)}, bf16[512,128]{1,0:T(8,128)(2,1)S(1)}, u32[]{:S(2)}, u32[]{:S(2)}) collective-permute-start(bf16[512,128]{1,0:T(8,128)(2,1)S(1)} %get-tuple-element.73), channel_id=1, source_target_pairs={{0,24},{8,0},{16,8},{24,16},{1,25},{9,1},{17,9},{25,17},{2,26},{10... | collective-permute-start | bytes 393224 | tf_op jit(solution)/shard_map/ppermute | solution.py:488
  65.4 9.7 %collective-permute-start.13 = (bf16[1312,128]{1,0:T(8,128)(2,1)S(1)}, bf16[1312,128]{1,0:T(8,128)(2,1)S(1)}, u32[]{:S(2)}, u32[]{:S(2)}) collective-permute-start(bf16[1312,128]{1,0:T(8,128)(2,1)S(1)} %get-tuple-element.68.refs_0_), channel_id=1, source_target_pairs={{0,4},{1,5},{2,6},{3,7},{4,0},{5,1},{6,2},{7,3},{8,12},{9,13},{10,... | collective-permute-start | bytes 1007624 | tf_op jit(solution)/shard_map/ppermute | solution.py:491
  76.0 19.9 %collective-permute-start.17 = (bf16[10,128,128]{2,1,0:T(8,128)(2,1)S(1)}, bf16[10,128,128]{2,1,0:T(8,128)(2,1)S(1)}, u32[]{:S(2)}, u32[]{:S(2)}) collective-permute-start(bf16[10,128,128]{2,1,0:T(8,128)(2,1)S(1)} %get-tuple-element.75), channel_id=1, source_target_pairs={{0,8},{8,0},{16,24},{24,16},{1,9},{9,1},{17,25},{25,17},{2,10},{10... | collective-permute-start | bytes 983048 | tf_op jit(solution)/shard_map/ppermute | solution.py:491
  76.5 15.9 %collective-permute-start.18 = (bf16[512,256]{1,0:T(8,128)(2,1)S(1)}, bf16[512,256]{1,0:T(8,128)(2,1)S(1)}, u32[]{:S(2)}, u32[]{:S(2)}) collective-permute-start(bf16[512,256]{1,0:T(8,128)(2,1)S(1)} %get-tuple-element.76), channel_id=1, source_target_pairs={{0,8},{8,16},{16,24},{24,0},{1,9},{9,17},{17,25},{25,1},{2,10},{10... | collective-permute-start | bytes 786440 | tf_op jit(solution)/shard_map/ppermute | solution.py:488
  78.8 24.6 %collective-permute-start.19 = (bf16[512,256]{1,0:T(8,128)(2,1)S(1)}, bf16[512,256]{1,0:T(8,128)(2,1)S(1)}, u32[]{:S(2)}, u32[]{:S(2)}) collective-permute-start(bf16[512,256]{1,0:T(8,128)(2,1)S(1)} %get-tuple-element.78), channel_id=1, source_target_pairs={{0,16},{8,24},{16,0},{24,8},{1,17},{9,25},{17,1},{25,9},{2,18},{10... | collective-permute-start | bytes 786440 | tf_op jit(solution)/shard_map/ppermute | solution.py:488
  80.4 27.5 %collective-permute-start.20 = (bf16[512,256]{1,0:T(8,128)(2,1)S(1)}, bf16[512,256]{1,0:T(8,128)(2,1)S(1)}, u32[]{:S(2)}, u32[]{:S(2)}) collective-permute-start(bf16[512,256]{1,0:T(8,128)(2,1)S(1)} %get-tuple-element.79), channel_id=1, source_target_pairs={{0,24},{8,0},{16,8},{24,16},{1,25},{9,1},{17,9},{25,17},{2,26},{10... | collective-permute-start | bytes 786440 | tf_op jit(solution)/shard_map/ppermute | solution.py:488
  98.4 14.4 %collective-permute-start.21 = (bf16[512,128]{1,0:T(8,128)(2,1)S(1)}, bf16[512,128]{1,0:T(8,128)(2,1)S(1)}, u32[]{:S(2)}, u32[]{:S(2)}) collective-permute-start(bf16[512,128]{1,0:T(8,128)(2,1)S(1)} %get-tuple-element.81), channel_id=1, source_target_pairs={{0,8},{8,16},{16,24},{24,0},{1,9},{9,17},{17,25},{25,1},{2,10},{10... | collective-permute-start | bytes 393224 | tf_op jit(solution)/shard_map/ppermute | solution.py:488
  98.8 22.8 %collective-permute-start.22 = (bf16[512,128]{1,0:T(8,128)(2,1)S(1)}, bf16[512,128]{1,0:T(8,128)(2,1)S(1)}, u32[]{:S(2)}, u32[]{:S(2)}) collective-permute-start(bf16[512,128]{1,0:T(8,128)(2,1)S(1)} %get-tuple-element.82), channel_id=1, source_target_pairs={{0,24},{8,0},{16,8},{24,16},{1,25},{9,1},{17,9},{25,17},{2,26},{10... | collective-permute-start | bytes 393224 | tf_op jit(solution)/shard_map/ppermute | solution.py:488
  101.0 25.4 %collective-permute-start.29 = (bf16[512,128]{1,0:T(8,128)(2,1)S(1)}, bf16[512,128]{1,0:T(8,128)(2,1)S(1)}, u32[]{:S(2)}, u32[]{:S(2)}) collective-permute-start(bf16[512,128]{1,0:T(8,128)(2,1)S(1)} %get-tuple-element.90), channel_id=1, source_target_pairs={{0,16},{8,24},{16,0},{24,8},{1,17},{9,25},{17,1},{25,9},{2,18},{10... | collective-permute-start | bytes 393224 | tf_op jit(solution)/shard_map/ppermute | solution.py:488
  112.6 20.5 %collective-permute-start.26 = (bf16[512,256]{1,0:T(8,128)(2,1)S(1)}, bf16[512,256]{1,0:T(8,128)(2,1)S(1)}, u32[]{:S(2)}, u32[]{:S(2)}) collective-permute-start(bf16[512,256]{1,0:T(8,128)(2,1)S(1)} %get-tuple-element.87), channel_id=1, source_target_pairs={{0,8},{8,16},{16,24},{24,0},{1,9},{9,17},{17,25},{25,1},{2,10},{10... | collective-permute-start | bytes 786440 | tf_op jit(solution)/shard_map/ppermute | solution.py:488
  112.7 33.6 %collective-permute-start.27 = (bf16[512,256]{1,0:T(8,128)(2,1)S(1)}, bf16[512,256]{1,0:T(8,128)(2,1)S(1)}, u32[]{:S(2)}, u32[]{:S(2)}) collective-permute-start(bf16[512,256]{1,0:T(8,128)(2,1)S(1)} %get-tuple-element.88), channel_id=1, source_target_pairs={{0,16},{8,24},{16,0},{24,8},{1,17},{9,25},{17,1},{25,9},{2,18},{10... | collective-permute-start | bytes 786440 | tf_op jit(solution)/shard_map/ppermute | solution.py:488
  112.8 35.7 %collective-permute-start.28 = (bf16[512,256]{1,0:T(8,128)(2,1)S(1)}, bf16[512,256]{1,0:T(8,128)(2,1)S(1)}, u32[]{:S(2)}, u32[]{:S(2)}) collective-permute-start(bf16[512,256]{1,0:T(8,128)(2,1)S(1)} %get-tuple-element.89), channel_id=1, source_target_pairs={{0,24},{8,0},{16,8},{24,16},{1,25},{9,1},{17,9},{25,17},{2,26},{10... | collective-permute-start | bytes 786440 | tf_op jit(solution)/shard_map/ppermute | solution.py:488
  126.3 25.5 %collective-permute-start.23 = (bf16[512,256]{1,0:T(8,128)(2,1)S(1)}, bf16[512,256]{1,0:T(8,128)(2,1)S(1)}, u32[]{:S(2)}, u32[]{:S(2)}) collective-permute-start(bf16[512,256]{1,0:T(8,128)(2,1)S(1)} %get-tuple-element.84), channel_id=1, source_target_pairs={{0,8},{8,16},{16,24},{24,0},{1,9},{9,17},{17,25},{25,1},{2,10},{10... | collective-permute-start | bytes 786440 | tf_op jit(solution)/shard_map/ppermute | solution.py:488
  126.4 30.2 %collective-permute-start.24 = (bf16[512,256]{1,0:T(8,128)(2,1)S(1)}, bf16[512,256]{1,0:T(8,128)(2,1)S(1)}, u32[]{:S(2)}, u32[]{:S(2)}) collective-permute-start(bf16[512,256]{1,0:T(8,128)(2,1)S(1)} %get-tuple-element.85), channel_id=1, source_target_pairs={{0,16},{8,24},{16,0},{24,8},{1,17},{9,25},{17,1},{25,9},{2,18},{10... | collective-permute-start | bytes 786440 | tf_op jit(solution)/shard_map/ppermute | solution.py:488
  133.2 24.4 %collective-permute-start.25 = (bf16[512,256]{1,0:T(8,128)(2,1)S(1)}, bf16[512,256]{1,0:T(8,128)(2,1)S(1)}, u32[]{:S(2)}, u32[]{:S(2)}) collective-permute-start(bf16[512,256]{1,0:T(8,128)(2,1)S(1)} %get-tuple-element.86), channel_id=1, source_target_pairs={{0,24},{8,0},{16,8},{24,16},{1,25},{9,1},{17,9},{25,17},{2,26},{10... | collective-permute-start | bytes 786440 | tf_op jit(solution)/shard_map/ppermute | solution.py:488
